TPU v7x, 32 devices: a whole 2x2x4 slice. The times are simulated.
32 devices in a mesh: dom: 32 (over z, y, x, core).
Axes of the slice: x: 2, y: 2, z: 4, core: 2. Of those that a mesh axis runs over, the one named last changes fastest.
Arguments:
- features: bfloat16 [36864, 128], P('dom'), may hold values from -6 to 6
- targets: bfloat16 [36864, 128], P('dom'), may hold values from -6 to 6
- first_weight: bfloat16 [128, 128], replicated, may hold values from -0.5 to 0.5
- second_weight: bfloat16 [128, 128], replicated, may hold values from -0.5 to 0.5
- local_bonds: bfloat16 [36864, 1152], P('dom'), may hold values from -0.4375 to 0.4375
- halo_bonds: bfloat16 [36864, 512], P('dom'), may hold values from -0.4375 to 0.4375
- tile_mask: int32 [576, 18], P('dom'), may hold values 0 or 1
- send_rows: int32 [128, 128], P('dom'), may hold values from 0 to 1151
Outputs:
- prediction: bfloat16 [36864, 128], P('dom')
- grad_first: float32 [128, 128], replicated
- grad_second: float32 [128, 128], replicated
Inputs may be any that keep to these rules, and one draw needn't show every extreme that they name: `tile_mask`: tile presence flags. `send_rows`: local atom numbers of the sending partition; repeats allowed.
All inputs are finite; a program needn't handle non-finite values. No bound on the sum of `tile_mask` on one device may be relied on, other than what follows from the above.
Results may differ from a plain program's by a relative error of at most 0.004.
The roundings to bfloat16 on the way count: a program that leaves them out, or rounds other values in their place, can miss the bound.
Values may be sent and summed in bfloat16 or wider, within the bound.
No kernel may reach another device: no remote copies, remote signals or barrier semaphores. Data moves between devices by JAX's collectives and lax.ppermute only.
A program may use at most 64 MiB of HBM per device.

v0:
```python
import math

import jax
import jax.numpy as jnp
from jax import lax
from jax.sharding import PartitionSpec as P

ROUNDS = 4


def swapped(value, axis, apart):
    mask = 2**apart
    pairs = [(source, source ^ mask) for source in range(lax.axis_size(axis))]
    return lax.ppermute(value, axis, pairs)


def spread_mask(tile_mask):
    return jnp.repeat(jnp.repeat(tile_mask, 64, axis=0), 64, axis=1).astype(jnp.bfloat16)


def contract_rows(left, right):
    return lax.dot_general(
        left, right, (((0,), (0,)), ((), ())), preferred_element_type=jnp.float32
    )


def fetch_inputs(rows, send_rows):
    pieces = []
    for turn in range(ROUNDS):
        chosen = jnp.take(rows, send_rows[turn], axis=0)
        pieces.append(swapped(chosen, "dom", turn))
    return jnp.concatenate(pieces, axis=0)


def fetch_hidden(rows, send_rows):
    pieces = []
    for turn in range(ROUNDS):
        chosen = jnp.take(rows, send_rows[turn], axis=0)
        pieces.append(swapped(chosen, "dom", turn))
    return jnp.concatenate(pieces, axis=0)


def return_grads(halo_cot, send_rows, row_count):
    width = send_rows.shape[1]
    total = jnp.zeros((row_count, halo_cot.shape[1]), jnp.float32)
    for turn in range(ROUNDS):
        block = halo_cot[turn * width : (turn + 1) * width]
        back = swapped(block.astype(jnp.bfloat16), "dom", turn).astype(block.dtype)
        total = total.at[send_rows[turn]].add(back)
    return total


def local(
    features, targets, first_weight, second_weight, local_bonds, halo_bonds, tile_mask, send_rows
):
    row_count = features.shape[0]
    bond_tiles = local_bonds * spread_mask(tile_mask)
    halo_inputs = fetch_inputs(features, send_rows)
    inner_first = jnp.dot(bond_tiles, features, preferred_element_type=jnp.float32)
    first_sum = inner_first + jnp.dot(halo_bonds, halo_inputs, preferred_element_type=jnp.float32)
    first_agg = first_sum.astype(jnp.bfloat16)
    first_pre = jnp.dot(first_agg, first_weight, preferred_element_type=jnp.float32)
    hidden = (features.astype(jnp.float32) + jax.nn.silu(first_pre)).astype(jnp.bfloat16)
    halo_hidden = fetch_hidden(hidden, send_rows)
    inner_second = jnp.dot(bond_tiles, hidden, preferred_element_type=jnp.float32)
    second_sum = inner_second + jnp.dot(halo_bonds, halo_hidden, preferred_element_type=jnp.float32)
    second_agg = second_sum.astype(jnp.bfloat16)
    output = hidden.astype(jnp.float32) + jnp.dot(
        second_agg, second_weight, preferred_element_type=jnp.float32
    )
    prediction = output.astype(jnp.bfloat16)
    scale = 1.0 / math.sqrt(row_count * lax.axis_size("dom"))
    error = (output - targets.astype(jnp.float32)) * scale
    error_b = error.astype(jnp.bfloat16)
    grad_second = contract_rows(second_agg, error_b)
    agg_cot = lax.dot_general(
        error_b, second_weight, (((1,), (1,)), ((), ())), preferred_element_type=jnp.float32
    ).astype(jnp.bfloat16)
    halo_cot = contract_rows(halo_bonds, agg_cot)
    returned = return_grads(halo_cot, send_rows, row_count)
    inner_cot = contract_rows(bond_tiles, agg_cot)
    hidden_cot = error + inner_cot + returned
    sigm = jax.nn.sigmoid(first_pre)
    pre_cot = (hidden_cot * sigm * (1.0 + first_pre * (1.0 - sigm))).astype(jnp.bfloat16)
    grad_first = contract_rows(first_agg, pre_cot)
    grad_first, grad_second = lax.psum((grad_first, grad_second), "dom")
    return (prediction, grad_first, grad_second)


def solution(mesh):
    in_specs = (
        P("dom", None),
        P("dom", None),
        P(),
        P(),
        P("dom", None),
        P("dom", None),
        P("dom", None),
        P("dom", None),
    )
    out_specs = (P("dom", None), P(), P())
    return jax.shard_map(local, mesh=mesh, in_specs=in_specs, out_specs=out_specs, check_vma=False)
```

profile of v0, /device:TPU:0, one launch (start us, length us, event | category | flops | bytes accessed | tf_op | source)
XLA Modules:
  0.0 186.2 jit_solution(2962976004252696705)
XLA Ops:
  7.2 0.0 copy-start
  7.2 0.0 all-reduce.3.cloned.1.call-start
  7.2 0.8 compare_and_fusion.3
  8.1 1.7 gather_fusion
  9.7 0.1 broadcast_select_fusion.7
  9.8 0.5 collective-permute-start
  10.4 1.6 gather_fusion.1
  12.0 0.1 broadcast_select_fusion.5
  12.1 2.6 %collective-permute-start.1 = (bf16[128,128]{1,0:T(8,128)(2,1)S(1)}, bf16[128,128]{1,0:T(8,128)(2,1)S(1)}, u32[]{:S(2)}, u32[]{:S(2)}) collective-permute-start(bf16[128,128]{1,0:T(8,128)(2,1)S(1)} %broadcast_select_fusion.5), channel_id=1, source_target_pairs={{0,2},{1,3},{2,0},{3,1},{4,6},{5,7},{6,4},{7,5},{8,10},{9,11},{10,... | collective-permute-start | bytes 98312 | tf_op jit(solution)/shard_map/ppermute | solution.py:14
  14.7 1.6 gather_fusion.2
  16.3 0.1 broadcast_select_fusion.3
  16.4 1.6 collective-permute-start.2
  18.0 1.7 gather_fusion.3
  19.7 0.1 broadcast_select_fusion.1
  19.8 0.0 copy-start.6
  19.8 1.6 collective-permute-start.3
  21.4 5.2 %copy.15 = bf16[1152,1152]{0,1:T(8,128)(2,1)} copy(bf16[1152,1152]{1,0:T(8,128)(2,1)} %param.14) | data formatting | bytes 5308416 | tf_op args[4]
  26.6 0.1 copy.14
  26.8 0.1 broadcast_in_dim.20
  26.9 0.1 convert_element_type.59
  27.0 0.0 copy-start.3
  27.0 2.1 %bitcast_multiply_fusion = bf16[1152,1152]{0,1:T(8,128)(2,1)S(1)} fusion(bf16[1152,1152]{0,1:T(8,128)(2,1)} %copy.15, bf16[1152,18]{0,1:T(8,128)(2,1)S(1)} %convert_element_type.59), kind=kLoop, calls=%fused_computation.12 | loop fusion | flops 1327104 | bytes 5349888 | tf_op jit(solution)/shard_map/mul | solution.py:57
  29.1 0.0 copy-start.7
  29.1 0.0 copy-start.8
  29.1 0.9 fusion.41
  30.1 0.5 fusion.2
  30.6 0.0 copy-done.1
  30.6 0.3 add_convert_fusion
  30.9 0.7 gather_fusion.4
  31.7 0.7 gather_fusion.5
  32.4 0.7 gather_fusion.6
  33.1 0.7 gather_fusion.7
  33.8 0.1 broadcast_select_fusion.6
  33.9 0.1 collective-permute-start.4
  34.0 0.1 broadcast_select_fusion.4
  34.0 0.6 collective-permute-start.5
  34.7 0.1 broadcast_select_fusion.2
  34.7 0.6 collective-permute-start.6
  35.3 0.1 broadcast_select_fusion
  35.4 0.0 copy-start.5
  35.4 0.1 collective-permute-start.7
  35.5 2.7 %fusion.42 = f32[1152,128]{1,0:T(8,128)S(1)} fusion(bf16[1152,1152]{0,1:T(8,128)(2,1)} %copy-done.1, bf16[1152,128]{1,0:T(8,128)(2,1)S(1)} %get-tuple-element.28), kind=kOutput, calls=%fused_computation.87 | convolution fusion | flops 339738624 | bytes 3538944 | tf_op jit(solution)/shard_map/dot_general | solution.py:65
  38.2 0.0 copy-start.4
  38.2 0.5 collective-permute-done.6
  38.7 0.7 collective-permute-done.7
  39.4 0.5 fusion.3
  39.9 0.9 fusion.40
  40.8 0.2 convolution_convert_fusion
  41.1 0.9 convolution_add_fusion
  41.9 0.6 fusion.4
  42.5 0.1 collective-permute-start.8
  42.6 1.6 collective-permute-start.9
  44.2 1.5 collective-permute-start.10
  45.7 1.0 collective-permute-start.11
  46.7 0.9 fusion.36
  47.6 1.5 scatter_custom_fusion
  49.1 1.5 scatter_custom_fusion.1
  50.7 1.5 scatter_custom_fusion.2
  52.2 1.5 scatter_custom_fusion.3
  53.7 1.0 fusion.6
  54.7 0.0 all-reduce.3.cloned.1.call-update
  54.7 121.7 %all-reduce.3.cloned.1.call-done = (f32[128,128]{1,0:T(8,128)}, f32[128,128]{1,0:T(8,128)}) async-done(((f32[128,128]{1,0:T(8,128)}, f32[128,128]{1,0:T(8,128)}), (f32[128,128]{1,0:T(8,128)}, f32[128,128]{1,0:T(8,128)})) %all-reduce.3.cloned.1.call-update) | async-done | bytes 131088 | tf_op jit(solution)/shard_map/psum | solution.py:86
  176.4 1.5 copy.28
  177.9 1.5 copy.29
  (27 shorter events, 0.1 us)
Async XLA Ops:
  7.2 23.0 %copy-start = (bf16[1152,512]{1,0:T(8,128)(2,1)S(1)}, bf16[1152,512]{1,0:T(8,128)(2,1)}, u32[]{:S(2)}) copy-start(bf16[1152,512]{1,0:T(8,128)(2,1)} %param.15) | copy-start | bytes 3538948
  7.2 169.2 %all-reduce.3.cloned.1.call-start = ((), (), s32[]{:S(2)}) async-start(), calls=%async_computation | async-start | bytes 262144 | tf_op jit(solution)/shard_map/psum | solution.py:86
  9.8 20.2 %collective-permute-start = (bf16[128,128]{1,0:T(8,128)(2,1)S(1)}, bf16[128,128]{1,0:T(8,128)(2,1)S(1)}, u32[]{:S(2)}, u32[]{:S(2)}) collective-permute-start(bf16[128,128]{1,0:T(8,128)(2,1)S(1)} %broadcast_select_fusion.7), channel_id=1, source_target_pairs={{0,1},{1,0},{2,3},{3,2},{4,5},{5,4},{6,7},{7,6},{8,9},{9,8},{10,11... | collective-permute-start | bytes 98312 | tf_op jit(solution)/shard_map/ppermute | solution.py:14
  12.1 18.0 %collective-permute-start.1 = (bf16[128,128]{1,0:T(8,128)(2,1)S(1)}, bf16[128,128]{1,0:T(8,128)(2,1)S(1)}, u32[]{:S(2)}, u32[]{:S(2)}) collective-permute-start(bf16[128,128]{1,0:T(8,128)(2,1)S(1)} %broadcast_select_fusion.5), channel_id=1, source_target_pairs={{0,2},{1,3},{2,0},{3,1},{4,6},{5,7},{6,4},{7,5},{8,10},{9,11},{10,... | collective-permute-start | bytes 98312 | tf_op jit(solution)/shard_map/ppermute | solution.py:14
  16.4 13.7 %collective-permute-start.2 = (bf16[128,128]{1,0:T(8,128)(2,1)S(1)}, bf16[128,128]{1,0:T(8,128)(2,1)S(1)}, u32[]{:S(2)}, u32[]{:S(2)}) collective-permute-start(bf16[128,128]{1,0:T(8,128)(2,1)S(1)} %broadcast_select_fusion.3), channel_id=1, source_target_pairs={{0,4},{1,5},{2,6},{3,7},{4,0},{5,1},{6,2},{7,3},{8,12},{9,13},{10,... | collective-permute-start | bytes 98312 | tf_op jit(solution)/shard_map/ppermute | solution.py:14
  19.8 6.9 %copy-start.6 = (s32[18,18]{1,0:T(8,128)S(1)}, s32[18,18]{1,0:T(8,128)}, u32[]{:S(2)}) copy-start(s32[18,18]{1,0:T(8,128)} %param.16) | copy-start | bytes 3892
  19.8 10.3 %collective-permute-start.3 = (bf16[128,128]{1,0:T(8,128)(2,1)S(1)}, bf16[128,128]{1,0:T(8,128)(2,1)S(1)}, u32[]{:S(2)}, u32[]{:S(2)}) collective-permute-start(bf16[128,128]{1,0:T(8,128)(2,1)S(1)} %broadcast_select_fusion.1), channel_id=1, source_target_pairs={{0,8},{1,9},{2,10},{3,11},{4,12},{5,13},{6,14},{7,15},{8,0},{9,1},... | collective-permute-start | bytes 98312 | tf_op jit(solution)/shard_map/ppermute | solution.py:14
  27.0 2.1 %copy-start.3 = (bf16[1152,128]{1,0:T(8,128)(2,1)S(1)}, bf16[1152,128]{1,0:T(8,128)(2,1)}, u32[]{:S(2)}) copy-start(bf16[1152,128]{1,0:T(8,128)(2,1)} %param.10) | copy-start | bytes 884740
  29.1 1.5 copy-start.1
  29.1 0.9 copy-start.7
  29.1 1.5 copy-start.8
  33.9 4.3 %collective-permute-start.4 = (bf16[128,128]{1,0:T(8,128)(2,1)S(1)}, bf16[128,128]{1,0:T(8,128)(2,1)S(1)}, u32[]{:S(2)}, u32[]{:S(2)}) collective-permute-start(bf16[128,128]{1,0:T(8,128)(2,1)S(1)} %broadcast_select_fusion.6), channel_id=1, source_target_pairs={{0,1},{1,0},{2,3},{3,2},{4,5},{5,4},{6,7},{7,6},{8,9},{9,8},{10,11... | collective-permute-start | bytes 98312 | tf_op jit(solution)/shard_map/ppermute | solution.py:14
  34.0 4.1 %collective-permute-start.5 = (bf16[128,128]{1,0:T(8,128)(2,1)S(1)}, bf16[128,128]{1,0:T(8,128)(2,1)S(1)}, u32[]{:S(2)}, u32[]{:S(2)}) collective-permute-start(bf16[128,128]{1,0:T(8,128)(2,1)S(1)} %broadcast_select_fusion.4), channel_id=1, source_target_pairs={{0,2},{1,3},{2,0},{3,1},{4,6},{5,7},{6,4},{7,5},{8,10},{9,11},{10,... | collective-permute-start | bytes 98312 | tf_op jit(solution)/shard_map/ppermute | solution.py:14
  34.7 4.0 %collective-permute-start.6 = (bf16[128,128]{1,0:T(8,128)(2,1)S(1)}, bf16[128,128]{1,0:T(8,128)(2,1)S(1)}, u32[]{:S(2)}, u32[]{:S(2)}) collective-permute-start(bf16[128,128]{1,0:T(8,128)(2,1)S(1)} %broadcast_select_fusion.2), channel_id=1, source_target_pairs={{0,4},{1,5},{2,6},{3,7},{4,0},{5,1},{6,2},{7,3},{8,12},{9,13},{10,... | collective-permute-start | bytes 98312 | tf_op jit(solution)/shard_map/ppermute | solution.py:14
  35.4 4.5 %copy-start.5 = (bf16[128,128]{1,0:T(8,128)(2,1)S(1)}, bf16[128,128]{1,0:T(8,128)(2,1)}, u32[]{:S(2)}) copy-start(bf16[128,128]{1,0:T(8,128)(2,1)} %param.13) | copy-start | bytes 98308
  35.4 4.0 %collective-permute-start.7 = (bf16[128,128]{1,0:T(8,128)(2,1)S(1)}, bf16[128,128]{1,0:T(8,128)(2,1)S(1)}, u32[]{:S(2)}, u32[]{:S(2)}) collective-permute-start(bf16[128,128]{1,0:T(8,128)(2,1)S(1)} %broadcast_select_fusion), channel_id=1, source_target_pairs={{0,8},{1,9},{2,10},{3,11},{4,12},{5,13},{6,14},{7,15},{8,0},{9,1},... | collective-permute-start | bytes 98312 | tf_op jit(solution)/shard_map/ppermute | solution.py:14
  38.2 2.7 %copy-start.4 = (bf16[1152,128]{1,0:T(8,128)(2,1)S(1)}, bf16[1152,128]{1,0:T(8,128)(2,1)}, u32[]{:S(2)}) copy-start(bf16[1152,128]{1,0:T(8,128)(2,1)} %param.11) | copy-start | bytes 884740
  38.2 2.9 %copy-start.2 = (bf16[1152,1152]{0,1:T(8,128)(2,1)S(1)}, bf16[1152,1152]{0,1:T(8,128)(2,1)}, u32[]{:S(2)}) copy-start(bf16[1152,1152]{0,1:T(8,128)(2,1)} %copy-done.1) | copy-start | bytes 7962628
  42.5 5.1 %collective-permute-start.8 = (bf16[128,128]{1,0:T(8,128)(2,1)S(1)}, bf16[128,128]{1,0:T(8,128)(2,1)S(1)}, u32[]{:S(2)}, u32[]{:S(2)}) collective-permute-start(bf16[128,128]{1,0:T(8,128)(2,1)S(1)} %get-tuple-element.17), channel_id=1, source_target_pairs={{0,1},{1,0},{2,3},{3,2},{4,5},{5,4},{6,7},{7,6},{8,9},{9,8},{10,11... | collective-permute-start | bytes 98312 | tf_op jit(solution)/shard_map/ppermute | solution.py:14
  42.6 6.5 %collective-permute-start.9 = (bf16[128,128]{1,0:T(8,128)(2,1)S(1)}, bf16[128,128]{1,0:T(8,128)(2,1)S(1)}, u32[]{:S(2)}, u32[]{:S(2)}) collective-permute-start(bf16[128,128]{1,0:T(8,128)(2,1)S(1)} %get-tuple-element.16), channel_id=1, source_target_pairs={{0,2},{1,3},{2,0},{3,1},{4,6},{5,7},{6,4},{7,5},{8,10},{9,11},{10,... | collective-permute-start | bytes 98312 | tf_op jit(solution)/shard_map/ppermute | solution.py:14
  44.2 6.5 %collective-permute-start.10 = (bf16[128,128]{1,0:T(8,128)(2,1)S(1)}, bf16[128,128]{1,0:T(8,128)(2,1)S(1)}, u32[]{:S(2)}, u32[]{:S(2)}) collective-permute-start(bf16[128,128]{1,0:T(8,128)(2,1)S(1)} %get-tuple-element.15), channel_id=1, source_target_pairs={{0,4},{1,5},{2,6},{3,7},{4,0},{5,1},{6,2},{7,3},{8,12},{9,13},{10,... | collective-permute-start | bytes 98312 | tf_op jit(solution)/shard_map/ppermute | solution.py:14
  45.7 6.5 %collective-permute-start.11 = (bf16[128,128]{1,0:T(8,128)(2,1)S(1)}, bf16[128,128]{1,0:T(8,128)(2,1)S(1)}, u32[]{:S(2)}, u32[]{:S(2)}) collective-permute-start(bf16[128,128]{1,0:T(8,128)(2,1)S(1)} %get-tuple-element.14), channel_id=1, source_target_pairs={{0,8},{1,9},{2,10},{3,11},{4,12},{5,13},{6,14},{7,15},{8,0},{9,1},... | collective-permute-start | bytes 98312 | tf_op jit(solution)/shard_map/ppermute | solution.py:14
Sparse Core Ops, SparseCore 0:
  54.8 121.5 all-reduce.2
where the time goes:
time: 187 us; the launch traced here: 186 us
  waiting for transfers between devices  123 us (66%)
  local copies, waits for them, and re-layouts  18 us (10%)
  between operations  14.4 us (8%)
  starting transfers between devices  11.9 us (6%)
  other arithmetic  9.57 us (5%)
  matrix products  9.33 us (5%)
    psum x1, waiting for transfers between devices, local(): grad_first, grad_second = lax.psum((grad_first, grad_second), 'dom')  122 us
    ppermute x12, starting transfers between devices, swapped(): return lax.ppermute(value, axis, pairs)  11.8 us
    unnamed x21, local copies, waits for them, and re-layouts  8.24 us
    gather x4, local copies, waits for them, and re-layouts, fetch_inputs(): chosen = jnp.take(rows, send_rows[turn], axis=0)  6.6 us
    scatter-add x4, other arithmetic, return_grads(): total = total.at[send_rows[turn]].add(back)  5.95 us
  transfers between devices with their start and end apart: 13, of which 3 were waited for; matrix products, arithmetic and copies ran while one was open for 12% of the time, Pallas kernels for 0%

commit v1 on v0

v1 whole, which is shorter than its diff:
```python
import functools
import math

import jax
import jax.numpy as jnp
from jax import lax
from jax.experimental import pallas as pl
from jax.experimental.pallas import tpu as pltpu
from jax.sharding import PartitionSpec as P

TILE = 64
PARAMS = pltpu.CompilerParams(vmem_limit_bytes=16 * 2**20)


def swapped(value, mask):
    pairs = [(source, source ^ mask) for source in range(lax.axis_size("dom"))]
    return lax.ppermute(value, "dom", pairs)


def dot(left, right):
    return jnp.dot(left, right, preferred_element_type=jnp.float32)


def dot_rows(left, right):
    return lax.dot_general(
        left, right, (((0,), (0,)), ((), ())), preferred_element_type=jnp.float32
    )


def dot_last(left, right):
    return lax.dot_general(
        left, right, (((1,), (1,)), ((), ())), preferred_element_type=jnp.float32
    )


def call(body, outs, *args):
    args = [pltpu.with_memory_space_constraint(arg, pltpu.VMEM) for arg in args]
    return pl.pallas_call(
        body,
        out_shape=[pltpu.VMEM(shape, dtype) for shape, dtype in outs],
        in_specs=[pl.BlockSpec(memory_space=pltpu.VMEM)] * len(args),
        out_specs=[pl.BlockSpec(memory_space=pltpu.VMEM)] * len(outs),
        compiler_params=PARAMS,
    )(*args)


def pick_kernel(features, send_rows, picker, *picked):
    rounds, width = send_rows.shape
    atoms = features.shape[0]
    rows = jnp.concatenate(
        [send_rows[...], jnp.zeros((8 - rounds, width), jnp.int32)], axis=0
    ).T
    column = lax.broadcasted_iota(jnp.int32, (width, atoms), 1)
    for turn in range(rounds):
        chosen = (rows[:, turn : turn + 1] == column).astype(jnp.float32).astype(jnp.bfloat16)
        picker[turn * width : (turn + 1) * width, :] = chosen
        picked[turn][...] = dot(chosen, features[...]).astype(jnp.bfloat16)


def inner_kernel(local_bonds, tile_mask, features, bonds, inner):
    tiles = tile_mask.shape[0]
    atoms = local_bonds.shape[0]
    spread = (
        lax.broadcasted_iota(jnp.int32, (tiles, atoms), 1) // TILE
        == lax.broadcasted_iota(jnp.int32, (tiles, atoms), 0)
    ).astype(jnp.float32).astype(jnp.bfloat16)
    wide = dot(tile_mask[...].astype(jnp.float32).astype(jnp.bfloat16), spread).astype(jnp.bfloat16)
    for tile in range(tiles):
        rows = slice(tile * TILE, (tile + 1) * TILE)
        bonds[rows, :] = local_bonds[rows, :] * wide[tile : tile + 1, :]
    inner[...] = dot(bonds[...], features[...])


def first_kernel(inner, halo_bonds, picker, halo0, halo1, halo2, halo3, agg, *picked):
    width = halo0.shape[0]
    total = inner[...]
    for turn, halo in enumerate((halo0, halo1, halo2, halo3)):
        total += dot(halo_bonds[:, turn * width : (turn + 1) * width], halo[...])
    agg[...] = total.astype(jnp.bfloat16)
    for turn in range(len(picked)):
        rows = picker[turn * width : (turn + 1) * width, :]
        picked[turn][...] = dot(rows, agg[...]).astype(jnp.bfloat16)


def hidden_kernel(agg, first_weight, features, bonds, hidden, slope, inner):
    pre = dot(agg[...], first_weight[...])
    sigm = jax.nn.sigmoid(pre)
    slope[...] = sigm * (1.0 + pre * (1.0 - sigm))
    hidden[...] = (features[...].astype(jnp.float32) + pre * sigm).astype(jnp.bfloat16)
    inner[...] = dot(bonds[...], hidden[...])


def back_kernel(
    scale,
    inner,
    hidden,
    slope,
    agg,
    bonds,
    halo_bonds,
    targets,
    first_weight,
    second_weight,
    halo0,
    halo1,
    halo2,
    halo3,
    agg0,
    agg1,
    agg2,
    agg3,
    prediction,
    grad_first,
    grad_second,
):
    halo = jnp.concatenate([part[...] for part in (halo0, halo1, halo2, halo3)], axis=0)
    halo_agg = jnp.concatenate([part[...] for part in (agg0, agg1, agg2, agg3)], axis=0)
    pre = dot(halo_agg, first_weight[...])
    sigm = jax.nn.sigmoid(pre)
    halo_slope = sigm * (1.0 + pre * (1.0 - sigm))
    halo_hidden = (halo.astype(jnp.float32) + pre * sigm).astype(jnp.bfloat16)
    second_agg = (inner[...] + dot(halo_bonds[...], halo_hidden)).astype(jnp.bfloat16)
    output = hidden[...].astype(jnp.float32) + dot(second_agg, second_weight[...])
    prediction[...] = output.astype(jnp.bfloat16)
    error = (output - targets[...].astype(jnp.float32)) * scale
    error_b = error.astype(jnp.bfloat16)
    grad_second[...] = dot_rows(second_agg, error_b)
    agg_cot = dot_last(error_b, second_weight[...]).astype(jnp.bfloat16)
    halo_cot = dot_rows(halo_bonds[...], agg_cot)
    halo_cot = (halo_cot * halo_slope).astype(jnp.bfloat16)
    own_cot = (error + dot_rows(bonds[...], agg_cot)) * slope[...]
    grad_first[...] = dot_rows(agg[...], own_cot.astype(jnp.bfloat16)) + dot_rows(
        halo_agg, halo_cot
    )


def summed(first, second):
    size = lax.axis_size("dom")
    even = lax.axis_index("dom") % 2 == 0
    total = jnp.where(even, first, second) + swapped(jnp.where(even, second, first), 1)
    mask = 2
    while mask < size:
        total = total + swapped(total, mask)
        mask *= 2
    other = swapped(total, 1)
    return jnp.where(even, total, other), jnp.where(even, other, total)


def local(
    features, targets, first_weight, second_weight, local_bonds, halo_bonds, tile_mask, send_rows
):
    atoms, wide = features.shape
    rounds, width = send_rows.shape
    low, high = jnp.bfloat16, jnp.float32
    sent = [((width, wide), low)] * rounds
    picker, *picked = call(
        pick_kernel, [((rounds * width, atoms), low)] + sent, features, send_rows
    )
    halo = [swapped(part, 2**turn) for turn, part in enumerate(picked)]
    bonds, inner = call(
        inner_kernel,
        [((atoms, atoms), low), ((atoms, wide), high)],
        local_bonds,
        tile_mask,
        features,
    )
    agg, *picked = call(
        first_kernel, [((atoms, wide), low)] + sent, inner, halo_bonds, picker, *halo
    )
    halo_agg = [swapped(part, 2**turn) for turn, part in enumerate(picked)]
    hidden, slope, inner = call(
        hidden_kernel,
        [((atoms, wide), low), ((atoms, wide), high), ((atoms, wide), high)],
        agg,
        first_weight,
        features,
        bonds,
    )
    scale = 1.0 / math.sqrt(atoms * lax.axis_size("dom"))
    prediction, grad_first, grad_second = call(
        functools.partial(back_kernel, scale),
        [((atoms, wide), low), ((wide, wide), high), ((wide, wide), high)],
        inner,
        hidden,
        slope,
        agg,
        bonds,
        halo_bonds,
        targets,
        first_weight,
        second_weight,
        *halo,
        *halo_agg,
    )
    grad_first, grad_second = summed(grad_first, grad_second)
    return prediction, grad_first, grad_second


def solution(mesh):
    rows = P("dom", None)
    in_specs = (rows, rows, P(), P(), rows, rows, rows, rows)
    out_specs = (rows, P(), P())
    return jax.shard_map(local, mesh=mesh, in_specs=in_specs, out_specs=out_specs, check_vma=False)
```

time: 187 us -> 47.4 us (0.25)
  waiting for transfers between devices: 123 us -> 16.5 us
  between operations: 14.4 us -> 0.89 us
  local copies, waits for them, and re-layouts: 18 us -> 6.77 us
  matrix products: 9.33 us -> 0 us
  other arithmetic: 9.57 us -> 0.72 us
  Pallas kernels: 0 us -> 8.73 us
    psum x1 -> x0, waiting for transfers between devices: 122 us -> none  [local(): grad_first, grad_second = lax.psum((grad_first, grad_second), 'dom')]
    ppermute x12 -> x14, waiting for transfers between devices: 1.23 us -> 16.5 us  [swapped(): return lax.ppermute(value, 'dom', pairs)]
    gather x8 -> x0, local copies, waits for them, and re-layouts: 9.44 us -> none  [the longest x4 6.6 us: fetch_inputs(): chosen = jnp.take(rows, send_rows[turn], axis=0)]
    dot_general x11 -> x0, matrix products: 9.33 us -> none  [the longest x4 3.35 us: contract_rows(): lax.dot_general(left, right, (((0,), (0,)), ((), ())), preferred_element_...]
    pallas_call x0 -> x5, Pallas kernels: none -> 8.73 us  [call(): pl.pallas_call(body, out_shape=[pltpu.VMEM(shape, dtype) for shape, dtype...]
    scatter-add x4 -> x0, other arithmetic: 5.95 us -> none  [return_grads(): total = total.at[send_rows[turn]].add(back)]
    mul x1 -> x0, other arithmetic: 2.07 us -> none  [local(): bond_tiles = local_bonds * spread_mask(tile_mask)]
    ppermute x12 -> x14, starting transfers between devices: 11.8 us -> 13.4 us  [swapped(): return lax.ppermute(value, 'dom', pairs)]
  transfers between devices with their start and end apart: 13 -> 14, of which waited for: 3 -> 9; matrix products, arithmetic and copies ran while one was open for 12% -> 2% of each run, Pallas kernels for 0% -> 5%
where the time goes in v1:
time: 47.4 us; the launch traced here: 47 us
  waiting for transfers between devices  16.5 us (35%)
  starting transfers between devices  13.4 us (28%)
  Pallas kernels  8.73 us (18%)
  local copies, waits for them, and re-layouts  6.77 us (14%)
  between operations  0.89 us (2%)
  other arithmetic  0.72 us (2%)
    ppermute x14, waiting for transfers between devices, swapped(): return lax.ppermute(value, 'dom', pairs)  16.5 us
    ppermute x14, starting transfers between devices, swapped(): return lax.ppermute(value, 'dom', pairs)  13.4 us
    pallas_call x5, Pallas kernels, call(): pl.pallas_call(body, out_shape=[pltpu.VMEM(shape, dtype) for shape, dtype...  8.73 us
    unnamed x39, local copies, waits for them, and re-layouts  6.77 us
  transfers between devices with their start and end apart: 14, of which 9 were waited for; matrix products, arithmetic and copies ran while one was open for 2% of the time, Pallas kernels for 5%

profile of v1, /device:TPU:0, one launch (start us, length us, event | category | flops | bytes accessed | tf_op | source)
XLA Modules:
  0.0 47.0 jit_solution(3315205944469927007)
XLA Ops:
  0.6 0.0 copy-start
  0.6 0.0 copy-start.2
  0.7 1.0 %copy-done.2 = bf16[1152,128]{1,0:T(8,128)(2,1)S(1)} copy-done((bf16[1152,128]{1,0:T(8,128)(2,1)S(1)}, bf16[1152,128]{1,0:T(8,128)(2,1)}, u32[]{:S(2)}) %copy-start.2) | copy-done | bytes 294936
  1.7 0.0 copy-start.18
  1.7 0.7 %copy-done.18 = s32[4,128]{1,0:T(4,128)S(1)} copy-done((s32[4,128]{1,0:T(4,128)S(1)}, s32[4,128]{1,0:T(4,128)}, u32[]{:S(2)}) %copy-start.18) | copy-done | bytes 2072
  2.4 0.8 %shard_map.104 = (bf16[512,1152]{1,0:T(8,128)(2,1)S(1)}, bf16[128,128]{1,0:T(8,128)(2,1)S(1)}, bf16[128,128]{1,0:T(8,128)(2,1)S(1)}, bf16[128,128]{1,0:T(8,128)(2,1)S(1)}, bf16[128,128]{1,0:T(8,128)(2,1)S(1)}) custom-call(bf16[1152,128]{1,0:T(8,128)(2,1)S(1)} %copy-done.2, s32[4,128]{1,0:T(4,128)S(1)} %copy-done.18), custom_call_target="tpu_custom_call" | custom-call | tf_op jit(solution)/shard_map/pallas_call | solution.py:38
  3.2 0.5 %collective-permute-start = (bf16[128,128]{1,0:T(8,128)(2,1)S(1)}, bf16[128,128]{1,0:T(8,128)(2,1)S(1)}, u32[]{:S(2)}, u32[]{:S(2)}) collective-permute-start(bf16[128,128]{1,0:T(8,128)(2,1)S(1)} %get-tuple-element.23), channel_id=1, source_target_pairs={{0,1},{1,0},{2,3},{3,2},{4,5},{5,4},{6,7},{7,6},{8,9},{9,8},{10,11... | collective-permute-start | bytes 98312 | tf_op jit(solution)/shard_map/ppermute | solution.py:17
  3.7 2.6 %collective-permute-start.1 = (bf16[128,128]{1,0:T(8,128)(2,1)S(1)}, bf16[128,128]{1,0:T(8,128)(2,1)S(1)}, u32[]{:S(2)}, u32[]{:S(2)}) collective-permute-start(bf16[128,128]{1,0:T(8,128)(2,1)S(1)} %get-tuple-element.24), channel_id=1, source_target_pairs={{0,2},{1,3},{2,0},{3,1},{4,6},{5,7},{6,4},{7,5},{8,10},{9,11},{10,... | collective-permute-start | bytes 98312 | tf_op jit(solution)/shard_map/ppermute | solution.py:17
  6.3 1.5 %collective-permute-start.2 = (bf16[128,128]{1,0:T(8,128)(2,1)S(1)}, bf16[128,128]{1,0:T(8,128)(2,1)S(1)}, u32[]{:S(2)}, u32[]{:S(2)}) collective-permute-start(bf16[128,128]{1,0:T(8,128)(2,1)S(1)} %get-tuple-element.25), channel_id=1, source_target_pairs={{0,4},{1,5},{2,6},{3,7},{4,0},{5,1},{6,2},{7,3},{8,12},{9,13},{10,... | collective-permute-start | bytes 98312 | tf_op jit(solution)/shard_map/ppermute | solution.py:17
  7.8 1.6 %collective-permute-start.3 = (bf16[128,128]{1,0:T(8,128)(2,1)S(1)}, bf16[128,128]{1,0:T(8,128)(2,1)S(1)}, u32[]{:S(2)}, u32[]{:S(2)}) collective-permute-start(bf16[128,128]{1,0:T(8,128)(2,1)S(1)} %get-tuple-element.26), channel_id=1, source_target_pairs={{0,8},{1,9},{2,10},{3,11},{4,12},{5,13},{6,14},{7,15},{8,0},{9,1},... | collective-permute-start | bytes 98312 | tf_op jit(solution)/shard_map/ppermute | solution.py:17
  9.4 0.0 copy-start.3
  9.4 1.0 %copy-done.3 = bf16[1152,128]{1,0:T(8,128)(2,1)S(1)} copy-done((bf16[1152,128]{1,0:T(8,128)(2,1)S(1)}, bf16[1152,128]{1,0:T(8,128)(2,1)}, u32[]{:S(2)}) %copy-start.3) | copy-done | bytes 294936
  10.3 1.7 %copy-done.5 = bf16[1152,1152]{1,0:T(8,128)(2,1)S(1)} copy-done((bf16[1152,1152]{1,0:T(8,128)(2,1)S(1)}, bf16[1152,1152]{1,0:T(8,128)(2,1)}, u32[]{:S(2)}) %copy-start.5) | copy-done | bytes 2654232
  12.1 0.7 %copy-done.17 = s32[18,18]{1,0:T(8,128)S(1)} copy-done((s32[18,18]{1,0:T(8,128)S(1)}, s32[18,18]{1,0:T(8,128)}, u32[]{:S(2)}) %copy-start.17) | copy-done | bytes 1320
  12.8 1.1 %shard_map.103 = (bf16[1152,1152]{1,0:T(8,128)(2,1)S(1)}, f32[1152,128]{1,0:T(8,128)S(1)}) custom-call(bf16[1152,1152]{1,0:T(8,128)(2,1)S(1)} %copy-done.5, s32[18,18]{1,0:T(8,128)S(1)} %copy-done.17, bf16[1152,128]{1,0:T(8,128)(2,1)S(1)} %copy-done.3), custom_call_target="tpu_custom_call" | custom-call | tf_op jit(solution)/shard_map/pallas_call | solution.py:38
  13.9 0.0 collective-permute-done.halo0
  13.9 0.0 copy-start.8
  13.9 0.0 collective-permute-done.1.halo1
  13.9 0.0 copy-start.10
  13.9 0.0 collective-permute-done.2.halo2
  13.9 0.0 copy-start.12
  13.9 0.0 collective-permute-done.3.halo3
  13.9 0.0 copy-start.14
  14.0 0.0 copy-done
  14.0 0.0 copy-start.6
  14.0 2.0 %shard_map.105 = (bf16[1152,128]{1,0:T(8,128)(2,1)S(1)}, bf16[128,128]{1,0:T(8,128)(2,1)}, bf16[128,128]{1,0:T(8,128)(2,1)}, bf16[128,128]{1,0:T(8,128)(2,1)}, bf16[128,128]{1,0:T(8,128)(2,1)}) custom-call(f32[1152,128]{1,0:T(8,128)S(1)} %get-tuple-element.21.inner, bf16[1152,512]{1,0:T(8,128)(2,1)S(1)} %copy-done, ...), custom_call_target="tpu_custom_call" | custom-call | tf_op jit(solution)/shard_map/pallas_call | solution.py:38
  16.0 0.0 copy-done.8
  16.0 0.0 copy-done.10
  16.0 0.0 collective-permute-start.4
  16.0 0.0 copy-done.12
  16.0 0.0 copy-done.14
  16.0 0.6 %collective-permute-start.5 = (bf16[128,128]{1,0:T(8,128)(2,1)}, bf16[128,128]{1,0:T(8,128)(2,1)}, u32[]{:S(2)}, u32[]{:S(2)}) collective-permute-start(bf16[128,128]{1,0:T(8,128)(2,1)} %get-tuple-element.33), channel_id=1, source_target_pairs={{0,2},{1,3},{2,0},{3,1},{4,6},{5,7},{6,4},{7,5},{8,10},{9,11},{10,... | collective-permute-start | bytes 98312 | tf_op jit(solution)/shard_map/ppermute | solution.py:17
  16.6 0.5 %collective-permute-start.6 = (bf16[128,128]{1,0:T(8,128)(2,1)}, bf16[128,128]{1,0:T(8,128)(2,1)}, u32[]{:S(2)}, u32[]{:S(2)}) collective-permute-start(bf16[128,128]{1,0:T(8,128)(2,1)} %get-tuple-element.34), channel_id=1, source_target_pairs={{0,4},{1,5},{2,6},{3,7},{4,0},{5,1},{6,2},{7,3},{8,12},{9,13},{10,... | collective-permute-start | bytes 98312 | tf_op jit(solution)/shard_map/ppermute | solution.py:17
  17.1 0.0 collective-permute-start.7
  17.1 0.0 copy-done.4
  17.1 0.8 %copy-done.7 = bf16[128,128]{1,0:T(8,128)(2,1)S(1)} copy-done((bf16[128,128]{1,0:T(8,128)(2,1)S(1)}, bf16[128,128]{1,0:T(8,128)(2,1)}, u32[]{:S(2)}) %copy-start.7) | copy-done | bytes 32792
  18.0 0.0 copy-start.16
  18.0 1.1 %shard_map.106 = (bf16[1152,128]{1,0:T(8,128)(2,1)S(1)}, f32[1152,128]{1,0:T(8,128)S(1)}, f32[1152,128]{1,0:T(8,128)S(1)}) custom-call(bf16[1152,128]{1,0:T(8,128)(2,1)S(1)} %get-tuple-element.27.agg, bf16[128,128]{1,0:T(8,128)(2,1)S(1)} %copy-done.7, bf16[1152,128]{1,0:T(8,128)(2,1)S(1)} %copy-done.4, bf16[1152,1152]{1,0:T(8,128)(2,1)S(1)} %get-tuple-element.28.bonds), custom_call_target="tpu_custom_call" | custom-call | tf_op jit(solution)/shard_map/pallas_call | solution.py:38
  19.2 0.0 collective-permute-done.4.agg0
  19.2 1.1 %collective-permute-done.5.agg1 = bf16[128,128]{1,0:T(8,128)(2,1)} collective-permute-done((bf16[128,128]{1,0:T(8,128)(2,1)}, bf16[128,128]{1,0:T(8,128)(2,1)}, u32[]{:S(2)}, u32[]{:S(2)}) %collective-permute-start.5) | collective-permute-done | bytes 32800 | tf_op jit(solution)/shard_map/ppermute | solution.py:17
  20.3 0.5 %collective-permute-done.6.agg2 = bf16[128,128]{1,0:T(8,128)(2,1)} collective-permute-done((bf16[128,128]{1,0:T(8,128)(2,1)}, bf16[128,128]{1,0:T(8,128)(2,1)}, u32[]{:S(2)}, u32[]{:S(2)}) %collective-permute-start.6) | collective-permute-done | bytes 32800 | tf_op jit(solution)/shard_map/ppermute | solution.py:17
  20.9 0.5 %collective-permute-done.7.agg3 = bf16[128,128]{1,0:T(8,128)(2,1)} collective-permute-done((bf16[128,128]{1,0:T(8,128)(2,1)}, bf16[128,128]{1,0:T(8,128)(2,1)}, u32[]{:S(2)}, u32[]{:S(2)}) %collective-permute-start.7) | collective-permute-done | bytes 32800 | tf_op jit(solution)/shard_map/ppermute | solution.py:17
  21.4 0.0 copy-done.6
  21.4 0.0 copy-done.1
  21.4 0.0 copy-done.9
  21.4 0.0 copy-done.11
  21.4 0.0 copy-done.13
  21.4 0.0 copy-done.15
  21.4 0.0 copy-done.16
  21.4 3.7 %shard_map.107 = (bf16[1152,128]{1,0:T(8,128)(2,1)S(1)}, f32[128,128]{1,0:T(8,128)S(1)}, f32[128,128]{1,0:T(8,128)S(1)}) custom-call(f32[1152,128]{1,0:T(8,128)S(1)} %get-tuple-element.29.inner, bf16[1152,128]{1,0:T(8,128)(2,1)S(1)} %get-tuple-element.30.hidden, f32[1152,128]{1,0:T(8,128)S(1)} %get-tuple-element.31.slope, ...), custom_call_target="tpu_custom_call" | custom-call | tf_op jit(solution)/shard_map/pallas_call | solution.py:38
  25.1 0.1 collective-permute-start.8
  25.2 1.2 %collective-permute-done.8 = f32[128,128]{1,0:T(8,128)S(1)} collective-permute-done((f32[128,128]{1,0:T(8,128)S(1)}, f32[128,128]{1,0:T(8,128)S(1)}, u32[]{:S(2)}, u32[]{:S(2)}) %collective-permute-start.8) | collective-permute-done | bytes 65568 | tf_op jit(solution)/shard_map/ppermute | solution.py:17
  26.5 1.6 %collective-permute-start.9 = (f32[128,128]{1,0:T(8,128)S(1)}, f32[128,128]{1,0:T(8,128)S(1)}, u32[]{:S(2)}, u32[]{:S(2)}) collective-permute-start(f32[128,128]{1,0:T(8,128)S(1)} %select_add_fusion), channel_id=1, source_target_pairs={{0,2},{1,3},{2,0},{3,1},{4,6},{5,7},{6,4},{7,5},{8,10},{9,11},{10,... | collective-permute-start | bytes 196616 | tf_op jit(solution)/shard_map/ppermute | solution.py:17
  28.0 2.8 %collective-permute-done.9 = f32[128,128]{1,0:T(8,128)S(1)} collective-permute-done((f32[128,128]{1,0:T(8,128)S(1)}, f32[128,128]{1,0:T(8,128)S(1)}, u32[]{:S(2)}, u32[]{:S(2)}) %collective-permute-start.9) | collective-permute-done | bytes 65568 | tf_op jit(solution)/shard_map/ppermute | solution.py:17
  30.8 1.6 %collective-permute-start.10 = (f32[128,128]{1,0:T(8,128)S(1)}, f32[128,128]{1,0:T(8,128)S(1)}, u32[]{:S(2)}, u32[]{:S(2)}) collective-permute-start(f32[128,128]{1,0:T(8,128)S(1)} %add.21), channel_id=1, source_target_pairs={{0,4},{1,5},{2,6},{3,7},{4,0},{5,1},{6,2},{7,3},{8,12},{9,13},{10,... | collective-permute-start | bytes 196616 | tf_op jit(solution)/shard_map/ppermute | solution.py:17
  32.4 2.7 %collective-permute-done.10 = f32[128,128]{1,0:T(8,128)S(1)} collective-permute-done((f32[128,128]{1,0:T(8,128)S(1)}, f32[128,128]{1,0:T(8,128)S(1)}, u32[]{:S(2)}, u32[]{:S(2)}) %collective-permute-start.10) | collective-permute-done | bytes 65568 | tf_op jit(solution)/shard_map/ppermute | solution.py:17
  35.2 0.2 collective-permute-start.11
  35.3 4.2 %collective-permute-done.11 = f32[128,128]{1,0:T(8,128)S(1)} collective-permute-done((f32[128,128]{1,0:T(8,128)S(1)}, f32[128,128]{1,0:T(8,128)S(1)}, u32[]{:S(2)}, u32[]{:S(2)}) %collective-permute-start.11) | collective-permute-done | bytes 65568 | tf_op jit(solution)/shard_map/ppermute | solution.py:17
  39.5 2.7 %collective-permute-start.12 = (f32[128,128]{1,0:T(8,128)S(1)}, f32[128,128]{1,0:T(8,128)S(1)}, u32[]{:S(2)}, u32[]{:S(2)}) collective-permute-start(f32[128,128]{1,0:T(8,128)S(1)} %add.23), channel_id=1, source_target_pairs={{0,16},{1,17},{2,18},{3,19},{4,20},{5,21},{6,22},{7,23},{8,24},{9,... | collective-permute-start | bytes 196616 | tf_op jit(solution)/shard_map/ppermute | solution.py:17
  42.2 2.8 %collective-permute-done.12 = f32[128,128]{1,0:T(8,128)S(1)} collective-permute-done((f32[128,128]{1,0:T(8,128)S(1)}, f32[128,128]{1,0:T(8,128)S(1)}, u32[]{:S(2)}, u32[]{:S(2)}) %collective-permute-start.12) | collective-permute-done | bytes 65568 | tf_op jit(solution)/shard_map/ppermute | solution.py:17
  45.0 0.1 collective-permute-start.13
  45.1 0.7 %copy.11 = bf16[1152,128]{1,0:T(8,128)(2,1)} copy(bf16[1152,128]{1,0:T(8,128)(2,1)S(1)} %get-tuple-element.41) | data formatting | bytes 589824
  45.8 0.5 %collective-permute-done.13 = f32[128,128]{1,0:T(8,128)S(1)} collective-permute-done((f32[128,128]{1,0:T(8,128)S(1)}, f32[128,128]{1,0:T(8,128)S(1)}, u32[]{:S(2)}, u32[]{:S(2)}) %collective-permute-start.13) | collective-permute-done | bytes 65568 | tf_op jit(solution)/shard_map/ppermute | solution.py:17
  46.3 0.7 %broadcast_select_fusion = (f32[128,128]{1,0:T(8,128)}, f32[128,128]{1,0:T(8,128)}) fusion(f32[128,128]{1,0:T(8,128)S(1)} %collective-permute-done.13, f32[128,128]{1,0:T(8,128)S(1)} %add.24, pred[]{:T(512)S(6)} %eq.5), kind=kLoop, calls=%fused_computation.1 | loop fusion | flops 32768 | bytes 262145 | tf_op jit(solution)/shard_map/jit(_where)/select_n | solution.py:146
  (15 shorter events, 0.1 us)
Async XLA Ops:
  0.6 13.3 %copy-start = (bf16[1152,512]{1,0:T(8,128)(2,1)S(1)}, bf16[1152,512]{1,0:T(8,128)(2,1)}, u32[]{:S(2)}) copy-start(bf16[1152,512]{1,0:T(8,128)(2,1)} %halo_bonds.3) | copy-start | bytes 3538948
  0.6 1.1 %copy-start.2 = (bf16[1152,128]{1,0:T(8,128)(2,1)S(1)}, bf16[1152,128]{1,0:T(8,128)(2,1)}, u32[]{:S(2)}) copy-start(bf16[1152,128]{1,0:T(8,128)(2,1)} %features.5) | copy-start | bytes 884740
  1.7 0.7 %copy-start.18 = (s32[4,128]{1,0:T(4,128)S(1)}, s32[4,128]{1,0:T(4,128)}, u32[]{:S(2)}) copy-start(s32[4,128]{1,0:T(4,128)} %send_rows.1) | copy-start | bytes 6148
  3.2 10.7 %collective-permute-start = (bf16[128,128]{1,0:T(8,128)(2,1)S(1)}, bf16[128,128]{1,0:T(8,128)(2,1)S(1)}, u32[]{:S(2)}, u32[]{:S(2)}) collective-permute-start(bf16[128,128]{1,0:T(8,128)(2,1)S(1)} %get-tuple-element.23), channel_id=1, source_target_pairs={{0,1},{1,0},{2,3},{3,2},{4,5},{5,4},{6,7},{7,6},{8,9},{9,8},{10,11... | collective-permute-start | bytes 98312 | tf_op jit(solution)/shard_map/ppermute | solution.py:17
  3.7 10.2 %collective-permute-start.1 = (bf16[128,128]{1,0:T(8,128)(2,1)S(1)}, bf16[128,128]{1,0:T(8,128)(2,1)S(1)}, u32[]{:S(2)}, u32[]{:S(2)}) collective-permute-start(bf16[128,128]{1,0:T(8,128)(2,1)S(1)} %get-tuple-element.24), channel_id=1, source_target_pairs={{0,2},{1,3},{2,0},{3,1},{4,6},{5,7},{6,4},{7,5},{8,10},{9,11},{10,... | collective-permute-start | bytes 98312 | tf_op jit(solution)/shard_map/ppermute | solution.py:17
  6.3 7.6 %collective-permute-start.2 = (bf16[128,128]{1,0:T(8,128)(2,1)S(1)}, bf16[128,128]{1,0:T(8,128)(2,1)S(1)}, u32[]{:S(2)}, u32[]{:S(2)}) collective-permute-start(bf16[128,128]{1,0:T(8,128)(2,1)S(1)} %get-tuple-element.25), channel_id=1, source_target_pairs={{0,4},{1,5},{2,6},{3,7},{4,0},{5,1},{6,2},{7,3},{8,12},{9,13},{10,... | collective-permute-start | bytes 98312 | tf_op jit(solution)/shard_map/ppermute | solution.py:17
  7.8 6.1 %collective-permute-start.3 = (bf16[128,128]{1,0:T(8,128)(2,1)S(1)}, bf16[128,128]{1,0:T(8,128)(2,1)S(1)}, u32[]{:S(2)}, u32[]{:S(2)}) collective-permute-start(bf16[128,128]{1,0:T(8,128)(2,1)S(1)} %get-tuple-element.26), channel_id=1, source_target_pairs={{0,8},{1,9},{2,10},{3,11},{4,12},{5,13},{6,14},{7,15},{8,0},{9,1},... | collective-permute-start | bytes 98312 | tf_op jit(solution)/shard_map/ppermute | solution.py:17
  9.4 1.0 %copy-start.3 = (bf16[1152,128]{1,0:T(8,128)(2,1)S(1)}, bf16[1152,128]{1,0:T(8,128)(2,1)}, u32[]{:S(2)}) copy-start(bf16[1152,128]{1,0:T(8,128)(2,1)} %features.5) | copy-start | bytes 884740
  10.3 1.7 %copy-start.5 = (bf16[1152,1152]{1,0:T(8,128)(2,1)S(1)}, bf16[1152,1152]{1,0:T(8,128)(2,1)}, u32[]{:S(2)}) copy-start(bf16[1152,1152]{1,0:T(8,128)(2,1)} %local_bonds.1) | copy-start | bytes 7962628
  12.1 0.7 %copy-start.17 = (s32[18,18]{1,0:T(8,128)S(1)}, s32[18,18]{1,0:T(8,128)}, u32[]{:S(2)}) copy-start(s32[18,18]{1,0:T(8,128)} %tile_mask.1) | copy-start | bytes 3892
  12.8 4.3 %copy-start.4 = (bf16[1152,128]{1,0:T(8,128)(2,1)S(1)}, bf16[1152,128]{1,0:T(8,128)(2,1)}, u32[]{:S(2)}) copy-start(bf16[1152,128]{1,0:T(8,128)(2,1)} %features.5) | copy-start | bytes 884740
  13.9 2.1 %copy-start.8 = (bf16[128,128]{1,0:T(8,128)(2,1)}, bf16[128,128]{1,0:T(8,128)(2,1)S(1)}, u32[]{:S(2)}) copy-start(bf16[128,128]{1,0:T(8,128)(2,1)S(1)} %collective-permute-done.halo0) | copy-start | bytes 98308
  13.9 2.1 %copy-start.10 = (bf16[128,128]{1,0:T(8,128)(2,1)}, bf16[128,128]{1,0:T(8,128)(2,1)S(1)}, u32[]{:S(2)}) copy-start(bf16[128,128]{1,0:T(8,128)(2,1)S(1)} %collective-permute-done.1.halo1) | copy-start | bytes 98308
  13.9 2.1 %copy-start.12 = (bf16[128,128]{1,0:T(8,128)(2,1)}, bf16[128,128]{1,0:T(8,128)(2,1)S(1)}, u32[]{:S(2)}) copy-start(bf16[128,128]{1,0:T(8,128)(2,1)S(1)} %collective-permute-done.2.halo2) | copy-start | bytes 98308
  13.9 2.1 %copy-start.14 = (bf16[128,128]{1,0:T(8,128)(2,1)}, bf16[128,128]{1,0:T(8,128)(2,1)S(1)}, u32[]{:S(2)}) copy-start(bf16[128,128]{1,0:T(8,128)(2,1)S(1)} %collective-permute-done.3.halo3) | copy-start | bytes 98308
  14.0 7.4 %copy-start.6 = (bf16[1152,128]{1,0:T(8,128)(2,1)S(1)}, bf16[1152,128]{1,0:T(8,128)(2,1)}, u32[]{:S(2)}) copy-start(bf16[1152,128]{1,0:T(8,128)(2,1)} %targets.1) | copy-start | bytes 884740
  16.0 3.2 %collective-permute-start.4 = (bf16[128,128]{1,0:T(8,128)(2,1)}, bf16[128,128]{1,0:T(8,128)(2,1)}, u32[]{:S(2)}, u32[]{:S(2)}) collective-permute-start(bf16[128,128]{1,0:T(8,128)(2,1)} %get-tuple-element.32), channel_id=1, source_target_pairs={{0,1},{1,0},{2,3},{3,2},{4,5},{5,4},{6,7},{7,6},{8,9},{9,8},{10,11... | collective-permute-start | bytes 98312 | tf_op jit(solution)/shard_map/ppermute | solution.py:17
  16.0 4.3 %collective-permute-start.5 = (bf16[128,128]{1,0:T(8,128)(2,1)}, bf16[128,128]{1,0:T(8,128)(2,1)}, u32[]{:S(2)}, u32[]{:S(2)}) collective-permute-start(bf16[128,128]{1,0:T(8,128)(2,1)} %get-tuple-element.33), channel_id=1, source_target_pairs={{0,2},{1,3},{2,0},{3,1},{4,6},{5,7},{6,4},{7,5},{8,10},{9,11},{10,... | collective-permute-start | bytes 98312 | tf_op jit(solution)/shard_map/ppermute | solution.py:17
  16.6 4.2 %collective-permute-start.6 = (bf16[128,128]{1,0:T(8,128)(2,1)}, bf16[128,128]{1,0:T(8,128)(2,1)}, u32[]{:S(2)}, u32[]{:S(2)}) collective-permute-start(bf16[128,128]{1,0:T(8,128)(2,1)} %get-tuple-element.34), channel_id=1, source_target_pairs={{0,4},{1,5},{2,6},{3,7},{4,0},{5,1},{6,2},{7,3},{8,12},{9,13},{10,... | collective-permute-start | bytes 98312 | tf_op jit(solution)/shard_map/ppermute | solution.py:17
  17.1 4.2 %collective-permute-start.7 = (bf16[128,128]{1,0:T(8,128)(2,1)}, bf16[128,128]{1,0:T(8,128)(2,1)}, u32[]{:S(2)}, u32[]{:S(2)}) collective-permute-start(bf16[128,128]{1,0:T(8,128)(2,1)} %get-tuple-element.35), channel_id=1, source_target_pairs={{0,8},{1,9},{2,10},{3,11},{4,12},{5,13},{6,14},{7,15},{8,0},{9,1},... | collective-permute-start | bytes 98312 | tf_op jit(solution)/shard_map/ppermute | solution.py:17
  17.1 4.2 %copy-start.1 = (bf16[1152,512]{1,0:T(8,128)(2,1)S(1)}, bf16[1152,512]{1,0:T(8,128)(2,1)}, u32[]{:S(2)}) copy-start(bf16[1152,512]{1,0:T(8,128)(2,1)} %halo_bonds.3) | copy-start | bytes 3538948
  17.1 0.9 %copy-start.7 = (bf16[128,128]{1,0:T(8,128)(2,1)S(1)}, bf16[128,128]{1,0:T(8,128)(2,1)}, u32[]{:S(2)}) copy-start(bf16[128,128]{1,0:T(8,128)(2,1)} %first_weight.3) | copy-start | bytes 98308
  18.0 3.4 %copy-start.9 = (bf16[128,128]{1,0:T(8,128)(2,1)S(1)}, bf16[128,128]{1,0:T(8,128)(2,1)}, u32[]{:S(2)}) copy-start(bf16[128,128]{1,0:T(8,128)(2,1)} %copy-done.8) | copy-start | bytes 98308
  18.0 3.4 %copy-start.11 = (bf16[128,128]{1,0:T(8,128)(2,1)S(1)}, bf16[128,128]{1,0:T(8,128)(2,1)}, u32[]{:S(2)}) copy-start(bf16[128,128]{1,0:T(8,128)(2,1)} %copy-done.10) | copy-start | bytes 98308
  18.0 3.4 %copy-start.13 = (bf16[128,128]{1,0:T(8,128)(2,1)S(1)}, bf16[128,128]{1,0:T(8,128)(2,1)}, u32[]{:S(2)}) copy-start(bf16[128,128]{1,0:T(8,128)(2,1)} %copy-done.12) | copy-start | bytes 98308
  18.0 3.4 %copy-start.15 = (bf16[128,128]{1,0:T(8,128)(2,1)S(1)}, bf16[128,128]{1,0:T(8,128)(2,1)}, u32[]{:S(2)}) copy-start(bf16[128,128]{1,0:T(8,128)(2,1)} %copy-done.14) | copy-start | bytes 98308
  18.0 3.4 %copy-start.16 = (bf16[128,128]{1,0:T(8,128)(2,1)S(1)}, bf16[128,128]{1,0:T(8,128)(2,1)}, u32[]{:S(2)}) copy-start(bf16[128,128]{1,0:T(8,128)(2,1)} %second_weight.1) | copy-start | bytes 98308
  25.1 1.3 %collective-permute-start.8 = (f32[128,128]{1,0:T(8,128)S(1)}, f32[128,128]{1,0:T(8,128)S(1)}, u32[]{:S(2)}, u32[]{:S(2)}) collective-permute-start(f32[128,128]{1,0:T(8,128)S(1)} %broadcast_select_fusion.2), channel_id=1, source_target_pairs={{0,1},{1,0},{2,3},{3,2},{4,5},{5,4},{6,7},{7,6},{8,9},{9,8},{10,11... | collective-permute-start | bytes 196616 | tf_op jit(solution)/shard_map/ppermute | solution.py:17
  26.5 4.3 %collective-permute-start.9 = (f32[128,128]{1,0:T(8,128)S(1)}, f32[128,128]{1,0:T(8,128)S(1)}, u32[]{:S(2)}, u32[]{:S(2)}) collective-permute-start(f32[128,128]{1,0:T(8,128)S(1)} %select_add_fusion), channel_id=1, source_target_pairs={{0,2},{1,3},{2,0},{3,1},{4,6},{5,7},{6,4},{7,5},{8,10},{9,11},{10,... | collective-permute-start | bytes 196616 | tf_op jit(solution)/shard_map/ppermute | solution.py:17
  30.8 4.3 %collective-permute-start.10 = (f32[128,128]{1,0:T(8,128)S(1)}, f32[128,128]{1,0:T(8,128)S(1)}, u32[]{:S(2)}, u32[]{:S(2)}) collective-permute-start(f32[128,128]{1,0:T(8,128)S(1)} %add.21), channel_id=1, source_target_pairs={{0,4},{1,5},{2,6},{3,7},{4,0},{5,1},{6,2},{7,3},{8,12},{9,13},{10,... | collective-permute-start | bytes 196616 | tf_op jit(solution)/shard_map/ppermute | solution.py:17
  35.2 4.3 %collective-permute-start.11 = (f32[128,128]{1,0:T(8,128)S(1)}, f32[128,128]{1,0:T(8,128)S(1)}, u32[]{:S(2)}, u32[]{:S(2)}) collective-permute-start(f32[128,128]{1,0:T(8,128)S(1)} %add.22), channel_id=1, source_target_pairs={{0,8},{1,9},{2,10},{3,11},{4,12},{5,13},{6,14},{7,15},{8,0},{9,1},... | collective-permute-start | bytes 196616 | tf_op jit(solution)/shard_map/ppermute | solution.py:17
  39.5 5.5 %collective-permute-start.12 = (f32[128,128]{1,0:T(8,128)S(1)}, f32[128,128]{1,0:T(8,128)S(1)}, u32[]{:S(2)}, u32[]{:S(2)}) collective-permute-start(f32[128,128]{1,0:T(8,128)S(1)} %add.23), channel_id=1, source_target_pairs={{0,16},{1,17},{2,18},{3,19},{4,20},{5,21},{6,22},{7,23},{8,24},{9,... | collective-permute-start | bytes 196616 | tf_op jit(solution)/shard_map/ppermute | solution.py:17
  45.0 1.3 %collective-permute-start.13 = (f32[128,128]{1,0:T(8,128)S(1)}, f32[128,128]{1,0:T(8,128)S(1)}, u32[]{:S(2)}, u32[]{:S(2)}) collective-permute-start(f32[128,128]{1,0:T(8,128)S(1)} %add.24), channel_id=1, source_target_pairs={{0,1},{1,0},{2,3},{3,2},{4,5},{5,4},{6,7},{7,6},{8,9},{9,8},{10,11... | collective-permute-start | bytes 196616 | tf_op jit(solution)/shard_map/ppermute | solution.py:17

commit v2 on v1

v2 whole, which is shorter than its diff:
```python
import functools
import math

import jax
import jax.numpy as jnp
from jax import lax
from jax.experimental import pallas as pl
from jax.experimental.pallas import tpu as pltpu
from jax.sharding import PartitionSpec as P

TILE = 64
COST = pl.CostEstimate(flops=4 * 10**9, bytes_accessed=2**20, transcendentals=0)
PARAMS = pltpu.CompilerParams(vmem_limit_bytes=16 * 2**20)


def swapped(value, mask):
    pairs = [(source, source ^ mask) for source in range(lax.axis_size("dom"))]
    return lax.ppermute(value, "dom", pairs)


def dot(left, right):
    return jnp.dot(left, right, preferred_element_type=jnp.float32)


def dot_rows(left, right):
    return lax.dot_general(
        left, right, (((0,), (0,)), ((), ())), preferred_element_type=jnp.float32
    )


def dot_last(left, right):
    return lax.dot_general(
        left, right, (((1,), (1,)), ((), ())), preferred_element_type=jnp.float32
    )


def call(body, outs, *args, scratch=(), cost=None, remain=0):
    places = [pltpu.HBM] * remain + [pltpu.VMEM] * (len(args) - remain)
    args = [pltpu.with_memory_space_constraint(arg, place) for arg, place in zip(args, places)]
    return pl.pallas_call(
        body,
        out_shape=[pltpu.VMEM(shape, dtype) for shape, dtype in outs],
        in_specs=[pl.BlockSpec(memory_space=place) for place in places],
        out_specs=[pl.BlockSpec(memory_space=pltpu.VMEM)] * len(outs),
        scratch_shapes=list(scratch),
        cost_estimate=cost,
        compiler_params=PARAMS,
    )(*args)


def pick_kernel(features, send_rows, kept, picker, *rest):
    *picked, index, sems = rest
    rounds, width = send_rows.shape
    atoms = features.shape[0]
    indices = pltpu.make_async_copy(send_rows, index, sems.at[0])
    rows = pltpu.make_async_copy(features, kept, sems.at[1])
    indices.start()
    rows.start()
    column = lax.broadcasted_iota(jnp.int32, (width, atoms), 1)
    indices.wait()
    index = jnp.concatenate([index[...], jnp.zeros((8 - rounds, width), jnp.int32)], axis=0).T
    for turn in range(rounds):
        chosen = (index[:, turn : turn + 1] == column).astype(jnp.float32).astype(jnp.bfloat16)
        picker[turn * width : (turn + 1) * width, :] = chosen
    rows.wait()
    for turn, part in enumerate(picked):
        chosen = picker[turn * width : (turn + 1) * width, :]
        part[...] = dot(chosen, kept[...]).astype(jnp.bfloat16)


def inner_kernel(local_bonds, tile_mask, features, bonds, inner):
    tiles = tile_mask.shape[0]
    atoms = local_bonds.shape[0]
    spread = (
        lax.broadcasted_iota(jnp.int32, (tiles, atoms), 1) // TILE
        == lax.broadcasted_iota(jnp.int32, (tiles, atoms), 0)
    ).astype(jnp.float32).astype(jnp.bfloat16)
    wide = dot(tile_mask[...].astype(jnp.float32).astype(jnp.bfloat16), spread).astype(jnp.bfloat16)
    for tile in range(tiles):
        rows = slice(tile * TILE, (tile + 1) * TILE)
        bonds[rows, :] = local_bonds[rows, :] * wide[tile : tile + 1, :]
    inner[...] = dot(bonds[...], features[...])


def first_kernel(inner, halo_bonds, picker, *rest):
    rounds = len(rest) // 2 - 1
    halo, agg, picked, stacked = rest[:rounds], rest[rounds], rest[rounds + 1 : -1], rest[-1]
    width = halo[0].shape[0]
    for turn, part in enumerate(halo):
        stacked[turn * width : (turn + 1) * width, :] = part[...]
    agg[...] = (inner[...] + dot(halo_bonds[...], stacked[...])).astype(jnp.bfloat16)
    for turn, part in enumerate(picked):
        chosen = picker[turn * width : (turn + 1) * width, :]
        part[...] = dot(chosen, agg[...]).astype(jnp.bfloat16)


def hidden_kernel(agg, first_weight, features, bonds, hidden, slope, inner):
    pre = dot(agg[...], first_weight[...])
    sigm = jax.nn.sigmoid(pre)
    slope[...] = (sigm * (1.0 + pre * (1.0 - sigm))).T
    hidden[...] = (features[...].astype(jnp.float32) + pre * sigm).astype(jnp.bfloat16)
    inner[...] = dot(bonds[...], hidden[...])


def back_kernel(
    scale,
    inner,
    hidden,
    slope,
    agg,
    bonds,
    halo_bonds,
    targets,
    first_weight,
    second_weight,
    *rest,
):
    *halo, prediction, kept, given, halo_hidden, halo_agg = rest
    rounds = len(halo) // 2
    width = halo[0].shape[0]
    spans = [slice(turn * width, (turn + 1) * width) for turn in range(rounds)]
    for span, part in zip(spans, halo[rounds:]):
        halo_agg[span, :] = part[...]
    pre = dot(halo_agg[...], first_weight[...])
    sigm = jax.nn.sigmoid(pre)
    halo_slope = (sigm * (1.0 + pre * (1.0 - sigm))).T
    act = pre * sigm
    for span, part in zip(spans, halo[:rounds]):
        halo_hidden[span, :] = (part[...].astype(jnp.float32) + act[span]).astype(jnp.bfloat16)
    second_agg = (inner[...] + dot(halo_bonds[...], halo_hidden[...])).astype(jnp.bfloat16)
    output = hidden[...].astype(jnp.float32) + dot(second_agg, second_weight[...])
    prediction[...] = output.astype(jnp.bfloat16)
    error = (output - targets[...].astype(jnp.float32)) * scale
    error_b = error.astype(jnp.bfloat16)
    agg_cot = dot_last(second_weight[...], error_b).astype(jnp.bfloat16)
    halo_cot = (dot(agg_cot, halo_bonds[...]) * halo_slope).astype(jnp.bfloat16)
    own_cot = ((error.T + dot(agg_cot, bonds[...])) * slope[...]).astype(jnp.bfloat16)
    grad_first = (dot(halo_cot, halo_agg[...]) + dot(own_cot, agg[...])).T
    grad_second = dot_rows(second_agg, error_b)
    even = lax.rem(lax.axis_index("dom"), 2) == 0
    kept[...] = jnp.where(even, grad_first, grad_second)
    given[...] = jnp.where(even, grad_second, grad_first)


def split_kernel(total, other, grad_first, grad_second):
    even = lax.rem(lax.axis_index("dom"), 2) == 0
    grad_first[...] = jnp.where(even, total[...], other[...])
    grad_second[...] = jnp.where(even, other[...], total[...])


def summed(kept, given):
    total = kept + swapped(given, 1)
    mask = 2
    while mask < lax.axis_size("dom"):
        total = total + swapped(total, mask)
        mask *= 2
    whole = pl.BlockSpec(memory_space=pltpu.VMEM)
    return pl.pallas_call(
        split_kernel,
        out_shape=[jax.ShapeDtypeStruct(total.shape, total.dtype)] * 2,
        in_specs=[whole] * 2,
        out_specs=[whole] * 2,
        compiler_params=PARAMS,
    )(total, swapped(total, 1))


def local(
    features, targets, first_weight, second_weight, local_bonds, halo_bonds, tile_mask, send_rows
):
    atoms, wide = features.shape
    rounds, width = send_rows.shape
    low, high = jnp.bfloat16, jnp.float32
    sent = [((width, wide), low)] * rounds
    stacked = pltpu.VMEM((rounds * width, wide), low)
    features, picker, *picked = call(
        pick_kernel,
        [((atoms, wide), low), ((rounds * width, atoms), low)] + sent,
        features,
        send_rows,
        remain=2,
        scratch=[pltpu.VMEM((rounds, width), jnp.int32), pltpu.SemaphoreType.DMA((2,))],
        cost=COST,
    )
    halo = [swapped(part, 2**turn) for turn, part in enumerate(picked)]
    bonds, inner = call(
        inner_kernel,
        [((atoms, atoms), low), ((atoms, wide), high)],
        local_bonds,
        tile_mask,
        features,
    )
    agg, *picked = call(
        first_kernel,
        [((atoms, wide), low)] + sent,
        inner,
        halo_bonds,
        picker,
        *halo,
        scratch=[stacked],
    )
    halo_agg = [swapped(part, 2**turn) for turn, part in enumerate(picked)]
    hidden, slope, inner = call(
        hidden_kernel,
        [((atoms, wide), low), ((wide, atoms), high), ((atoms, wide), high)],
        agg,
        first_weight,
        features,
        bonds,
    )
    scale = 1.0 / math.sqrt(atoms * lax.axis_size("dom"))
    prediction, kept, given = call(
        functools.partial(back_kernel, scale),
        [((atoms, wide), low), ((wide, wide), high), ((wide, wide), high)],
        inner,
        hidden,
        slope,
        agg,
        bonds,
        halo_bonds,
        targets,
        first_weight,
        second_weight,
        *halo,
        *halo_agg,
        scratch=[stacked, stacked],
    )
    return (prediction, *summed(kept, given))


def solution(mesh):
    rows = P("dom", None)
    in_specs = (rows, rows, P(), P(), rows, rows, rows, rows)
    out_specs = (rows, P(), P())
    return jax.shard_map(local, mesh=mesh, in_specs=in_specs, out_specs=out_specs, check_vma=False)
```

time: 47.4 us -> 40.8 us (0.86)
  local copies, waits for them, and re-layouts: 6.77 us -> 0.74 us
  starting transfers between devices: 13.4 us -> 18.7 us
  waiting for transfers between devices: 16.5 us -> 13.1 us
  Pallas kernels: 8.73 us -> 7.26 us
  other arithmetic: 0.72 us -> 0.05 us
    unnamed x39 -> x13, local copies, waits for them, and re-layouts: 6.77 us -> 0.74 us
    ppermute x14, starting transfers between devices: 13.4 us -> 18.7 us  [swapped(): return lax.ppermute(value, 'dom', pairs)]
    ppermute x14, waiting for transfers between devices: 16.5 us -> 13.1 us  [swapped(): return lax.ppermute(value, 'dom', pairs)]
    pallas_call x5, Pallas kernels: 8.73 us -> 6.6 us  [call(): pl.pallas_call(body, out_shape=[pltpu.VMEM(shape, dtype) for shape, dtype...]
    select_n x2 -> x0, other arithmetic: 0.67 us -> none  [the longest x1 0.66 us: summed(): return (jnp.where(even, total, other), jnp.where(even, other, total))]
    pallas_call x0 -> x1, Pallas kernels: none -> 0.66 us  [summed(): pl.pallas_call(split_kernel, out_shape=[jax.ShapeDtypeStruct(total.shape,...]
  transfers between devices with their start and end apart: 14 -> 14, of which waited for: 9 -> 10; matrix products, arithmetic and copies ran while one was open for 2% -> 2% of each run, Pallas kernels for 5% -> 5%
where the time goes in v2:
time: 40.8 us; the launch traced here: 40.6 us
  starting transfers between devices  18.7 us (46%)
  waiting for transfers between devices  13.1 us (32%)
  Pallas kernels  7.26 us (18%)
  between operations  0.77 us (2%)
  local copies, waits for them, and re-layouts  0.74 us (2%)
    ppermute x14, starting transfers between devices, swapped(): return lax.ppermute(value, 'dom', pairs)  18.7 us
    ppermute x14, waiting for transfers between devices, swapped(): return lax.ppermute(value, 'dom', pairs)  13.1 us
    pallas_call x5, Pallas kernels, call(): pl.pallas_call(body, out_shape=[pltpu.VMEM(shape, dtype) for shape, dtype...  6.6 us
  transfers between devices with their start and end apart: 14, of which 10 were waited for; matrix products, arithmetic and copies ran while one was open for 2% of the time, Pallas kernels for 5%

profile of v2, /device:TPU:0, one launch (start us, length us, event | category | flops | bytes accessed | tf_op | source)
XLA Modules:
  0.0 40.6 jit_solution(13673018819406163633)
XLA Ops:
  0.6 0.0 copy-start.5
  0.6 0.0 copy-start.1
  0.7 1.7 %shard_map.103 = (bf16[1152,128]{1,0:T(8,128)(2,1)S(1)}, bf16[512,1152]{1,0:T(8,128)(2,1)S(1)}, bf16[128,128]{1,0:T(8,128)(2,1)S(1)}, bf16[128,128]{1,0:T(8,128)...) custom-call(bf16[1152,128]{1,0:T(8,128)(2,1)} %features.1, s32[4,128]{1,0:T(4,128)} %send_rows.1), custom_call_target="tpu_custom_call" | custom-call | flops 4000000000 | bytes 1048576 | tf_op jit(solution)/shard_map/pallas_call | solution.py:40
  2.3 0.0 copy-start
  2.3 0.5 %collective-permute-start = (bf16[128,128]{1,0:T(8,128)(2,1)S(1)}, bf16[128,128]{1,0:T(8,128)(2,1)S(1)}, u32[]{:S(2)}, u32[]{:S(2)}) collective-permute-start(bf16[128,128]{1,0:T(8,128)(2,1)S(1)} %get-tuple-element.27), channel_id=1, source_target_pairs={{0,1},{1,0},{2,3},{3,2},{4,5},{5,4},{6,7},{7,6},{8,9},{9,8},{10,11... | collective-permute-start | bytes 98312 | tf_op jit(solution)/shard_map/ppermute | solution.py:18
  2.8 2.6 %collective-permute-start.1 = (bf16[128,128]{1,0:T(8,128)(2,1)S(1)}, bf16[128,128]{1,0:T(8,128)(2,1)S(1)}, u32[]{:S(2)}, u32[]{:S(2)}) collective-permute-start(bf16[128,128]{1,0:T(8,128)(2,1)S(1)} %get-tuple-element.28), channel_id=1, source_target_pairs={{0,2},{1,3},{2,0},{3,1},{4,6},{5,7},{6,4},{7,5},{8,10},{9,11},{10,... | collective-permute-start | bytes 98312 | tf_op jit(solution)/shard_map/ppermute | solution.py:18
  5.4 1.5 %collective-permute-start.2 = (bf16[128,128]{1,0:T(8,128)(2,1)S(1)}, bf16[128,128]{1,0:T(8,128)(2,1)S(1)}, u32[]{:S(2)}, u32[]{:S(2)}) collective-permute-start(bf16[128,128]{1,0:T(8,128)(2,1)S(1)} %get-tuple-element.29), channel_id=1, source_target_pairs={{0,4},{1,5},{2,6},{3,7},{4,0},{5,1},{6,2},{7,3},{8,12},{9,13},{10,... | collective-permute-start | bytes 98312 | tf_op jit(solution)/shard_map/ppermute | solution.py:18
  6.9 1.6 %collective-permute-start.3 = (bf16[128,128]{1,0:T(8,128)(2,1)S(1)}, bf16[128,128]{1,0:T(8,128)(2,1)S(1)}, u32[]{:S(2)}, u32[]{:S(2)}) collective-permute-start(bf16[128,128]{1,0:T(8,128)(2,1)S(1)} %get-tuple-element.30), channel_id=1, source_target_pairs={{0,8},{1,9},{2,10},{3,11},{4,12},{5,13},{6,14},{7,15},{8,0},{9,1},... | collective-permute-start | bytes 98312 | tf_op jit(solution)/shard_map/ppermute | solution.py:18
  8.5 0.0 copy-done.5
  8.5 0.0 copy-done.1
  8.5 0.0 copy-start.3
  8.5 1.1 %shard_map.104 = (bf16[1152,1152]{1,0:T(8,128)(2,1)S(1)}, f32[1152,128]{1,0:T(8,128)S(1)}) custom-call(bf16[1152,1152]{1,0:T(8,128)(2,1)S(1)} %copy-done.1, s32[18,18]{1,0:T(8,128)S(1)} %copy-done.5, bf16[1152,128]{1,0:T(8,128)(2,1)S(1)} %get-tuple-element.24.features), custom_call_target="tpu_custom_call" | custom-call | tf_op jit(solution)/shard_map/pallas_call | solution.py:40
  9.6 0.0 collective-permute-done.rest_0_
  9.6 0.0 collective-permute-done.1.rest_1_
  9.6 0.0 collective-permute-done.2.rest_2_
  9.6 1.2 %collective-permute-done.3.rest_3_ = bf16[128,128]{1,0:T(8,128)(2,1)S(1)} collective-permute-done((bf16[128,128]{1,0:T(8,128)(2,1)S(1)}, bf16[128,128]{1,0:T(8,128)(2,1)S(1)}, u32[]{:S(2)}, u32[]{:S(2)}) %collective-permute-start.3) | collective-permute-done | bytes 32800 | tf_op jit(solution)/shard_map/ppermute | solution.py:18
  10.8 0.0 copy-done
  10.8 0.0 copy-start.2
  10.9 0.0 copy-start.4
  10.9 0.9 %shard_map.105 = (bf16[1152,128]{1,0:T(8,128)(2,1)S(1)}, bf16[128,128]{1,0:T(8,128)(2,1)S(1)}, bf16[128,128]{1,0:T(8,128)(2,1)S(1)}, bf16[128,128]{1,0:T(8,128)(2,1)S(1)}, bf16[128,128]{1,0:T(8,128)(2,1)S(1)}) custom-call(f32[1152,128]{1,0:T(8,128)S(1)} %get-tuple-element.25.inner, bf16[1152,512]{1,0:T(8,128)(2,1)S(1)} %copy-done, ...), custom_call_target="tpu_custom_call" | custom-call | tf_op jit(solution)/shard_map/pallas_call | solution.py:40
  11.8 0.1 collective-permute-start.4
  11.8 0.6 %collective-permute-start.5 = (bf16[128,128]{1,0:T(8,128)(2,1)S(1)}, bf16[128,128]{1,0:T(8,128)(2,1)S(1)}, u32[]{:S(2)}, u32[]{:S(2)}) collective-permute-start(bf16[128,128]{1,0:T(8,128)(2,1)S(1)} %get-tuple-element.37), channel_id=1, source_target_pairs={{0,2},{1,3},{2,0},{3,1},{4,6},{5,7},{6,4},{7,5},{8,10},{9,11},{10,... | collective-permute-start | bytes 98312 | tf_op jit(solution)/shard_map/ppermute | solution.py:18
  12.4 0.1 collective-permute-start.6
  12.5 2.0 %collective-permute-start.7 = (bf16[128,128]{1,0:T(8,128)(2,1)S(1)}, bf16[128,128]{1,0:T(8,128)(2,1)S(1)}, u32[]{:S(2)}, u32[]{:S(2)}) collective-permute-start(bf16[128,128]{1,0:T(8,128)(2,1)S(1)} %get-tuple-element.39), channel_id=1, source_target_pairs={{0,8},{1,9},{2,10},{3,11},{4,12},{5,13},{6,14},{7,15},{8,0},{9,1},... | collective-permute-start | bytes 98312 | tf_op jit(solution)/shard_map/ppermute | solution.py:18
  14.5 0.0 copy-done.3
  14.5 1.1 %shard_map.106 = (bf16[1152,128]{1,0:T(8,128)(2,1)S(1)}, f32[128,1152]{1,0:T(8,128)S(1)}, f32[1152,128]{1,0:T(8,128)S(1)}) custom-call(bf16[1152,128]{1,0:T(8,128)(2,1)S(1)} %get-tuple-element.31.agg, bf16[128,128]{1,0:T(8,128)(2,1)S(1)} %copy-done.3, bf16[1152,128]{1,0:T(8,128)(2,1)S(1)} %get-tuple-element.24.features, ...), custom_call_target="tpu_custom_call" | custom-call | tf_op jit(solution)/shard_map/pallas_call | solution.py:40
  15.7 0.0 collective-permute-done.4.rest_4_
  15.7 0.2 collective-permute-done.5.rest_5_
  15.8 0.5 %collective-permute-done.6.rest_6_ = bf16[128,128]{1,0:T(8,128)(2,1)S(1)} collective-permute-done((bf16[128,128]{1,0:T(8,128)(2,1)S(1)}, bf16[128,128]{1,0:T(8,128)(2,1)S(1)}, u32[]{:S(2)}, u32[]{:S(2)}) %collective-permute-start.6) | collective-permute-done | bytes 32800 | tf_op jit(solution)/shard_map/ppermute | solution.py:18
  16.4 0.1 collective-permute-done.7.rest_7_
  16.4 0.0 copy-done.2
  16.4 0.0 copy-done.4
  16.4 1.8 %shard_map.107 = (bf16[1152,128]{1,0:T(8,128)(2,1)S(1)}, f32[128,128]{1,0:T(8,128)S(1)}, f32[128,128]{1,0:T(8,128)S(1)}) custom-call(f32[1152,128]{1,0:T(8,128)S(1)} %get-tuple-element.33.inner, bf16[1152,128]{1,0:T(8,128)(2,1)S(1)} %get-tuple-element.34.hidden, f32[128,1152]{1,0:T(8,128)S(1)} %get-tuple-element.35.slope, ...), custom_call_target="tpu_custom_call" | custom-call | tf_op jit(solution)/shard_map/pallas_call | solution.py:40
  18.2 0.1 collective-permute-start.8
  18.3 1.2 %collective-permute-done.8 = f32[128,128]{1,0:T(8,128)S(1)} collective-permute-done((f32[128,128]{1,0:T(8,128)S(1)}, f32[128,128]{1,0:T(8,128)S(1)}, u32[]{:S(2)}, u32[]{:S(2)}) %collective-permute-start.8) | collective-permute-done | bytes 65568 | tf_op jit(solution)/shard_map/ppermute | solution.py:18
  19.6 2.0 %collective-permute-start.9 = (f32[128,128]{1,0:T(8,128)S(1)}, f32[128,128]{1,0:T(8,128)S(1)}, u32[]{:S(2)}, u32[]{:S(2)}) collective-permute-start(f32[128,128]{1,0:T(8,128)S(1)} %add.15), channel_id=1, source_target_pairs={{0,2},{1,3},{2,0},{3,1},{4,6},{5,7},{6,4},{7,5},{8,10},{9,11},{10,... | collective-permute-start | bytes 196616 | tf_op jit(solution)/shard_map/ppermute | solution.py:18
  21.6 2.4 %collective-permute-done.9 = f32[128,128]{1,0:T(8,128)S(1)} collective-permute-done((f32[128,128]{1,0:T(8,128)S(1)}, f32[128,128]{1,0:T(8,128)S(1)}, u32[]{:S(2)}, u32[]{:S(2)}) %collective-permute-start.9) | collective-permute-done | bytes 65568 | tf_op jit(solution)/shard_map/ppermute | solution.py:18
  24.0 1.9 %collective-permute-start.10 = (f32[128,128]{1,0:T(8,128)S(1)}, f32[128,128]{1,0:T(8,128)S(1)}, u32[]{:S(2)}, u32[]{:S(2)}) collective-permute-start(f32[128,128]{1,0:T(8,128)S(1)} %add.16), channel_id=1, source_target_pairs={{0,4},{1,5},{2,6},{3,7},{4,0},{5,1},{6,2},{7,3},{8,12},{9,13},{10,... | collective-permute-start | bytes 196616 | tf_op jit(solution)/shard_map/ppermute | solution.py:18
  26.0 2.4 %collective-permute-done.10 = f32[128,128]{1,0:T(8,128)S(1)} collective-permute-done((f32[128,128]{1,0:T(8,128)S(1)}, f32[128,128]{1,0:T(8,128)S(1)}, u32[]{:S(2)}, u32[]{:S(2)}) %collective-permute-start.10) | collective-permute-done | bytes 65568 | tf_op jit(solution)/shard_map/ppermute | solution.py:18
  28.4 2.0 %collective-permute-start.11 = (f32[128,128]{1,0:T(8,128)S(1)}, f32[128,128]{1,0:T(8,128)S(1)}, u32[]{:S(2)}, u32[]{:S(2)}) collective-permute-start(f32[128,128]{1,0:T(8,128)S(1)} %add.17), channel_id=1, source_target_pairs={{0,8},{1,9},{2,10},{3,11},{4,12},{5,13},{6,14},{7,15},{8,0},{9,1},... | collective-permute-start | bytes 196616 | tf_op jit(solution)/shard_map/ppermute | solution.py:18
  30.4 2.3 %collective-permute-done.11 = f32[128,128]{1,0:T(8,128)S(1)} collective-permute-done((f32[128,128]{1,0:T(8,128)S(1)}, f32[128,128]{1,0:T(8,128)S(1)}, u32[]{:S(2)}, u32[]{:S(2)}) %collective-permute-start.11) | collective-permute-done | bytes 65568 | tf_op jit(solution)/shard_map/ppermute | solution.py:18
  32.7 3.7 %collective-permute-start.12 = (f32[128,128]{1,0:T(8,128)S(1)}, f32[128,128]{1,0:T(8,128)S(1)}, u32[]{:S(2)}, u32[]{:S(2)}) collective-permute-start(f32[128,128]{1,0:T(8,128)S(1)} %add.18), channel_id=1, source_target_pairs={{0,16},{1,17},{2,18},{3,19},{4,20},{5,21},{6,22},{7,23},{8,24},{9,... | collective-permute-start | bytes 196616 | tf_op jit(solution)/shard_map/ppermute | solution.py:18
  36.4 2.3 %collective-permute-done.12 = f32[128,128]{1,0:T(8,128)S(1)} collective-permute-done((f32[128,128]{1,0:T(8,128)S(1)}, f32[128,128]{1,0:T(8,128)S(1)}, u32[]{:S(2)}, u32[]{:S(2)}) %collective-permute-start.12) | collective-permute-done | bytes 65568 | tf_op jit(solution)/shard_map/ppermute | solution.py:18
  38.7 0.1 collective-permute-start.13
  38.7 0.7 %copy.11 = bf16[1152,128]{1,0:T(8,128)(2,1)} copy(bf16[1152,128]{1,0:T(8,128)(2,1)S(1)} %get-tuple-element.45) | data formatting | bytes 589824
  39.4 0.5 %collective-permute-done.13.other = f32[128,128]{1,0:T(8,128)S(1)} collective-permute-done((f32[128,128]{1,0:T(8,128)S(1)}, f32[128,128]{1,0:T(8,128)S(1)}, u32[]{:S(2)}, u32[]{:S(2)}) %collective-permute-start.13) | collective-permute-done | bytes 65568 | tf_op jit(solution)/shard_map/ppermute | solution.py:18
  40.0 0.7 %shard_map.108 = (f32[128,128]{1,0:T(8,128)}, f32[128,128]{1,0:T(8,128)}) custom-call(f32[128,128]{1,0:T(8,128)S(1)} %add.19.total, f32[128,128]{1,0:T(8,128)S(1)} %collective-permute-done.13.other), custom_call_target="tpu_custom_call" | custom-call | tf_op jit(solution)/shard_map/pallas_call | solution.py:158
  (5 shorter events, 0.0 us)
Async XLA Ops:
  0.6 7.9 %copy-start.5 = (s32[18,18]{1,0:T(8,128)S(1)}, s32[18,18]{1,0:T(8,128)}, u32[]{:S(2)}) copy-start(s32[18,18]{1,0:T(8,128)} %tile_mask.1) | copy-start | bytes 3892
  0.6 7.9 %copy-start.1 = (bf16[1152,1152]{1,0:T(8,128)(2,1)S(1)}, bf16[1152,1152]{1,0:T(8,128)(2,1)}, u32[]{:S(2)}) copy-start(bf16[1152,1152]{1,0:T(8,128)(2,1)} %local_bonds.1) | copy-start | bytes 7962628
  2.3 8.5 %copy-start = (bf16[1152,512]{1,0:T(8,128)(2,1)S(1)}, bf16[1152,512]{1,0:T(8,128)(2,1)}, u32[]{:S(2)}) copy-start(bf16[1152,512]{1,0:T(8,128)(2,1)} %halo_bonds.3) | copy-start | bytes 3538948
  2.3 7.3 %collective-permute-start = (bf16[128,128]{1,0:T(8,128)(2,1)S(1)}, bf16[128,128]{1,0:T(8,128)(2,1)S(1)}, u32[]{:S(2)}, u32[]{:S(2)}) collective-permute-start(bf16[128,128]{1,0:T(8,128)(2,1)S(1)} %get-tuple-element.27), channel_id=1, source_target_pairs={{0,1},{1,0},{2,3},{3,2},{4,5},{5,4},{6,7},{7,6},{8,9},{9,8},{10,11... | collective-permute-start | bytes 98312 | tf_op jit(solution)/shard_map/ppermute | solution.py:18
  2.8 6.8 %collective-permute-start.1 = (bf16[128,128]{1,0:T(8,128)(2,1)S(1)}, bf16[128,128]{1,0:T(8,128)(2,1)S(1)}, u32[]{:S(2)}, u32[]{:S(2)}) collective-permute-start(bf16[128,128]{1,0:T(8,128)(2,1)S(1)} %get-tuple-element.28), channel_id=1, source_target_pairs={{0,2},{1,3},{2,0},{3,1},{4,6},{5,7},{6,4},{7,5},{8,10},{9,11},{10,... | collective-permute-start | bytes 98312 | tf_op jit(solution)/shard_map/ppermute | solution.py:18
  5.4 4.2 %collective-permute-start.2 = (bf16[128,128]{1,0:T(8,128)(2,1)S(1)}, bf16[128,128]{1,0:T(8,128)(2,1)S(1)}, u32[]{:S(2)}, u32[]{:S(2)}) collective-permute-start(bf16[128,128]{1,0:T(8,128)(2,1)S(1)} %get-tuple-element.29), channel_id=1, source_target_pairs={{0,4},{1,5},{2,6},{3,7},{4,0},{5,1},{6,2},{7,3},{8,12},{9,13},{10,... | collective-permute-start | bytes 98312 | tf_op jit(solution)/shard_map/ppermute | solution.py:18
  6.9 3.9 %collective-permute-start.3 = (bf16[128,128]{1,0:T(8,128)(2,1)S(1)}, bf16[128,128]{1,0:T(8,128)(2,1)S(1)}, u32[]{:S(2)}, u32[]{:S(2)}) collective-permute-start(bf16[128,128]{1,0:T(8,128)(2,1)S(1)} %get-tuple-element.30), channel_id=1, source_target_pairs={{0,8},{1,9},{2,10},{3,11},{4,12},{5,13},{6,14},{7,15},{8,0},{9,1},... | collective-permute-start | bytes 98312 | tf_op jit(solution)/shard_map/ppermute | solution.py:18
  8.5 6.0 %copy-start.3 = (bf16[128,128]{1,0:T(8,128)(2,1)S(1)}, bf16[128,128]{1,0:T(8,128)(2,1)}, u32[]{:S(2)}) copy-start(bf16[128,128]{1,0:T(8,128)(2,1)} %first_weight.3) | copy-start | bytes 98308
  10.8 5.6 %copy-start.2 = (bf16[1152,128]{1,0:T(8,128)(2,1)S(1)}, bf16[1152,128]{1,0:T(8,128)(2,1)}, u32[]{:S(2)}) copy-start(bf16[1152,128]{1,0:T(8,128)(2,1)} %targets.1) | copy-start | bytes 884740
  10.9 5.6 %copy-start.4 = (bf16[128,128]{1,0:T(8,128)(2,1)S(1)}, bf16[128,128]{1,0:T(8,128)(2,1)}, u32[]{:S(2)}) copy-start(bf16[128,128]{1,0:T(8,128)(2,1)} %second_weight.1) | copy-start | bytes 98308
  11.8 3.9 %collective-permute-start.4 = (bf16[128,128]{1,0:T(8,128)(2,1)S(1)}, bf16[128,128]{1,0:T(8,128)(2,1)S(1)}, u32[]{:S(2)}, u32[]{:S(2)}) collective-permute-start(bf16[128,128]{1,0:T(8,128)(2,1)S(1)} %get-tuple-element.36), channel_id=1, source_target_pairs={{0,1},{1,0},{2,3},{3,2},{4,5},{5,4},{6,7},{7,6},{8,9},{9,8},{10,11... | collective-permute-start | bytes 98312 | tf_op jit(solution)/shard_map/ppermute | solution.py:18
  11.8 4.0 %collective-permute-start.5 = (bf16[128,128]{1,0:T(8,128)(2,1)S(1)}, bf16[128,128]{1,0:T(8,128)(2,1)S(1)}, u32[]{:S(2)}, u32[]{:S(2)}) collective-permute-start(bf16[128,128]{1,0:T(8,128)(2,1)S(1)} %get-tuple-element.37), channel_id=1, source_target_pairs={{0,2},{1,3},{2,0},{3,1},{4,6},{5,7},{6,4},{7,5},{8,10},{9,11},{10,... | collective-permute-start | bytes 98312 | tf_op jit(solution)/shard_map/ppermute | solution.py:18
  12.4 3.9 %collective-permute-start.6 = (bf16[128,128]{1,0:T(8,128)(2,1)S(1)}, bf16[128,128]{1,0:T(8,128)(2,1)S(1)}, u32[]{:S(2)}, u32[]{:S(2)}) collective-permute-start(bf16[128,128]{1,0:T(8,128)(2,1)S(1)} %get-tuple-element.38), channel_id=1, source_target_pairs={{0,4},{1,5},{2,6},{3,7},{4,0},{5,1},{6,2},{7,3},{8,12},{9,13},{10,... | collective-permute-start | bytes 98312 | tf_op jit(solution)/shard_map/ppermute | solution.py:18
  12.5 3.9 %collective-permute-start.7 = (bf16[128,128]{1,0:T(8,128)(2,1)S(1)}, bf16[128,128]{1,0:T(8,128)(2,1)S(1)}, u32[]{:S(2)}, u32[]{:S(2)}) collective-permute-start(bf16[128,128]{1,0:T(8,128)(2,1)S(1)} %get-tuple-element.39), channel_id=1, source_target_pairs={{0,8},{1,9},{2,10},{3,11},{4,12},{5,13},{6,14},{7,15},{8,0},{9,1},... | collective-permute-start | bytes 98312 | tf_op jit(solution)/shard_map/ppermute | solution.py:18
  18.2 1.3 %collective-permute-start.8 = (f32[128,128]{1,0:T(8,128)S(1)}, f32[128,128]{1,0:T(8,128)S(1)}, u32[]{:S(2)}, u32[]{:S(2)}) collective-permute-start(f32[128,128]{1,0:T(8,128)S(1)} %get-tuple-element.42), channel_id=1, source_target_pairs={{0,1},{1,0},{2,3},{3,2},{4,5},{5,4},{6,7},{7,6},{8,9},{9,8},{10,11... | collective-permute-start | bytes 196616 | tf_op jit(solution)/shard_map/ppermute | solution.py:18
  19.6 4.4 %collective-permute-start.9 = (f32[128,128]{1,0:T(8,128)S(1)}, f32[128,128]{1,0:T(8,128)S(1)}, u32[]{:S(2)}, u32[]{:S(2)}) collective-permute-start(f32[128,128]{1,0:T(8,128)S(1)} %add.15), channel_id=1, source_target_pairs={{0,2},{1,3},{2,0},{3,1},{4,6},{5,7},{6,4},{7,5},{8,10},{9,11},{10,... | collective-permute-start | bytes 196616 | tf_op jit(solution)/shard_map/ppermute | solution.py:18
  24.0 4.3 %collective-permute-start.10 = (f32[128,128]{1,0:T(8,128)S(1)}, f32[128,128]{1,0:T(8,128)S(1)}, u32[]{:S(2)}, u32[]{:S(2)}) collective-permute-start(f32[128,128]{1,0:T(8,128)S(1)} %add.16), channel_id=1, source_target_pairs={{0,4},{1,5},{2,6},{3,7},{4,0},{5,1},{6,2},{7,3},{8,12},{9,13},{10,... | collective-permute-start | bytes 196616 | tf_op jit(solution)/shard_map/ppermute | solution.py:18
  28.4 4.3 %collective-permute-start.11 = (f32[128,128]{1,0:T(8,128)S(1)}, f32[128,128]{1,0:T(8,128)S(1)}, u32[]{:S(2)}, u32[]{:S(2)}) collective-permute-start(f32[128,128]{1,0:T(8,128)S(1)} %add.17), channel_id=1, source_target_pairs={{0,8},{1,9},{2,10},{3,11},{4,12},{5,13},{6,14},{7,15},{8,0},{9,1},... | collective-permute-start | bytes 196616 | tf_op jit(solution)/shard_map/ppermute | solution.py:18
  32.7 5.9 %collective-permute-start.12 = (f32[128,128]{1,0:T(8,128)S(1)}, f32[128,128]{1,0:T(8,128)S(1)}, u32[]{:S(2)}, u32[]{:S(2)}) collective-permute-start(f32[128,128]{1,0:T(8,128)S(1)} %add.18), channel_id=1, source_target_pairs={{0,16},{1,17},{2,18},{3,19},{4,20},{5,21},{6,22},{7,23},{8,24},{9,... | collective-permute-start | bytes 196616 | tf_op jit(solution)/shard_map/ppermute | solution.py:18
  38.7 1.3 %collective-permute-start.13 = (f32[128,128]{1,0:T(8,128)S(1)}, f32[128,128]{1,0:T(8,128)S(1)}, u32[]{:S(2)}, u32[]{:S(2)}) collective-permute-start(f32[128,128]{1,0:T(8,128)S(1)} %add.19.total), channel_id=1, source_target_pairs={{0,1},{1,0},{2,3},{3,2},{4,5},{5,4},{6,7},{7,6},{8,9},{9,8},{10,11... | collective-permute-start | bytes 196616 | tf_op jit(solution)/shard_map/ppermute | solution.py:18

commit v3 on v2

--- a/solution.py
+++ b/solution.py
@@ -68,7 +68,22 @@
         part[...] = dot(chosen, kept[...]).astype(jnp.bfloat16)
 
 
-def inner_kernel(local_bonds, tile_mask, features, bonds, inner):
+def inner_kernel(
+    local_bonds,
+    tile_mask,
+    features,
+    halo_bonds,
+    picker,
+    send_rows,
+    bonds,
+    inner,
+    inner_sent,
+    halo_sent,
+    index,
+    sem,
+):
+    indices = pltpu.make_async_copy(send_rows, index, sem)
+    indices.start()
     tiles = tile_mask.shape[0]
     atoms = local_bonds.shape[0]
     spread = (
@@ -80,21 +95,31 @@
         rows = slice(tile * TILE, (tile + 1) * TILE)
         bonds[rows, :] = local_bonds[rows, :] * wide[tile : tile + 1, :]
     inner[...] = dot(bonds[...], features[...])
-
-
-def first_kernel(inner, halo_bonds, picker, *rest):
-    rounds = len(rest) // 2 - 1
-    halo, agg, picked, stacked = rest[:rounds], rest[rounds], rest[rounds + 1 : -1], rest[-1]
+    halo_sent[...] = dot(picker[...], halo_bonds[...]).astype(jnp.bfloat16)
+    indices.wait()
+    rounds, width = index.shape
+    for turn in range(rounds):
+        for place in range(width):
+            row = turn * width + place
+            inner_sent[row : row + 1, :] = inner[pl.ds(index[turn, place], 1), :]
+
+
+def sent_kernel(inner_sent, halo_sent, *rest):
+    rounds = len(rest) // 2
+    total = inner_sent[...]
+    width = total.shape[0] // rounds
+    for turn, part in enumerate(rest[:rounds]):
+        total += dot(halo_sent[:, turn * width : (turn + 1) * width], part[...])
+    for turn, part in enumerate(rest[rounds:]):
+        part[...] = total[turn * width : (turn + 1) * width].astype(jnp.bfloat16)
+
+
+def hidden_kernel(inner_first, halo_bonds, first_weight, features, bonds, *rest):
+    *halo, agg, hidden, slope, inner, stacked = rest
     width = halo[0].shape[0]
     for turn, part in enumerate(halo):
         stacked[turn * width : (turn + 1) * width, :] = part[...]
-    agg[...] = (inner[...] + dot(halo_bonds[...], stacked[...])).astype(jnp.bfloat16)
-    for turn, part in enumerate(picked):
-        chosen = picker[turn * width : (turn + 1) * width, :]
-        part[...] = dot(chosen, agg[...]).astype(jnp.bfloat16)
-
-
-def hidden_kernel(agg, first_weight, features, bonds, hidden, slope, inner):
+    agg[...] = (inner_first[...] + dot(halo_bonds[...], stacked[...])).astype(jnp.bfloat16)
     pre = dot(agg[...], first_weight[...])
     sigm = jax.nn.sigmoid(pre)
     slope[...] = (sigm * (1.0 + pre * (1.0 - sigm))).T
@@ -150,10 +175,14 @@
 
 def summed(kept, given):
     total = kept + swapped(given, 1)
+    size = lax.axis_size("dom")
     mask = 2
-    while mask < lax.axis_size("dom"):
+    while 2 * mask < size:
+        near, far, both = (swapped(total, mask * way) for way in (1, 2, 3))
+        total = (total + near) + (far + both)
+        mask *= 4
+    if mask < size:
         total = total + swapped(total, mask)
-        mask *= 2
     whole = pl.BlockSpec(memory_space=pltpu.VMEM)
     return pl.pallas_call(
         split_kernel,
@@ -182,30 +211,39 @@
         cost=COST,
     )
     halo = [swapped(part, 2**turn) for turn, part in enumerate(picked)]
-    bonds, inner = call(
+    bonds, inner, inner_sent, halo_sent = call(
         inner_kernel,
-        [((atoms, atoms), low), ((atoms, wide), high)],
+        [
+            ((atoms, atoms), low),
+            ((atoms, wide), high),
+            ((rounds * width, wide), high),
+            ((rounds * width, rounds * width), low),
+        ],
         local_bonds,
         tile_mask,
         features,
-    )
-    agg, *picked = call(
-        first_kernel,
-        [((atoms, wide), low)] + sent,
+        halo_bonds,
+        picker,
+        send_rows,
+        scratch=[pltpu.SMEM((rounds, width), jnp.int32), pltpu.SemaphoreType.DMA],
+    )
+    picked = call(sent_kernel, sent, inner_sent, halo_sent, *halo)
+    halo_agg = [swapped(part, 2**turn) for turn, part in enumerate(picked)]
+    agg, hidden, slope, inner = call(
+        hidden_kernel,
+        [
+            ((atoms, wide), low),
+            ((atoms, wide), low),
+            ((wide, atoms), high),
+            ((atoms, wide), high),
+        ],
         inner,
         halo_bonds,
-        picker,
-        *halo,
-        scratch=[stacked],
-    )
-    halo_agg = [swapped(part, 2**turn) for turn, part in enumerate(picked)]
-    hidden, slope, inner = call(
-        hidden_kernel,
-        [((atoms, wide), low), ((wide, atoms), high), ((atoms, wide), high)],
-        agg,
         first_weight,
         features,
         bonds,
+        *halo,
+        scratch=[stacked],
     )
     scale = 1.0 / math.sqrt(atoms * lax.axis_size("dom"))
     prediction, kept, given = call(

time: 40.8 us -> 37.7 us (0.924)
  waiting for transfers between devices: 13.1 us -> 10.3 us
  starting transfers between devices: 18.7 us -> 17.1 us
  Pallas kernels: 7.26 us -> 8.58 us
    ppermute x14 -> x16, waiting for transfers between devices: 13.1 us -> 10.3 us  [swapped(): return lax.ppermute(value, 'dom', pairs)]
    ppermute x14 -> x16, starting transfers between devices: 18.7 us -> 17.1 us  [swapped(): return lax.ppermute(value, 'dom', pairs)]
    pallas_call x5, Pallas kernels: 6.6 us -> 7.92 us  [call(): pl.pallas_call(body, out_shape=[pltpu.VMEM(shape, dtype) for shape, dtype...]
  transfers between devices with their start and end apart: 14 -> 16, of which waited for: 10 -> 9; matrix products, arithmetic and copies ran while one was open for 2% -> 2% of each run, Pallas kernels for 5% -> 11%
where the time goes in v3:
time: 37.7 us; the launch traced here: 37.6 us
  starting transfers between devices  17.1 us (45%)
  waiting for transfers between devices  10.3 us (27%)
  Pallas kernels  8.58 us (23%)
  between operations  0.82 us (2%)
  local copies, waits for them, and re-layouts  0.75 us (2%)
    ppermute x16, starting transfers between devices, swapped(): return lax.ppermute(value, 'dom', pairs)  17.1 us
    ppermute x16, waiting for transfers between devices, swapped(): return lax.ppermute(value, 'dom', pairs)  10.3 us
    pallas_call x5, Pallas kernels, call(): pl.pallas_call(body, out_shape=[pltpu.VMEM(shape, dtype) for shape, dtype...  7.92 us
  transfers between devices with their start and end apart: 16, of which 9 were waited for; matrix products, arithmetic and copies ran while one was open for 2% of the time, Pallas kernels for 11%

profile of v3, /device:TPU:0, one launch (start us, length us, event | category | flops | bytes accessed | tf_op | source)
XLA Modules:
  0.0 37.6 jit_solution(2747791351435669677)
XLA Ops:
  0.6 0.0 copy-start.6
  0.6 0.0 copy-start
  0.7 0.0 copy-start.5
  0.7 0.0 copy-start.1
  0.7 1.7 %shard_map.103 = (bf16[1152,128]{1,0:T(8,128)(2,1)S(1)}, bf16[512,1152]{1,0:T(8,128)(2,1)S(1)}, bf16[128,128]{1,0:T(8,128)(2,1)S(1)}, bf16[128,128]{1,0:T(8,128)...) custom-call(bf16[1152,128]{1,0:T(8,128)(2,1)} %features.1, s32[4,128]{1,0:T(4,128)} %send_rows.3), custom_call_target="tpu_custom_call" | custom-call | flops 4000000000 | bytes 1048576 | tf_op jit(solution)/shard_map/pallas_call | solution.py:40
  2.3 0.5 %collective-permute-start = (bf16[128,128]{1,0:T(8,128)(2,1)S(1)}, bf16[128,128]{1,0:T(8,128)(2,1)S(1)}, u32[]{:S(2)}, u32[]{:S(2)}) collective-permute-start(bf16[128,128]{1,0:T(8,128)(2,1)S(1)} %get-tuple-element.30), channel_id=1, source_target_pairs={{0,1},{1,0},{2,3},{3,2},{4,5},{5,4},{6,7},{7,6},{8,9},{9,8},{10,11... | collective-permute-start | bytes 98312 | tf_op jit(solution)/shard_map/ppermute | solution.py:18
  2.9 2.6 %collective-permute-start.1 = (bf16[128,128]{1,0:T(8,128)(2,1)S(1)}, bf16[128,128]{1,0:T(8,128)(2,1)S(1)}, u32[]{:S(2)}, u32[]{:S(2)}) collective-permute-start(bf16[128,128]{1,0:T(8,128)(2,1)S(1)} %get-tuple-element.31), channel_id=1, source_target_pairs={{0,2},{1,3},{2,0},{3,1},{4,6},{5,7},{6,4},{7,5},{8,10},{9,11},{10,... | collective-permute-start | bytes 98312 | tf_op jit(solution)/shard_map/ppermute | solution.py:18
  5.4 1.5 %collective-permute-start.2 = (bf16[128,128]{1,0:T(8,128)(2,1)S(1)}, bf16[128,128]{1,0:T(8,128)(2,1)S(1)}, u32[]{:S(2)}, u32[]{:S(2)}) collective-permute-start(bf16[128,128]{1,0:T(8,128)(2,1)S(1)} %get-tuple-element.32), channel_id=1, source_target_pairs={{0,4},{1,5},{2,6},{3,7},{4,0},{5,1},{6,2},{7,3},{8,12},{9,13},{10,... | collective-permute-start | bytes 98312 | tf_op jit(solution)/shard_map/ppermute | solution.py:18
  6.9 1.6 %collective-permute-start.3 = (bf16[128,128]{1,0:T(8,128)(2,1)S(1)}, bf16[128,128]{1,0:T(8,128)(2,1)S(1)}, u32[]{:S(2)}, u32[]{:S(2)}) collective-permute-start(bf16[128,128]{1,0:T(8,128)(2,1)S(1)} %get-tuple-element.33), channel_id=1, source_target_pairs={{0,8},{1,9},{2,10},{3,11},{4,12},{5,13},{6,14},{7,15},{8,0},{9,1},... | collective-permute-start | bytes 98312 | tf_op jit(solution)/shard_map/ppermute | solution.py:18
  8.5 0.0 copy-done.6
  8.5 0.0 copy-done
  8.5 0.0 copy-done.5
  8.5 0.0 copy-done.1
  8.5 0.0 copy-start.3
  8.5 2.1 %shard_map.104 = (bf16[1152,1152]{1,0:T(8,128)(2,1)S(1)}, f32[1152,128]{1,0:T(8,128)S(1)}, f32[512,128]{1,0:T(8,128)S(1)}, bf16[512,512]{1,0:T(8,128)(2,1)S(1)}) custom-call(bf16[1152,1152]{1,0:T(8,128)(2,1)S(1)} %copy-done.1, s32[18,18]{1,0:T(8,128)S(1)} %copy-done.5, bf16[1152,128]{1,0:T(8,128)(2,1)S(1)} %get-tuple-element.26.features, ...), custom_call_target="tpu_custom_call" | custom-call | tf_op jit(solution)/shard_map/pallas_call | solution.py:40
  10.6 0.0 collective-permute-done.rest_0_
  10.7 0.0 collective-permute-done.1.rest_1_
  10.7 0.0 collective-permute-done.2.rest_2_
  10.7 0.2 collective-permute-done.3.rest_3_
  10.9 0.3 shard_map.106
  11.1 0.0 copy-start.2
  11.2 0.0 copy-start.4
  11.2 0.1 collective-permute-start.4
  11.2 0.6 %collective-permute-start.5 = (bf16[128,128]{1,0:T(8,128)(2,1)S(1)}, bf16[128,128]{1,0:T(8,128)(2,1)S(1)}, u32[]{:S(2)}, u32[]{:S(2)}) collective-permute-start(bf16[128,128]{1,0:T(8,128)(2,1)S(1)} %get-tuple-element.41), channel_id=1, source_target_pairs={{0,2},{1,3},{2,0},{3,1},{4,6},{5,7},{6,4},{7,5},{8,10},{9,11},{10,... | collective-permute-start | bytes 98312 | tf_op jit(solution)/shard_map/ppermute | solution.py:18
  11.8 0.3 collective-permute-start.6
  12.2 1.7 %collective-permute-start.7 = (bf16[128,128]{1,0:T(8,128)(2,1)S(1)}, bf16[128,128]{1,0:T(8,128)(2,1)S(1)}, u32[]{:S(2)}, u32[]{:S(2)}) collective-permute-start(bf16[128,128]{1,0:T(8,128)(2,1)S(1)} %get-tuple-element.43), channel_id=1, source_target_pairs={{0,8},{1,9},{2,10},{3,11},{4,12},{5,13},{6,14},{7,15},{8,0},{9,1},... | collective-permute-start | bytes 98312 | tf_op jit(solution)/shard_map/ppermute | solution.py:18
  13.9 0.0 copy-done.3
  13.9 2.1 %shard_map.105 = (bf16[1152,128]{1,0:T(8,128)(2,1)S(1)}, bf16[1152,128]{1,0:T(8,128)(2,1)S(1)}, f32[128,1152]{1,0:T(8,128)S(1)}, f32[1152,128]{1,0:T(8,128)S(1)}) custom-call(f32[1152,128]{1,0:T(8,128)S(1)} %get-tuple-element.28.inner_first, bf16[1152,512]{1,0:T(8,128)(2,1)S(1)} %copy-done, bf16[128,128]{1,0:T(8,128)(2,1)S(1)} %copy-done.3, ...), custom_call_target="tpu_custom_call" | custom-call | tf_op jit(solution)/shard_map/pallas_call | solution.py:40
  16.0 0.0 collective-permute-done.4.rest_4_
  16.0 0.0 collective-permute-done.5.rest_5_
  16.0 0.0 collective-permute-done.6.rest_6_
  16.0 0.1 collective-permute-done.7.rest_7_
  16.1 0.0 copy-done.2
  16.1 0.0 copy-done.4
  16.1 1.8 %shard_map.107 = (bf16[1152,128]{1,0:T(8,128)(2,1)S(1)}, f32[128,128]{1,0:T(8,128)S(1)}, f32[128,128]{1,0:T(8,128)S(1)}) custom-call(f32[1152,128]{1,0:T(8,128)S(1)} %get-tuple-element.34.inner, bf16[1152,128]{1,0:T(8,128)(2,1)S(1)} %get-tuple-element.35.hidden, f32[128,1152]{1,0:T(8,128)S(1)} %get-tuple-element.36.slope, ...), custom_call_target="tpu_custom_call" | custom-call | tf_op jit(solution)/shard_map/pallas_call | solution.py:40
  17.9 0.1 collective-permute-start.8
  18.0 1.2 %collective-permute-done.8 = f32[128,128]{1,0:T(8,128)S(1)} collective-permute-done((f32[128,128]{1,0:T(8,128)S(1)}, f32[128,128]{1,0:T(8,128)S(1)}, u32[]{:S(2)}, u32[]{:S(2)}) %collective-permute-start.8) | collective-permute-done | bytes 65568 | tf_op jit(solution)/shard_map/ppermute | solution.py:18
  19.3 2.7 %collective-permute-start.11 = (f32[128,128]{1,0:T(8,128)S(1)}, f32[128,128]{1,0:T(8,128)S(1)}, u32[]{:S(2)}, u32[]{:S(2)}) collective-permute-start(f32[128,128]{1,0:T(8,128)S(1)} %add.21), channel_id=1, source_target_pairs={{0,6},{1,7},{2,4},{3,5},{4,2},{5,3},{6,0},{7,1},{8,14},{9,15},{10,... | collective-permute-start | bytes 196616 | tf_op jit(solution)/shard_map/ppermute | solution.py:18
  21.9 0.5 %collective-permute-start.10 = (f32[128,128]{1,0:T(8,128)S(1)}, f32[128,128]{1,0:T(8,128)S(1)}, u32[]{:S(2)}, u32[]{:S(2)}) collective-permute-start(f32[128,128]{1,0:T(8,128)S(1)} %add.21), channel_id=1, source_target_pairs={{0,4},{1,5},{2,6},{3,7},{4,0},{5,1},{6,2},{7,3},{8,12},{9,13},{10,... | collective-permute-start | bytes 196616 | tf_op jit(solution)/shard_map/ppermute | solution.py:18
  22.5 0.4 collective-permute-start.9
  22.8 1.7 %collective-permute-done.11 = f32[128,128]{1,0:T(8,128)S(1)} collective-permute-done((f32[128,128]{1,0:T(8,128)S(1)}, f32[128,128]{1,0:T(8,128)S(1)}, u32[]{:S(2)}, u32[]{:S(2)}) %collective-permute-start.11) | collective-permute-done | bytes 65568 | tf_op jit(solution)/shard_map/ppermute | solution.py:18
  24.5 1.7 %collective-permute-done.10 = f32[128,128]{1,0:T(8,128)S(1)} collective-permute-done((f32[128,128]{1,0:T(8,128)S(1)}, f32[128,128]{1,0:T(8,128)S(1)}, u32[]{:S(2)}, u32[]{:S(2)}) %collective-permute-start.10) | collective-permute-done | bytes 65568 | tf_op jit(solution)/shard_map/ppermute | solution.py:18
  26.2 0.5 %collective-permute-done.9 = f32[128,128]{1,0:T(8,128)S(1)} collective-permute-done((f32[128,128]{1,0:T(8,128)S(1)}, f32[128,128]{1,0:T(8,128)S(1)}, u32[]{:S(2)}, u32[]{:S(2)}) %collective-permute-start.9) | collective-permute-done | bytes 65568 | tf_op jit(solution)/shard_map/ppermute | solution.py:18
  26.7 3.7 %collective-permute-start.14 = (f32[128,128]{1,0:T(8,128)S(1)}, f32[128,128]{1,0:T(8,128)S(1)}, u32[]{:S(2)}, u32[]{:S(2)}) collective-permute-start(f32[128,128]{1,0:T(8,128)S(1)} %add_add_fusion.1), channel_id=1, source_target_pairs={{0,24},{1,25},{2,26},{3,27},{4,28},{5,29},{6,30},{7,31},{8,16},{9,... | collective-permute-start | bytes 196616 | tf_op jit(solution)/shard_map/ppermute | solution.py:18
  30.4 0.0 collective-permute-start.13
  30.4 0.8 %collective-permute-start.12 = (f32[128,128]{1,0:T(8,128)S(1)}, f32[128,128]{1,0:T(8,128)S(1)}, u32[]{:S(2)}, u32[]{:S(2)}) collective-permute-start(f32[128,128]{1,0:T(8,128)S(1)} %add_add_fusion.1), channel_id=1, source_target_pairs={{0,8},{1,9},{2,10},{3,11},{4,12},{5,13},{6,14},{7,15},{8,0},{9,1},... | collective-permute-start | bytes 196616 | tf_op jit(solution)/shard_map/ppermute | solution.py:18
  31.2 1.7 %collective-permute-done.14 = f32[128,128]{1,0:T(8,128)S(1)} collective-permute-done((f32[128,128]{1,0:T(8,128)S(1)}, f32[128,128]{1,0:T(8,128)S(1)}, u32[]{:S(2)}, u32[]{:S(2)}) %collective-permute-start.14) | collective-permute-done | bytes 65568 | tf_op jit(solution)/shard_map/ppermute | solution.py:18
  32.9 2.7 %collective-permute-done.13 = f32[128,128]{1,0:T(8,128)S(1)} collective-permute-done((f32[128,128]{1,0:T(8,128)S(1)}, f32[128,128]{1,0:T(8,128)S(1)}, u32[]{:S(2)}, u32[]{:S(2)}) %collective-permute-start.13) | collective-permute-done | bytes 65568 | tf_op jit(solution)/shard_map/ppermute | solution.py:18
  35.6 0.0 collective-permute-done.12
  35.6 0.1 collective-permute-start.15
  35.7 0.7 %copy.11 = bf16[1152,128]{1,0:T(8,128)(2,1)} copy(bf16[1152,128]{1,0:T(8,128)(2,1)S(1)} %get-tuple-element.49) | data formatting | bytes 589824
  36.4 0.5 %collective-permute-done.15.other = f32[128,128]{1,0:T(8,128)S(1)} collective-permute-done((f32[128,128]{1,0:T(8,128)S(1)}, f32[128,128]{1,0:T(8,128)S(1)}, u32[]{:S(2)}, u32[]{:S(2)}) %collective-permute-start.15) | collective-permute-done | bytes 65568 | tf_op jit(solution)/shard_map/ppermute | solution.py:18
  36.9 0.7 %shard_map.108 = (f32[128,128]{1,0:T(8,128)}, f32[128,128]{1,0:T(8,128)}) custom-call(f32[128,128]{1,0:T(8,128)S(1)} %add_add_fusion.total, f32[128,128]{1,0:T(8,128)S(1)} %collective-permute-done.15.other), custom_call_target="tpu_custom_call" | custom-call | tf_op jit(solution)/shard_map/pallas_call | solution.py:187
  (3 shorter events, 0.0 us)
Async XLA Ops:
  0.6 7.9 %copy-start.6 = (s32[4,128]{1,0:T(4,128)S(1)}, s32[4,128]{1,0:T(4,128)}, u32[]{:S(2)}) copy-start(s32[4,128]{1,0:T(4,128)} %send_rows.3) | copy-start | bytes 6148
  0.6 7.9 %copy-start = (bf16[1152,512]{1,0:T(8,128)(2,1)S(1)}, bf16[1152,512]{1,0:T(8,128)(2,1)}, u32[]{:S(2)}) copy-start(bf16[1152,512]{1,0:T(8,128)(2,1)} %halo_bonds.5) | copy-start | bytes 3538948
  0.7 7.9 %copy-start.5 = (s32[18,18]{1,0:T(8,128)S(1)}, s32[18,18]{1,0:T(8,128)}, u32[]{:S(2)}) copy-start(s32[18,18]{1,0:T(8,128)} %tile_mask.1) | copy-start | bytes 3892
  0.7 7.9 %copy-start.1 = (bf16[1152,1152]{1,0:T(8,128)(2,1)S(1)}, bf16[1152,1152]{1,0:T(8,128)(2,1)}, u32[]{:S(2)}) copy-start(bf16[1152,1152]{1,0:T(8,128)(2,1)} %local_bonds.1) | copy-start | bytes 7962628
  2.3 8.3 %collective-permute-start = (bf16[128,128]{1,0:T(8,128)(2,1)S(1)}, bf16[128,128]{1,0:T(8,128)(2,1)S(1)}, u32[]{:S(2)}, u32[]{:S(2)}) collective-permute-start(bf16[128,128]{1,0:T(8,128)(2,1)S(1)} %get-tuple-element.30), channel_id=1, source_target_pairs={{0,1},{1,0},{2,3},{3,2},{4,5},{5,4},{6,7},{7,6},{8,9},{9,8},{10,11... | collective-permute-start | bytes 98312 | tf_op jit(solution)/shard_map/ppermute | solution.py:18
  2.9 7.8 %collective-permute-start.1 = (bf16[128,128]{1,0:T(8,128)(2,1)S(1)}, bf16[128,128]{1,0:T(8,128)(2,1)S(1)}, u32[]{:S(2)}, u32[]{:S(2)}) collective-permute-start(bf16[128,128]{1,0:T(8,128)(2,1)S(1)} %get-tuple-element.31), channel_id=1, source_target_pairs={{0,2},{1,3},{2,0},{3,1},{4,6},{5,7},{6,4},{7,5},{8,10},{9,11},{10,... | collective-permute-start | bytes 98312 | tf_op jit(solution)/shard_map/ppermute | solution.py:18
  5.4 5.3 %collective-permute-start.2 = (bf16[128,128]{1,0:T(8,128)(2,1)S(1)}, bf16[128,128]{1,0:T(8,128)(2,1)S(1)}, u32[]{:S(2)}, u32[]{:S(2)}) collective-permute-start(bf16[128,128]{1,0:T(8,128)(2,1)S(1)} %get-tuple-element.32), channel_id=1, source_target_pairs={{0,4},{1,5},{2,6},{3,7},{4,0},{5,1},{6,2},{7,3},{8,12},{9,13},{10,... | collective-permute-start | bytes 98312 | tf_op jit(solution)/shard_map/ppermute | solution.py:18
  6.9 3.9 %collective-permute-start.3 = (bf16[128,128]{1,0:T(8,128)(2,1)S(1)}, bf16[128,128]{1,0:T(8,128)(2,1)S(1)}, u32[]{:S(2)}, u32[]{:S(2)}) collective-permute-start(bf16[128,128]{1,0:T(8,128)(2,1)S(1)} %get-tuple-element.33), channel_id=1, source_target_pairs={{0,8},{1,9},{2,10},{3,11},{4,12},{5,13},{6,14},{7,15},{8,0},{9,1},... | collective-permute-start | bytes 98312 | tf_op jit(solution)/shard_map/ppermute | solution.py:18
  8.5 5.4 %copy-start.3 = (bf16[128,128]{1,0:T(8,128)(2,1)S(1)}, bf16[128,128]{1,0:T(8,128)(2,1)}, u32[]{:S(2)}) copy-start(bf16[128,128]{1,0:T(8,128)(2,1)} %first_weight.3) | copy-start | bytes 98308
  11.1 5.0 %copy-start.2 = (bf16[1152,128]{1,0:T(8,128)(2,1)S(1)}, bf16[1152,128]{1,0:T(8,128)(2,1)}, u32[]{:S(2)}) copy-start(bf16[1152,128]{1,0:T(8,128)(2,1)} %targets.1) | copy-start | bytes 884740
  11.2 5.0 %copy-start.4 = (bf16[128,128]{1,0:T(8,128)(2,1)S(1)}, bf16[128,128]{1,0:T(8,128)(2,1)}, u32[]{:S(2)}) copy-start(bf16[128,128]{1,0:T(8,128)(2,1)} %second_weight.1) | copy-start | bytes 98308
  11.2 4.8 %collective-permute-start.4 = (bf16[128,128]{1,0:T(8,128)(2,1)S(1)}, bf16[128,128]{1,0:T(8,128)(2,1)S(1)}, u32[]{:S(2)}, u32[]{:S(2)}) collective-permute-start(bf16[128,128]{1,0:T(8,128)(2,1)S(1)} %get-tuple-element.40), channel_id=1, source_target_pairs={{0,1},{1,0},{2,3},{3,2},{4,5},{5,4},{6,7},{7,6},{8,9},{9,8},{10,11... | collective-permute-start | bytes 98312 | tf_op jit(solution)/shard_map/ppermute | solution.py:18
  11.2 4.8 %collective-permute-start.5 = (bf16[128,128]{1,0:T(8,128)(2,1)S(1)}, bf16[128,128]{1,0:T(8,128)(2,1)S(1)}, u32[]{:S(2)}, u32[]{:S(2)}) collective-permute-start(bf16[128,128]{1,0:T(8,128)(2,1)S(1)} %get-tuple-element.41), channel_id=1, source_target_pairs={{0,2},{1,3},{2,0},{3,1},{4,6},{5,7},{6,4},{7,5},{8,10},{9,11},{10,... | collective-permute-start | bytes 98312 | tf_op jit(solution)/shard_map/ppermute | solution.py:18
  11.8 4.2 %collective-permute-start.6 = (bf16[128,128]{1,0:T(8,128)(2,1)S(1)}, bf16[128,128]{1,0:T(8,128)(2,1)S(1)}, u32[]{:S(2)}, u32[]{:S(2)}) collective-permute-start(bf16[128,128]{1,0:T(8,128)(2,1)S(1)} %get-tuple-element.42), channel_id=1, source_target_pairs={{0,4},{1,5},{2,6},{3,7},{4,0},{5,1},{6,2},{7,3},{8,12},{9,13},{10,... | collective-permute-start | bytes 98312 | tf_op jit(solution)/shard_map/ppermute | solution.py:18
  12.2 3.9 %collective-permute-start.7 = (bf16[128,128]{1,0:T(8,128)(2,1)S(1)}, bf16[128,128]{1,0:T(8,128)(2,1)S(1)}, u32[]{:S(2)}, u32[]{:S(2)}) collective-permute-start(bf16[128,128]{1,0:T(8,128)(2,1)S(1)} %get-tuple-element.43), channel_id=1, source_target_pairs={{0,8},{1,9},{2,10},{3,11},{4,12},{5,13},{6,14},{7,15},{8,0},{9,1},... | collective-permute-start | bytes 98312 | tf_op jit(solution)/shard_map/ppermute | solution.py:18
  17.9 1.3 %collective-permute-start.8 = (f32[128,128]{1,0:T(8,128)S(1)}, f32[128,128]{1,0:T(8,128)S(1)}, u32[]{:S(2)}, u32[]{:S(2)}) collective-permute-start(f32[128,128]{1,0:T(8,128)S(1)} %get-tuple-element.46), channel_id=1, source_target_pairs={{0,1},{1,0},{2,3},{3,2},{4,5},{5,4},{6,7},{7,6},{8,9},{9,8},{10,11... | collective-permute-start | bytes 196616 | tf_op jit(solution)/shard_map/ppermute | solution.py:18
  19.3 5.2 %collective-permute-start.11 = (f32[128,128]{1,0:T(8,128)S(1)}, f32[128,128]{1,0:T(8,128)S(1)}, u32[]{:S(2)}, u32[]{:S(2)}) collective-permute-start(f32[128,128]{1,0:T(8,128)S(1)} %add.21), channel_id=1, source_target_pairs={{0,6},{1,7},{2,4},{3,5},{4,2},{5,3},{6,0},{7,1},{8,14},{9,15},{10,... | collective-permute-start | bytes 196616 | tf_op jit(solution)/shard_map/ppermute | solution.py:18
  21.9 4.3 %collective-permute-start.10 = (f32[128,128]{1,0:T(8,128)S(1)}, f32[128,128]{1,0:T(8,128)S(1)}, u32[]{:S(2)}, u32[]{:S(2)}) collective-permute-start(f32[128,128]{1,0:T(8,128)S(1)} %add.21), channel_id=1, source_target_pairs={{0,4},{1,5},{2,6},{3,7},{4,0},{5,1},{6,2},{7,3},{8,12},{9,13},{10,... | collective-permute-start | bytes 196616 | tf_op jit(solution)/shard_map/ppermute | solution.py:18
  22.5 4.3 %collective-permute-start.9 = (f32[128,128]{1,0:T(8,128)S(1)}, f32[128,128]{1,0:T(8,128)S(1)}, u32[]{:S(2)}, u32[]{:S(2)}) collective-permute-start(f32[128,128]{1,0:T(8,128)S(1)} %add.21), channel_id=1, source_target_pairs={{0,2},{1,3},{2,0},{3,1},{4,6},{5,7},{6,4},{7,5},{8,10},{9,11},{10,... | collective-permute-start | bytes 196616 | tf_op jit(solution)/shard_map/ppermute | solution.py:18
  26.7 6.1 %collective-permute-start.14 = (f32[128,128]{1,0:T(8,128)S(1)}, f32[128,128]{1,0:T(8,128)S(1)}, u32[]{:S(2)}, u32[]{:S(2)}) collective-permute-start(f32[128,128]{1,0:T(8,128)S(1)} %add_add_fusion.1), channel_id=1, source_target_pairs={{0,24},{1,25},{2,26},{3,27},{4,28},{5,29},{6,30},{7,31},{8,16},{9,... | collective-permute-start | bytes 196616 | tf_op jit(solution)/shard_map/ppermute | solution.py:18
  30.4 5.2 %collective-permute-start.13 = (f32[128,128]{1,0:T(8,128)S(1)}, f32[128,128]{1,0:T(8,128)S(1)}, u32[]{:S(2)}, u32[]{:S(2)}) collective-permute-start(f32[128,128]{1,0:T(8,128)S(1)} %add_add_fusion.1), channel_id=1, source_target_pairs={{0,16},{1,17},{2,18},{3,19},{4,20},{5,21},{6,22},{7,23},{8,24},{9,... | collective-permute-start | bytes 196616 | tf_op jit(solution)/shard_map/ppermute | solution.py:18
  30.4 5.2 %collective-permute-start.12 = (f32[128,128]{1,0:T(8,128)S(1)}, f32[128,128]{1,0:T(8,128)S(1)}, u32[]{:S(2)}, u32[]{:S(2)}) collective-permute-start(f32[128,128]{1,0:T(8,128)S(1)} %add_add_fusion.1), channel_id=1, source_target_pairs={{0,8},{1,9},{2,10},{3,11},{4,12},{5,13},{6,14},{7,15},{8,0},{9,1},... | collective-permute-start | bytes 196616 | tf_op jit(solution)/shard_map/ppermute | solution.py:18
  35.6 1.3 %collective-permute-start.15 = (f32[128,128]{1,0:T(8,128)S(1)}, f32[128,128]{1,0:T(8,128)S(1)}, u32[]{:S(2)}, u32[]{:S(2)}) collective-permute-start(f32[128,128]{1,0:T(8,128)S(1)} %add_add_fusion.total), channel_id=1, source_target_pairs={{0,1},{1,0},{2,3},{3,2},{4,5},{5,4},{6,7},{7,6},{8,9},{9,8},{10,11... | collective-permute-start | bytes 196616 | tf_op jit(solution)/shard_map/ppermute | solution.py:18

commit v4 on v3

--- a/solution.py
+++ b/solution.py
@@ -140,7 +140,7 @@
     second_weight,
     *rest,
 ):
-    *halo, prediction, kept, given, halo_hidden, halo_agg = rest
+    *halo, prediction, grads, halo_hidden, halo_agg = rest
     rounds = len(halo) // 2
     width = halo[0].shape[0]
     spans = [slice(turn * width, (turn + 1) * width) for turn in range(rounds)]
@@ -161,36 +161,25 @@
     halo_cot = (dot(agg_cot, halo_bonds[...]) * halo_slope).astype(jnp.bfloat16)
     own_cot = ((error.T + dot(agg_cot, bonds[...])) * slope[...]).astype(jnp.bfloat16)
     grad_first = (dot(halo_cot, halo_agg[...]) + dot(own_cot, agg[...])).T
-    grad_second = dot_rows(second_agg, error_b)
-    even = lax.rem(lax.axis_index("dom"), 2) == 0
-    kept[...] = jnp.where(even, grad_first, grad_second)
-    given[...] = jnp.where(even, grad_second, grad_first)
-
-
-def split_kernel(total, other, grad_first, grad_second):
-    even = lax.rem(lax.axis_index("dom"), 2) == 0
-    grad_first[...] = jnp.where(even, total[...], other[...])
-    grad_second[...] = jnp.where(even, other[...], total[...])
-
-
-def summed(kept, given):
-    total = kept + swapped(given, 1)
+    size = grad_first.shape[0]
+    grads[:size, :] = grad_first
+    grads[size:, :] = dot_rows(second_agg, error_b)
+
+
+def summed(total):
+    total = total + swapped(total, 1)
     size = lax.axis_size("dom")
     mask = 2
-    while 2 * mask < size:
-        near, far, both = (swapped(total, mask * way) for way in (1, 2, 3))
-        total = (total + near) + (far + both)
+    while mask < size:
+        low = total.astype(jnp.bfloat16)
+        ways = (1, 2, 3) if 2 * mask < size else (1,)
+        terms = [low, *(swapped(low, mask * way) for way in ways)]
+        pairs = [term.astype(jnp.float32) for term in terms]
+        while len(pairs) > 1:
+            pairs = [left + right for left, right in zip(pairs[::2], pairs[1::2])]
+        total = pairs[0]
         mask *= 4
-    if mask < size:
-        total = total + swapped(total, mask)
-    whole = pl.BlockSpec(memory_space=pltpu.VMEM)
-    return pl.pallas_call(
-        split_kernel,
-        out_shape=[jax.ShapeDtypeStruct(total.shape, total.dtype)] * 2,
-        in_specs=[whole] * 2,
-        out_specs=[whole] * 2,
-        compiler_params=PARAMS,
-    )(total, swapped(total, 1))
+    return total
 
 
 def local(
@@ -246,9 +235,9 @@
         scratch=[stacked],
     )
     scale = 1.0 / math.sqrt(atoms * lax.axis_size("dom"))
-    prediction, kept, given = call(
+    prediction, grads = call(
         functools.partial(back_kernel, scale),
-        [((atoms, wide), low), ((wide, wide), high), ((wide, wide), high)],
+        [((atoms, wide), low), ((2 * wide, wide), high)],
         inner,
         hidden,
         slope,
@@ -262,7 +251,8 @@
         *halo_agg,
         scratch=[stacked, stacked],
     )
-    return (prediction, *summed(kept, given))
+    grads = summed(grads)
+    return prediction, grads[:wide], grads[wide:]
 
 
 def solution(mesh):

time: 37.7 us -> 36.5 us (0.968)
  waiting for transfers between devices: 10.3 us -> 9.15 us
  local copies, waits for them, and re-layouts: 0.75 us -> 1.41 us
  Pallas kernels: 8.58 us -> 7.93 us
    ppermute x16 -> x15, waiting for transfers between devices: 10.3 us -> 9.15 us  [swapped(): return lax.ppermute(value, 'dom', pairs)]
    pallas_call x1 -> x0, Pallas kernels: 0.66 us -> none  [summed(): pl.pallas_call(split_kernel, out_shape=[jax.ShapeDtypeStruct(total.shape,...]
    slice x0 -> x1, local copies, waits for them, and re-layouts: none -> 0.66 us  [local(): return (prediction, grads[:wide], grads[wide:])]
    ppermute x16 -> x15, starting transfers between devices: 17.1 us -> 17 us  [swapped(): return lax.ppermute(value, 'dom', pairs)]
  transfers between devices with their start and end apart: 16 -> 15, of which waited for: 9 -> 8; matrix products, arithmetic and copies ran while one was open for 2% -> 2% of each run, Pallas kernels for 11% -> 11%
where the time goes in v4:
time: 36.5 us; the launch traced here: 36.4 us
  starting transfers between devices  17 us (47%)
  waiting for transfers between devices  9.15 us (25%)
  Pallas kernels  7.93 us (22%)
  local copies, waits for them, and re-layouts  1.41 us (4%)
  between operations  0.81 us (2%)
    ppermute x15, starting transfers between devices, swapped(): return lax.ppermute(value, 'dom', pairs)  17 us
    ppermute x15, waiting for transfers between devices, swapped(): return lax.ppermute(value, 'dom', pairs)  9.15 us
    pallas_call x5, Pallas kernels, call(): pl.pallas_call(body, out_shape=[pltpu.VMEM(shape, dtype) for shape, dtype...  7.93 us
    unnamed x15, local copies, waits for them, and re-layouts  0.75 us
  transfers between devices with their start and end apart: 15, of which 8 were waited for; matrix products, arithmetic and copies ran while one was open for 2% of the time, Pallas kernels for 11%

profile of v4, /device:TPU:0, one launch (start us, length us, event | category | flops | bytes accessed | tf_op | source)
XLA Modules:
  0.0 36.4 jit_solution(5548072569534689970)
XLA Ops:
  0.6 0.0 copy-start.6
  0.6 0.0 copy-start
  0.7 0.0 copy-start.5
  0.7 0.0 copy-start.1
  0.7 1.7 %shard_map.103 = (bf16[1152,128]{1,0:T(8,128)(2,1)S(1)}, bf16[512,1152]{1,0:T(8,128)(2,1)S(1)}, bf16[128,128]{1,0:T(8,128)(2,1)S(1)}, bf16[128,128]{1,0:T(8,128)...) custom-call(bf16[1152,128]{1,0:T(8,128)(2,1)} %features.1, s32[4,128]{1,0:T(4,128)} %send_rows.3), custom_call_target="tpu_custom_call" | custom-call | flops 4000000000 | bytes 1048576 | tf_op jit(solution)/shard_map/pallas_call | solution.py:40
  2.3 0.5 %collective-permute-start = (bf16[128,128]{1,0:T(8,128)(2,1)S(1)}, bf16[128,128]{1,0:T(8,128)(2,1)S(1)}, u32[]{:S(2)}, u32[]{:S(2)}) collective-permute-start(bf16[128,128]{1,0:T(8,128)(2,1)S(1)} %get-tuple-element.27), channel_id=1, source_target_pairs={{0,1},{1,0},{2,3},{3,2},{4,5},{5,4},{6,7},{7,6},{8,9},{9,8},{10,11... | collective-permute-start | bytes 98312 | tf_op jit(solution)/shard_map/ppermute | solution.py:18
  2.9 2.6 %collective-permute-start.1 = (bf16[128,128]{1,0:T(8,128)(2,1)S(1)}, bf16[128,128]{1,0:T(8,128)(2,1)S(1)}, u32[]{:S(2)}, u32[]{:S(2)}) collective-permute-start(bf16[128,128]{1,0:T(8,128)(2,1)S(1)} %get-tuple-element.28), channel_id=1, source_target_pairs={{0,2},{1,3},{2,0},{3,1},{4,6},{5,7},{6,4},{7,5},{8,10},{9,11},{10,... | collective-permute-start | bytes 98312 | tf_op jit(solution)/shard_map/ppermute | solution.py:18
  5.4 1.5 %collective-permute-start.2 = (bf16[128,128]{1,0:T(8,128)(2,1)S(1)}, bf16[128,128]{1,0:T(8,128)(2,1)S(1)}, u32[]{:S(2)}, u32[]{:S(2)}) collective-permute-start(bf16[128,128]{1,0:T(8,128)(2,1)S(1)} %get-tuple-element.29), channel_id=1, source_target_pairs={{0,4},{1,5},{2,6},{3,7},{4,0},{5,1},{6,2},{7,3},{8,12},{9,13},{10,... | collective-permute-start | bytes 98312 | tf_op jit(solution)/shard_map/ppermute | solution.py:18
  6.9 1.6 %collective-permute-start.3 = (bf16[128,128]{1,0:T(8,128)(2,1)S(1)}, bf16[128,128]{1,0:T(8,128)(2,1)S(1)}, u32[]{:S(2)}, u32[]{:S(2)}) collective-permute-start(bf16[128,128]{1,0:T(8,128)(2,1)S(1)} %get-tuple-element.30), channel_id=1, source_target_pairs={{0,8},{1,9},{2,10},{3,11},{4,12},{5,13},{6,14},{7,15},{8,0},{9,1},... | collective-permute-start | bytes 98312 | tf_op jit(solution)/shard_map/ppermute | solution.py:18
  8.5 0.0 copy-done.6
  8.5 0.0 copy-done
  8.5 0.0 copy-done.5
  8.5 0.0 copy-done.1
  8.5 0.0 copy-start.3
  8.5 2.1 %shard_map.104 = (bf16[1152,1152]{1,0:T(8,128)(2,1)S(1)}, f32[1152,128]{1,0:T(8,128)S(1)}, f32[512,128]{1,0:T(8,128)S(1)}, bf16[512,512]{1,0:T(8,128)(2,1)S(1)}) custom-call(bf16[1152,1152]{1,0:T(8,128)(2,1)S(1)} %copy-done.1, s32[18,18]{1,0:T(8,128)S(1)} %copy-done.5, bf16[1152,128]{1,0:T(8,128)(2,1)S(1)} %get-tuple-element.23.features, ...), custom_call_target="tpu_custom_call" | custom-call | tf_op jit(solution)/shard_map/pallas_call | solution.py:40
  10.6 0.0 collective-permute-done.rest_0_
  10.7 0.0 collective-permute-done.1.rest_1_
  10.7 0.0 collective-permute-done.2.rest_2_
  10.7 0.2 collective-permute-done.3.rest_3_
  10.9 0.3 shard_map.106
  11.1 0.0 copy-start.2
  11.2 0.0 copy-start.4
  11.2 0.1 collective-permute-start.4
  11.2 0.6 %collective-permute-start.5 = (bf16[128,128]{1,0:T(8,128)(2,1)S(1)}, bf16[128,128]{1,0:T(8,128)(2,1)S(1)}, u32[]{:S(2)}, u32[]{:S(2)}) collective-permute-start(bf16[128,128]{1,0:T(8,128)(2,1)S(1)} %get-tuple-element.38), channel_id=1, source_target_pairs={{0,2},{1,3},{2,0},{3,1},{4,6},{5,7},{6,4},{7,5},{8,10},{9,11},{10,... | collective-permute-start | bytes 98312 | tf_op jit(solution)/shard_map/ppermute | solution.py:18
  11.8 0.3 collective-permute-start.6
  12.2 1.7 %collective-permute-start.7 = (bf16[128,128]{1,0:T(8,128)(2,1)S(1)}, bf16[128,128]{1,0:T(8,128)(2,1)S(1)}, u32[]{:S(2)}, u32[]{:S(2)}) collective-permute-start(bf16[128,128]{1,0:T(8,128)(2,1)S(1)} %get-tuple-element.40), channel_id=1, source_target_pairs={{0,8},{1,9},{2,10},{3,11},{4,12},{5,13},{6,14},{7,15},{8,0},{9,1},... | collective-permute-start | bytes 98312 | tf_op jit(solution)/shard_map/ppermute | solution.py:18
  13.9 0.0 copy-done.3
  13.9 2.1 %shard_map.105 = (bf16[1152,128]{1,0:T(8,128)(2,1)S(1)}, bf16[1152,128]{1,0:T(8,128)(2,1)S(1)}, f32[128,1152]{1,0:T(8,128)S(1)}, f32[1152,128]{1,0:T(8,128)S(1)}) custom-call(f32[1152,128]{1,0:T(8,128)S(1)} %get-tuple-element.25.inner_first, bf16[1152,512]{1,0:T(8,128)(2,1)S(1)} %copy-done, bf16[128,128]{1,0:T(8,128)(2,1)S(1)} %copy-done.3, ...), custom_call_target="tpu_custom_call" | custom-call | tf_op jit(solution)/shard_map/pallas_call | solution.py:40
  16.0 0.0 collective-permute-done.4.rest_4_
  16.0 0.0 collective-permute-done.5.rest_5_
  16.0 0.0 collective-permute-done.6.rest_6_
  16.0 0.1 collective-permute-done.7.rest_7_
  16.1 0.0 copy-done.2
  16.1 0.0 copy-done.4
  16.1 1.8 %shard_map.107 = (bf16[1152,128]{1,0:T(8,128)(2,1)S(1)}, f32[256,128]{1,0:T(8,128)S(1)}) custom-call(f32[1152,128]{1,0:T(8,128)S(1)} %get-tuple-element.31.inner, bf16[1152,128]{1,0:T(8,128)(2,1)S(1)} %get-tuple-element.32.hidden, f32[128,1152]{1,0:T(8,128)S(1)} %get-tuple-element.33.slope, bf16[1152,128]{1,0:T(8,128)(2,1)S(1)} %get-tuple-element.34.agg, ...), custom_call_target="tpu_custom_call" | custom-call | tf_op jit(solution)/shard_map/pallas_call | solution.py:40
  17.9 0.1 collective-permute-start.8
  18.0 1.3 %collective-permute-done.8 = f32[256,128]{1,0:T(8,128)S(1)} collective-permute-done((f32[256,128]{1,0:T(8,128)S(1)}, f32[256,128]{1,0:T(8,128)S(1)}, u32[]{:S(2)}, u32[]{:S(2)}) %collective-permute-start.8) | collective-permute-done | bytes 131104 | tf_op jit(solution)/shard_map/ppermute | solution.py:18
  19.4 2.7 %collective-permute-start.11 = (bf16[256,128]{1,0:T(8,128)(2,1)S(1)}, bf16[256,128]{1,0:T(8,128)(2,1)S(1)}, u32[]{:S(2)}, u32[]{:S(2)}) collective-permute-start(bf16[256,128]{1,0:T(8,128)(2,1)S(1)} %add_convert_fusion.1), channel_id=1, source_target_pairs={{0,6},{1,7},{2,4},{3,5},{4,2},{5,3},{6,0},{7,1},{8,14},{9,15},{10,... | collective-permute-start | bytes 196616 | tf_op jit(solution)/shard_map/ppermute | solution.py:18
  22.1 0.5 %collective-permute-start.10 = (bf16[256,128]{1,0:T(8,128)(2,1)S(1)}, bf16[256,128]{1,0:T(8,128)(2,1)S(1)}, u32[]{:S(2)}, u32[]{:S(2)}) collective-permute-start(bf16[256,128]{1,0:T(8,128)(2,1)S(1)} %add_convert_fusion.1), channel_id=1, source_target_pairs={{0,4},{1,5},{2,6},{3,7},{4,0},{5,1},{6,2},{7,3},{8,12},{9,13},{10,... | collective-permute-start | bytes 196616 | tf_op jit(solution)/shard_map/ppermute | solution.py:18
  22.6 0.4 collective-permute-start.9
  22.9 1.7 %collective-permute-done.11 = bf16[256,128]{1,0:T(8,128)(2,1)S(1)} collective-permute-done((bf16[256,128]{1,0:T(8,128)(2,1)S(1)}, bf16[256,128]{1,0:T(8,128)(2,1)S(1)}, u32[]{:S(2)}, u32[]{:S(2)}) %collective-permute-start.11) | collective-permute-done | bytes 65568 | tf_op jit(solution)/shard_map/ppermute | solution.py:18
  24.6 1.7 %collective-permute-done.10 = bf16[256,128]{1,0:T(8,128)(2,1)S(1)} collective-permute-done((bf16[256,128]{1,0:T(8,128)(2,1)S(1)}, bf16[256,128]{1,0:T(8,128)(2,1)S(1)}, u32[]{:S(2)}, u32[]{:S(2)}) %collective-permute-start.10) | collective-permute-done | bytes 65568 | tf_op jit(solution)/shard_map/ppermute | solution.py:18
  26.3 0.5 %collective-permute-done.9 = bf16[256,128]{1,0:T(8,128)(2,1)S(1)} collective-permute-done((bf16[256,128]{1,0:T(8,128)(2,1)S(1)}, bf16[256,128]{1,0:T(8,128)(2,1)S(1)}, u32[]{:S(2)}, u32[]{:S(2)}) %collective-permute-start.9) | collective-permute-done | bytes 65568 | tf_op jit(solution)/shard_map/ppermute | solution.py:18
  26.9 3.7 %collective-permute-start.14 = (bf16[256,128]{1,0:T(8,128)(2,1)S(1)}, bf16[256,128]{1,0:T(8,128)(2,1)S(1)}, u32[]{:S(2)}, u32[]{:S(2)}) collective-permute-start(bf16[256,128]{1,0:T(8,128)(2,1)S(1)} %add_convert_fusion), channel_id=1, source_target_pairs={{0,24},{1,25},{2,26},{3,27},{4,28},{5,29},{6,30},{7,31},{8,16},{9,... | collective-permute-start | bytes 196616 | tf_op jit(solution)/shard_map/ppermute | solution.py:18
  30.5 0.0 collective-permute-start.13
  30.5 0.8 %collective-permute-start.12 = (bf16[256,128]{1,0:T(8,128)(2,1)S(1)}, bf16[256,128]{1,0:T(8,128)(2,1)S(1)}, u32[]{:S(2)}, u32[]{:S(2)}) collective-permute-start(bf16[256,128]{1,0:T(8,128)(2,1)S(1)} %add_convert_fusion), channel_id=1, source_target_pairs={{0,8},{1,9},{2,10},{3,11},{4,12},{5,13},{6,14},{7,15},{8,0},{9,1},... | collective-permute-start | bytes 196616 | tf_op jit(solution)/shard_map/ppermute | solution.py:18
  31.3 0.7 %copy.11 = bf16[1152,128]{1,0:T(8,128)(2,1)} copy(bf16[1152,128]{1,0:T(8,128)(2,1)S(1)} %get-tuple-element.45) | data formatting | bytes 589824
  32.0 1.0 %collective-permute-done.14 = bf16[256,128]{1,0:T(8,128)(2,1)S(1)} collective-permute-done((bf16[256,128]{1,0:T(8,128)(2,1)S(1)}, bf16[256,128]{1,0:T(8,128)(2,1)S(1)}, u32[]{:S(2)}, u32[]{:S(2)}) %collective-permute-start.14) | collective-permute-done | bytes 65568 | tf_op jit(solution)/shard_map/ppermute | solution.py:18
  33.0 2.7 %collective-permute-done.13 = bf16[256,128]{1,0:T(8,128)(2,1)S(1)} collective-permute-done((bf16[256,128]{1,0:T(8,128)(2,1)S(1)}, bf16[256,128]{1,0:T(8,128)(2,1)S(1)}, u32[]{:S(2)}, u32[]{:S(2)}) %collective-permute-start.13) | collective-permute-done | bytes 65568 | tf_op jit(solution)/shard_map/ppermute | solution.py:18
  35.7 0.0 collective-permute-done.12
  35.7 0.7 %fusion = (f32[128,128]{1,0:T(8,128)}, f32[128,128]{1,0:T(8,128)}) fusion(f32[256,128]{1,0:T(8,128)S(1)} %add_add_fusion), kind=kLoop, calls=%fused_computation.3 | loop fusion | bytes 262144 | tf_op jit(solution)/shard_map/slice | solution.py:255
  (3 shorter events, 0.1 us)
Async XLA Ops:
  0.6 7.9 %copy-start.6 = (s32[4,128]{1,0:T(4,128)S(1)}, s32[4,128]{1,0:T(4,128)}, u32[]{:S(2)}) copy-start(s32[4,128]{1,0:T(4,128)} %send_rows.3) | copy-start | bytes 6148
  0.6 7.9 %copy-start = (bf16[1152,512]{1,0:T(8,128)(2,1)S(1)}, bf16[1152,512]{1,0:T(8,128)(2,1)}, u32[]{:S(2)}) copy-start(bf16[1152,512]{1,0:T(8,128)(2,1)} %halo_bonds.5) | copy-start | bytes 3538948
  0.7 7.9 %copy-start.5 = (s32[18,18]{1,0:T(8,128)S(1)}, s32[18,18]{1,0:T(8,128)}, u32[]{:S(2)}) copy-start(s32[18,18]{1,0:T(8,128)} %tile_mask.1) | copy-start | bytes 3892
  0.7 7.9 %copy-start.1 = (bf16[1152,1152]{1,0:T(8,128)(2,1)S(1)}, bf16[1152,1152]{1,0:T(8,128)(2,1)}, u32[]{:S(2)}) copy-start(bf16[1152,1152]{1,0:T(8,128)(2,1)} %local_bonds.1) | copy-start | bytes 7962628
  2.3 8.3 %collective-permute-start = (bf16[128,128]{1,0:T(8,128)(2,1)S(1)}, bf16[128,128]{1,0:T(8,128)(2,1)S(1)}, u32[]{:S(2)}, u32[]{:S(2)}) collective-permute-start(bf16[128,128]{1,0:T(8,128)(2,1)S(1)} %get-tuple-element.27), channel_id=1, source_target_pairs={{0,1},{1,0},{2,3},{3,2},{4,5},{5,4},{6,7},{7,6},{8,9},{9,8},{10,11... | collective-permute-start | bytes 98312 | tf_op jit(solution)/shard_map/ppermute | solution.py:18
  2.9 7.8 %collective-permute-start.1 = (bf16[128,128]{1,0:T(8,128)(2,1)S(1)}, bf16[128,128]{1,0:T(8,128)(2,1)S(1)}, u32[]{:S(2)}, u32[]{:S(2)}) collective-permute-start(bf16[128,128]{1,0:T(8,128)(2,1)S(1)} %get-tuple-element.28), channel_id=1, source_target_pairs={{0,2},{1,3},{2,0},{3,1},{4,6},{5,7},{6,4},{7,5},{8,10},{9,11},{10,... | collective-permute-start | bytes 98312 | tf_op jit(solution)/shard_map/ppermute | solution.py:18
  5.4 5.3 %collective-permute-start.2 = (bf16[128,128]{1,0:T(8,128)(2,1)S(1)}, bf16[128,128]{1,0:T(8,128)(2,1)S(1)}, u32[]{:S(2)}, u32[]{:S(2)}) collective-permute-start(bf16[128,128]{1,0:T(8,128)(2,1)S(1)} %get-tuple-element.29), channel_id=1, source_target_pairs={{0,4},{1,5},{2,6},{3,7},{4,0},{5,1},{6,2},{7,3},{8,12},{9,13},{10,... | collective-permute-start | bytes 98312 | tf_op jit(solution)/shard_map/ppermute | solution.py:18
  6.9 3.9 %collective-permute-start.3 = (bf16[128,128]{1,0:T(8,128)(2,1)S(1)}, bf16[128,128]{1,0:T(8,128)(2,1)S(1)}, u32[]{:S(2)}, u32[]{:S(2)}) collective-permute-start(bf16[128,128]{1,0:T(8,128)(2,1)S(1)} %get-tuple-element.30), channel_id=1, source_target_pairs={{0,8},{1,9},{2,10},{3,11},{4,12},{5,13},{6,14},{7,15},{8,0},{9,1},... | collective-permute-start | bytes 98312 | tf_op jit(solution)/shard_map/ppermute | solution.py:18
  8.5 5.4 %copy-start.3 = (bf16[128,128]{1,0:T(8,128)(2,1)S(1)}, bf16[128,128]{1,0:T(8,128)(2,1)}, u32[]{:S(2)}) copy-start(bf16[128,128]{1,0:T(8,128)(2,1)} %first_weight.3) | copy-start | bytes 98308
  11.1 5.0 %copy-start.2 = (bf16[1152,128]{1,0:T(8,128)(2,1)S(1)}, bf16[1152,128]{1,0:T(8,128)(2,1)}, u32[]{:S(2)}) copy-start(bf16[1152,128]{1,0:T(8,128)(2,1)} %targets.1) | copy-start | bytes 884740
  11.2 5.0 %copy-start.4 = (bf16[128,128]{1,0:T(8,128)(2,1)S(1)}, bf16[128,128]{1,0:T(8,128)(2,1)}, u32[]{:S(2)}) copy-start(bf16[128,128]{1,0:T(8,128)(2,1)} %second_weight.1) | copy-start | bytes 98308
  11.2 4.8 %collective-permute-start.4 = (bf16[128,128]{1,0:T(8,128)(2,1)S(1)}, bf16[128,128]{1,0:T(8,128)(2,1)S(1)}, u32[]{:S(2)}, u32[]{:S(2)}) collective-permute-start(bf16[128,128]{1,0:T(8,128)(2,1)S(1)} %get-tuple-element.37), channel_id=1, source_target_pairs={{0,1},{1,0},{2,3},{3,2},{4,5},{5,4},{6,7},{7,6},{8,9},{9,8},{10,11... | collective-permute-start | bytes 98312 | tf_op jit(solution)/shard_map/ppermute | solution.py:18
  11.2 4.8 %collective-permute-start.5 = (bf16[128,128]{1,0:T(8,128)(2,1)S(1)}, bf16[128,128]{1,0:T(8,128)(2,1)S(1)}, u32[]{:S(2)}, u32[]{:S(2)}) collective-permute-start(bf16[128,128]{1,0:T(8,128)(2,1)S(1)} %get-tuple-element.38), channel_id=1, source_target_pairs={{0,2},{1,3},{2,0},{3,1},{4,6},{5,7},{6,4},{7,5},{8,10},{9,11},{10,... | collective-permute-start | bytes 98312 | tf_op jit(solution)/shard_map/ppermute | solution.py:18
  11.8 4.2 %collective-permute-start.6 = (bf16[128,128]{1,0:T(8,128)(2,1)S(1)}, bf16[128,128]{1,0:T(8,128)(2,1)S(1)}, u32[]{:S(2)}, u32[]{:S(2)}) collective-permute-start(bf16[128,128]{1,0:T(8,128)(2,1)S(1)} %get-tuple-element.39), channel_id=1, source_target_pairs={{0,4},{1,5},{2,6},{3,7},{4,0},{5,1},{6,2},{7,3},{8,12},{9,13},{10,... | collective-permute-start | bytes 98312 | tf_op jit(solution)/shard_map/ppermute | solution.py:18
  12.2 3.9 %collective-permute-start.7 = (bf16[128,128]{1,0:T(8,128)(2,1)S(1)}, bf16[128,128]{1,0:T(8,128)(2,1)S(1)}, u32[]{:S(2)}, u32[]{:S(2)}) collective-permute-start(bf16[128,128]{1,0:T(8,128)(2,1)S(1)} %get-tuple-element.40), channel_id=1, source_target_pairs={{0,8},{1,9},{2,10},{3,11},{4,12},{5,13},{6,14},{7,15},{8,0},{9,1},... | collective-permute-start | bytes 98312 | tf_op jit(solution)/shard_map/ppermute | solution.py:18
  17.9 1.4 %collective-permute-start.8 = (f32[256,128]{1,0:T(8,128)S(1)}, f32[256,128]{1,0:T(8,128)S(1)}, u32[]{:S(2)}, u32[]{:S(2)}) collective-permute-start(f32[256,128]{1,0:T(8,128)S(1)} %get-tuple-element.42), channel_id=1, source_target_pairs={{0,1},{1,0},{2,3},{3,2},{4,5},{5,4},{6,7},{7,6},{8,9},{9,8},{10,11... | collective-permute-start | bytes 393224 | tf_op jit(solution)/shard_map/ppermute | solution.py:18
  19.4 5.2 %collective-permute-start.11 = (bf16[256,128]{1,0:T(8,128)(2,1)S(1)}, bf16[256,128]{1,0:T(8,128)(2,1)S(1)}, u32[]{:S(2)}, u32[]{:S(2)}) collective-permute-start(bf16[256,128]{1,0:T(8,128)(2,1)S(1)} %add_convert_fusion.1), channel_id=1, source_target_pairs={{0,6},{1,7},{2,4},{3,5},{4,2},{5,3},{6,0},{7,1},{8,14},{9,15},{10,... | collective-permute-start | bytes 196616 | tf_op jit(solution)/shard_map/ppermute | solution.py:18
  22.1 4.3 %collective-permute-start.10 = (bf16[256,128]{1,0:T(8,128)(2,1)S(1)}, bf16[256,128]{1,0:T(8,128)(2,1)S(1)}, u32[]{:S(2)}, u32[]{:S(2)}) collective-permute-start(bf16[256,128]{1,0:T(8,128)(2,1)S(1)} %add_convert_fusion.1), channel_id=1, source_target_pairs={{0,4},{1,5},{2,6},{3,7},{4,0},{5,1},{6,2},{7,3},{8,12},{9,13},{10,... | collective-permute-start | bytes 196616 | tf_op jit(solution)/shard_map/ppermute | solution.py:18
  22.6 4.3 %collective-permute-start.9 = (bf16[256,128]{1,0:T(8,128)(2,1)S(1)}, bf16[256,128]{1,0:T(8,128)(2,1)S(1)}, u32[]{:S(2)}, u32[]{:S(2)}) collective-permute-start(bf16[256,128]{1,0:T(8,128)(2,1)S(1)} %add_convert_fusion.1), channel_id=1, source_target_pairs={{0,2},{1,3},{2,0},{3,1},{4,6},{5,7},{6,4},{7,5},{8,10},{9,11},{10,... | collective-permute-start | bytes 196616 | tf_op jit(solution)/shard_map/ppermute | solution.py:18
  26.9 6.1 %collective-permute-start.14 = (bf16[256,128]{1,0:T(8,128)(2,1)S(1)}, bf16[256,128]{1,0:T(8,128)(2,1)S(1)}, u32[]{:S(2)}, u32[]{:S(2)}) collective-permute-start(bf16[256,128]{1,0:T(8,128)(2,1)S(1)} %add_convert_fusion), channel_id=1, source_target_pairs={{0,24},{1,25},{2,26},{3,27},{4,28},{5,29},{6,30},{7,31},{8,16},{9,... | collective-permute-start | bytes 196616 | tf_op jit(solution)/shard_map/ppermute | solution.py:18
  30.5 5.2 %collective-permute-start.13 = (bf16[256,128]{1,0:T(8,128)(2,1)S(1)}, bf16[256,128]{1,0:T(8,128)(2,1)S(1)}, u32[]{:S(2)}, u32[]{:S(2)}) collective-permute-start(bf16[256,128]{1,0:T(8,128)(2,1)S(1)} %add_convert_fusion), channel_id=1, source_target_pairs={{0,16},{1,17},{2,18},{3,19},{4,20},{5,21},{6,22},{7,23},{8,24},{9,... | collective-permute-start | bytes 196616 | tf_op jit(solution)/shard_map/ppermute | solution.py:18
  30.5 5.2 %collective-permute-start.12 = (bf16[256,128]{1,0:T(8,128)(2,1)S(1)}, bf16[256,128]{1,0:T(8,128)(2,1)S(1)}, u32[]{:S(2)}, u32[]{:S(2)}) collective-permute-start(bf16[256,128]{1,0:T(8,128)(2,1)S(1)} %add_convert_fusion), channel_id=1, source_target_pairs={{0,8},{1,9},{2,10},{3,11},{4,12},{5,13},{6,14},{7,15},{8,0},{9,1},... | collective-permute-start | bytes 196616 | tf_op jit(solution)/shard_map/ppermute | solution.py:18

commit v5 on v4

--- a/solution.py
+++ b/solution.py
@@ -48,8 +48,7 @@
     )(*args)
 
 
-def pick_kernel(features, send_rows, kept, picker, *rest):
-    *picked, index, sems = rest
+def picker_kernel(features, send_rows, kept, picker, index, sems):
     rounds, width = send_rows.shape
     atoms = features.shape[0]
     indices = pltpu.make_async_copy(send_rows, index, sems.at[0])
@@ -63,9 +62,13 @@
         chosen = (index[:, turn : turn + 1] == column).astype(jnp.float32).astype(jnp.bfloat16)
         picker[turn * width : (turn + 1) * width, :] = chosen
     rows.wait()
+
+
+def pick_kernel(picker, features, *picked):
+    width = picked[0].shape[0]
+    rows = dot(picker[...], features[...]).astype(jnp.bfloat16)
     for turn, part in enumerate(picked):
-        chosen = picker[turn * width : (turn + 1) * width, :]
-        part[...] = dot(chosen, kept[...]).astype(jnp.bfloat16)
+        part[...] = rows[turn * width : (turn + 1) * width]
 
 
 def inner_kernel(
@@ -190,15 +193,15 @@
     low, high = jnp.bfloat16, jnp.float32
     sent = [((width, wide), low)] * rounds
     stacked = pltpu.VMEM((rounds * width, wide), low)
-    features, picker, *picked = call(
-        pick_kernel,
-        [((atoms, wide), low), ((rounds * width, atoms), low)] + sent,
+    features, picker = call(
+        picker_kernel,
+        [((atoms, wide), low), ((rounds * width, atoms), low)],
         features,
         send_rows,
         remain=2,
         scratch=[pltpu.VMEM((rounds, width), jnp.int32), pltpu.SemaphoreType.DMA((2,))],
-        cost=COST,
-    )
+    )
+    picked = call(pick_kernel, sent, picker, features, cost=COST)
     halo = [swapped(part, 2**turn) for turn, part in enumerate(picked)]
     bonds, inner, inner_sent, halo_sent = call(
         inner_kernel,

time: 36.5 us -> 36.4 us (level)
    pallas_call x5 -> x6, Pallas kernels: 7.93 us -> 7.76 us  [call(): pl.pallas_call(body, out_shape=[pltpu.VMEM(shape, dtype) for shape, dtype...]
  transfers between devices with their start and end apart: 15 -> 15, of which waited for: 8 -> 7; matrix products, arithmetic and copies ran while one was open for 2% -> 2% of each run, Pallas kernels for 11% -> 11%
where the time goes in v5:
time: 36.4 us; the launch traced here: 36.3 us
  starting transfers between devices  17 us (47%)
  waiting for transfers between devices  9.18 us (25%)
  Pallas kernels  7.76 us (21%)
  local copies, waits for them, and re-layouts  1.41 us (4%)
  between operations  0.81 us (2%)
    ppermute x15, starting transfers between devices, swapped(): return lax.ppermute(value, 'dom', pairs)  17 us
    ppermute x15, waiting for transfers between devices, swapped(): return lax.ppermute(value, 'dom', pairs)  9.18 us
    pallas_call x6, Pallas kernels, call(): pl.pallas_call(body, out_shape=[pltpu.VMEM(shape, dtype) for shape, dtype...  7.76 us
    unnamed x15, local copies, waits for them, and re-layouts  0.75 us
  transfers between devices with their start and end apart: 15, of which 7 were waited for; matrix products, arithmetic and copies ran while one was open for 2% of the time, Pallas kernels for 11%

profile of v5, /device:TPU:0, one launch (start us, length us, event | category | flops | bytes accessed | tf_op | source)
XLA Modules:
  0.0 36.3 jit_solution(5223893702252357494)
XLA Ops:
  0.6 1.0 %shard_map.103 = (bf16[1152,128]{1,0:T(8,128)(2,1)S(1)}, bf16[512,1152]{1,0:T(8,128)(2,1)S(1)}) custom-call(bf16[1152,128]{1,0:T(8,128)(2,1)} %features.1, s32[4,128]{1,0:T(4,128)} %send_rows.3), custom_call_target="tpu_custom_call" | custom-call | tf_op jit(solution)/shard_map/pallas_call | solution.py:40
  1.7 0.0 copy-start
  1.7 0.0 copy-start.1
  1.7 0.0 copy-start.5
  1.7 0.0 copy-start.6
  1.7 0.5 %shard_map.105 = (bf16[128,128]{1,0:T(8,128)(2,1)S(1)}, bf16[128,128]{1,0:T(8,128)(2,1)S(1)}, bf16[128,128]{1,0:T(8,128)(2,1)S(1)}, bf16[128,128]{1,0:T(8,128)(2,1)S(1)}) custom-call(bf16[512,1152]{1,0:T(8,128)(2,1)S(1)} %get-tuple-element.24.picker, bf16[1152,128]{1,0:T(8,128)(2,1)S(1)} %get-tuple-element.23.features), custom_call_target="tpu_custom_call" | custom-call | flops 4000000000 | bytes 1048576 | tf_op jit(solution)/shard_map/pallas_call | solution.py:40
  2.2 0.5 %collective-permute-start = (bf16[128,128]{1,0:T(8,128)(2,1)S(1)}, bf16[128,128]{1,0:T(8,128)(2,1)S(1)}, u32[]{:S(2)}, u32[]{:S(2)}) collective-permute-start(bf16[128,128]{1,0:T(8,128)(2,1)S(1)} %get-tuple-element.27), channel_id=1, source_target_pairs={{0,1},{1,0},{2,3},{3,2},{4,5},{5,4},{6,7},{7,6},{8,9},{9,8},{10,11... | collective-permute-start | bytes 98312 | tf_op jit(solution)/shard_map/ppermute | solution.py:18
  2.7 2.6 %collective-permute-start.1 = (bf16[128,128]{1,0:T(8,128)(2,1)S(1)}, bf16[128,128]{1,0:T(8,128)(2,1)S(1)}, u32[]{:S(2)}, u32[]{:S(2)}) collective-permute-start(bf16[128,128]{1,0:T(8,128)(2,1)S(1)} %get-tuple-element.28), channel_id=1, source_target_pairs={{0,2},{1,3},{2,0},{3,1},{4,6},{5,7},{6,4},{7,5},{8,10},{9,11},{10,... | collective-permute-start | bytes 98312 | tf_op jit(solution)/shard_map/ppermute | solution.py:18
  5.3 1.5 %collective-permute-start.2 = (bf16[128,128]{1,0:T(8,128)(2,1)S(1)}, bf16[128,128]{1,0:T(8,128)(2,1)S(1)}, u32[]{:S(2)}, u32[]{:S(2)}) collective-permute-start(bf16[128,128]{1,0:T(8,128)(2,1)S(1)} %get-tuple-element.29), channel_id=1, source_target_pairs={{0,4},{1,5},{2,6},{3,7},{4,0},{5,1},{6,2},{7,3},{8,12},{9,13},{10,... | collective-permute-start | bytes 98312 | tf_op jit(solution)/shard_map/ppermute | solution.py:18
  6.8 0.0 copy-start.3
  6.8 1.6 %collective-permute-start.3 = (bf16[128,128]{1,0:T(8,128)(2,1)S(1)}, bf16[128,128]{1,0:T(8,128)(2,1)S(1)}, u32[]{:S(2)}, u32[]{:S(2)}) collective-permute-start(bf16[128,128]{1,0:T(8,128)(2,1)S(1)} %get-tuple-element.30), channel_id=1, source_target_pairs={{0,8},{1,9},{2,10},{3,11},{4,12},{5,13},{6,14},{7,15},{8,0},{9,1},... | collective-permute-start | bytes 98312 | tf_op jit(solution)/shard_map/ppermute | solution.py:18
  8.4 0.0 copy-done
  8.4 0.0 copy-done.1
  8.4 0.0 copy-done.5
  8.4 0.0 copy-done.6
  8.4 2.1 %shard_map.104 = (bf16[1152,1152]{1,0:T(8,128)(2,1)S(1)}, f32[1152,128]{1,0:T(8,128)S(1)}, f32[512,128]{1,0:T(8,128)S(1)}, bf16[512,512]{1,0:T(8,128)(2,1)S(1)}) custom-call(bf16[1152,1152]{1,0:T(8,128)(2,1)S(1)} %copy-done.1, s32[18,18]{1,0:T(8,128)S(1)} %copy-done.5, bf16[1152,128]{1,0:T(8,128)(2,1)S(1)} %get-tuple-element.23.features, ...), custom_call_target="tpu_custom_call" | custom-call | tf_op jit(solution)/shard_map/pallas_call | solution.py:40
  10.5 0.0 collective-permute-done.rest_0_
  10.5 0.0 collective-permute-done.1.rest_1_
  10.5 0.0 collective-permute-done.2.rest_2_
  10.5 0.2 collective-permute-done.3.rest_3_
  10.7 0.3 shard_map.107
  11.0 0.0 copy-start.2
  11.0 0.0 copy-start.4
  11.0 0.1 collective-permute-start.4
  11.1 0.6 %collective-permute-start.5 = (bf16[128,128]{1,0:T(8,128)(2,1)S(1)}, bf16[128,128]{1,0:T(8,128)(2,1)S(1)}, u32[]{:S(2)}, u32[]{:S(2)}) collective-permute-start(bf16[128,128]{1,0:T(8,128)(2,1)S(1)} %get-tuple-element.38), channel_id=1, source_target_pairs={{0,2},{1,3},{2,0},{3,1},{4,6},{5,7},{6,4},{7,5},{8,10},{9,11},{10,... | collective-permute-start | bytes 98312 | tf_op jit(solution)/shard_map/ppermute | solution.py:18
  11.7 0.3 collective-permute-start.6
  12.0 1.8 %collective-permute-start.7 = (bf16[128,128]{1,0:T(8,128)(2,1)S(1)}, bf16[128,128]{1,0:T(8,128)(2,1)S(1)}, u32[]{:S(2)}, u32[]{:S(2)}) collective-permute-start(bf16[128,128]{1,0:T(8,128)(2,1)S(1)} %get-tuple-element.40), channel_id=1, source_target_pairs={{0,8},{1,9},{2,10},{3,11},{4,12},{5,13},{6,14},{7,15},{8,0},{9,1},... | collective-permute-start | bytes 98312 | tf_op jit(solution)/shard_map/ppermute | solution.py:18
  13.8 0.0 copy-done.3
  13.8 2.1 %shard_map.106 = (bf16[1152,128]{1,0:T(8,128)(2,1)S(1)}, bf16[1152,128]{1,0:T(8,128)(2,1)S(1)}, f32[128,1152]{1,0:T(8,128)S(1)}, f32[1152,128]{1,0:T(8,128)S(1)}) custom-call(f32[1152,128]{1,0:T(8,128)S(1)} %get-tuple-element.25.inner_first, bf16[1152,512]{1,0:T(8,128)(2,1)S(1)} %copy-done, bf16[128,128]{1,0:T(8,128)(2,1)S(1)} %copy-done.3, ...), custom_call_target="tpu_custom_call" | custom-call | tf_op jit(solution)/shard_map/pallas_call | solution.py:40
  15.9 0.0 collective-permute-done.4.rest_4_
  15.9 0.0 collective-permute-done.5.rest_5_
  15.9 0.0 collective-permute-done.6.rest_6_
  15.9 0.0 collective-permute-done.7.rest_7_
  16.0 0.0 copy-done.2
  16.0 0.0 copy-done.4
  16.0 1.8 %shard_map.108 = (bf16[1152,128]{1,0:T(8,128)(2,1)S(1)}, f32[256,128]{1,0:T(8,128)S(1)}) custom-call(f32[1152,128]{1,0:T(8,128)S(1)} %get-tuple-element.31.inner, bf16[1152,128]{1,0:T(8,128)(2,1)S(1)} %get-tuple-element.32.hidden, f32[128,1152]{1,0:T(8,128)S(1)} %get-tuple-element.33.slope, bf16[1152,128]{1,0:T(8,128)(2,1)S(1)} %get-tuple-element.34.agg, ...), custom_call_target="tpu_custom_call" | custom-call | tf_op jit(solution)/shard_map/pallas_call | solution.py:40
  17.8 0.1 collective-permute-start.8
  17.9 1.3 %collective-permute-done.8 = f32[256,128]{1,0:T(8,128)S(1)} collective-permute-done((f32[256,128]{1,0:T(8,128)S(1)}, f32[256,128]{1,0:T(8,128)S(1)}, u32[]{:S(2)}, u32[]{:S(2)}) %collective-permute-start.8) | collective-permute-done | bytes 131104 | tf_op jit(solution)/shard_map/ppermute | solution.py:18
  19.2 2.7 %collective-permute-start.11 = (bf16[256,128]{1,0:T(8,128)(2,1)S(1)}, bf16[256,128]{1,0:T(8,128)(2,1)S(1)}, u32[]{:S(2)}, u32[]{:S(2)}) collective-permute-start(bf16[256,128]{1,0:T(8,128)(2,1)S(1)} %add_convert_fusion.1), channel_id=1, source_target_pairs={{0,6},{1,7},{2,4},{3,5},{4,2},{5,3},{6,0},{7,1},{8,14},{9,15},{10,... | collective-permute-start | bytes 196616 | tf_op jit(solution)/shard_map/ppermute | solution.py:18
  21.9 0.5 %collective-permute-start.10 = (bf16[256,128]{1,0:T(8,128)(2,1)S(1)}, bf16[256,128]{1,0:T(8,128)(2,1)S(1)}, u32[]{:S(2)}, u32[]{:S(2)}) collective-permute-start(bf16[256,128]{1,0:T(8,128)(2,1)S(1)} %add_convert_fusion.1), channel_id=1, source_target_pairs={{0,4},{1,5},{2,6},{3,7},{4,0},{5,1},{6,2},{7,3},{8,12},{9,13},{10,... | collective-permute-start | bytes 196616 | tf_op jit(solution)/shard_map/ppermute | solution.py:18
  22.4 0.3 collective-permute-start.9
  22.8 1.7 %collective-permute-done.11 = bf16[256,128]{1,0:T(8,128)(2,1)S(1)} collective-permute-done((bf16[256,128]{1,0:T(8,128)(2,1)S(1)}, bf16[256,128]{1,0:T(8,128)(2,1)S(1)}, u32[]{:S(2)}, u32[]{:S(2)}) %collective-permute-start.11) | collective-permute-done | bytes 65568 | tf_op jit(solution)/shard_map/ppermute | solution.py:18
  24.4 1.7 %collective-permute-done.10 = bf16[256,128]{1,0:T(8,128)(2,1)S(1)} collective-permute-done((bf16[256,128]{1,0:T(8,128)(2,1)S(1)}, bf16[256,128]{1,0:T(8,128)(2,1)S(1)}, u32[]{:S(2)}, u32[]{:S(2)}) %collective-permute-start.10) | collective-permute-done | bytes 65568 | tf_op jit(solution)/shard_map/ppermute | solution.py:18
  26.2 0.5 %collective-permute-done.9 = bf16[256,128]{1,0:T(8,128)(2,1)S(1)} collective-permute-done((bf16[256,128]{1,0:T(8,128)(2,1)S(1)}, bf16[256,128]{1,0:T(8,128)(2,1)S(1)}, u32[]{:S(2)}, u32[]{:S(2)}) %collective-permute-start.9) | collective-permute-done | bytes 65568 | tf_op jit(solution)/shard_map/ppermute | solution.py:18
  26.7 3.7 %collective-permute-start.14 = (bf16[256,128]{1,0:T(8,128)(2,1)S(1)}, bf16[256,128]{1,0:T(8,128)(2,1)S(1)}, u32[]{:S(2)}, u32[]{:S(2)}) collective-permute-start(bf16[256,128]{1,0:T(8,128)(2,1)S(1)} %add_convert_fusion), channel_id=1, source_target_pairs={{0,24},{1,25},{2,26},{3,27},{4,28},{5,29},{6,30},{7,31},{8,16},{9,... | collective-permute-start | bytes 196616 | tf_op jit(solution)/shard_map/ppermute | solution.py:18
  30.4 0.0 collective-permute-start.13
  30.4 0.8 %collective-permute-start.12 = (bf16[256,128]{1,0:T(8,128)(2,1)S(1)}, bf16[256,128]{1,0:T(8,128)(2,1)S(1)}, u32[]{:S(2)}, u32[]{:S(2)}) collective-permute-start(bf16[256,128]{1,0:T(8,128)(2,1)S(1)} %add_convert_fusion), channel_id=1, source_target_pairs={{0,8},{1,9},{2,10},{3,11},{4,12},{5,13},{6,14},{7,15},{8,0},{9,1},... | collective-permute-start | bytes 196616 | tf_op jit(solution)/shard_map/ppermute | solution.py:18
  31.2 0.7 %copy.11 = bf16[1152,128]{1,0:T(8,128)(2,1)} copy(bf16[1152,128]{1,0:T(8,128)(2,1)S(1)} %get-tuple-element.45) | data formatting | bytes 589824
  31.9 1.0 %collective-permute-done.14 = bf16[256,128]{1,0:T(8,128)(2,1)S(1)} collective-permute-done((bf16[256,128]{1,0:T(8,128)(2,1)S(1)}, bf16[256,128]{1,0:T(8,128)(2,1)S(1)}, u32[]{:S(2)}, u32[]{:S(2)}) %collective-permute-start.14) | collective-permute-done | bytes 65568 | tf_op jit(solution)/shard_map/ppermute | solution.py:18
  32.9 2.7 %collective-permute-done.13 = bf16[256,128]{1,0:T(8,128)(2,1)S(1)} collective-permute-done((bf16[256,128]{1,0:T(8,128)(2,1)S(1)}, bf16[256,128]{1,0:T(8,128)(2,1)S(1)}, u32[]{:S(2)}, u32[]{:S(2)}) %collective-permute-start.13) | collective-permute-done | bytes 65568 | tf_op jit(solution)/shard_map/ppermute | solution.py:18
  35.6 0.0 collective-permute-done.12
  35.6 0.7 %fusion = (f32[128,128]{1,0:T(8,128)}, f32[128,128]{1,0:T(8,128)}) fusion(f32[256,128]{1,0:T(8,128)S(1)} %add_add_fusion), kind=kLoop, calls=%fused_computation.3 | loop fusion | bytes 262144 | tf_op jit(solution)/shard_map/slice | solution.py:258
  (3 shorter events, 0.1 us)
Async XLA Ops:
  1.7 6.7 %copy-start = (bf16[1152,512]{1,0:T(8,128)(2,1)S(1)}, bf16[1152,512]{1,0:T(8,128)(2,1)}, u32[]{:S(2)}) copy-start(bf16[1152,512]{1,0:T(8,128)(2,1)} %halo_bonds.5) | copy-start | bytes 3538948
  1.7 6.7 %copy-start.1 = (bf16[1152,1152]{1,0:T(8,128)(2,1)S(1)}, bf16[1152,1152]{1,0:T(8,128)(2,1)}, u32[]{:S(2)}) copy-start(bf16[1152,1152]{1,0:T(8,128)(2,1)} %local_bonds.1) | copy-start | bytes 7962628
  1.7 6.7 %copy-start.5 = (s32[18,18]{1,0:T(8,128)S(1)}, s32[18,18]{1,0:T(8,128)}, u32[]{:S(2)}) copy-start(s32[18,18]{1,0:T(8,128)} %tile_mask.1) | copy-start | bytes 3892
  1.7 6.7 %copy-start.6 = (s32[4,128]{1,0:T(4,128)S(1)}, s32[4,128]{1,0:T(4,128)}, u32[]{:S(2)}) copy-start(s32[4,128]{1,0:T(4,128)} %send_rows.3) | copy-start | bytes 6148
  2.2 8.3 %collective-permute-start = (bf16[128,128]{1,0:T(8,128)(2,1)S(1)}, bf16[128,128]{1,0:T(8,128)(2,1)S(1)}, u32[]{:S(2)}, u32[]{:S(2)}) collective-permute-start(bf16[128,128]{1,0:T(8,128)(2,1)S(1)} %get-tuple-element.27), channel_id=1, source_target_pairs={{0,1},{1,0},{2,3},{3,2},{4,5},{5,4},{6,7},{7,6},{8,9},{9,8},{10,11... | collective-permute-start | bytes 98312 | tf_op jit(solution)/shard_map/ppermute | solution.py:18
  2.7 7.8 %collective-permute-start.1 = (bf16[128,128]{1,0:T(8,128)(2,1)S(1)}, bf16[128,128]{1,0:T(8,128)(2,1)S(1)}, u32[]{:S(2)}, u32[]{:S(2)}) collective-permute-start(bf16[128,128]{1,0:T(8,128)(2,1)S(1)} %get-tuple-element.28), channel_id=1, source_target_pairs={{0,2},{1,3},{2,0},{3,1},{4,6},{5,7},{6,4},{7,5},{8,10},{9,11},{10,... | collective-permute-start | bytes 98312 | tf_op jit(solution)/shard_map/ppermute | solution.py:18
  5.3 5.2 %collective-permute-start.2 = (bf16[128,128]{1,0:T(8,128)(2,1)S(1)}, bf16[128,128]{1,0:T(8,128)(2,1)S(1)}, u32[]{:S(2)}, u32[]{:S(2)}) collective-permute-start(bf16[128,128]{1,0:T(8,128)(2,1)S(1)} %get-tuple-element.29), channel_id=1, source_target_pairs={{0,4},{1,5},{2,6},{3,7},{4,0},{5,1},{6,2},{7,3},{8,12},{9,13},{10,... | collective-permute-start | bytes 98312 | tf_op jit(solution)/shard_map/ppermute | solution.py:18
  6.8 7.0 %copy-start.3 = (bf16[128,128]{1,0:T(8,128)(2,1)S(1)}, bf16[128,128]{1,0:T(8,128)(2,1)}, u32[]{:S(2)}) copy-start(bf16[128,128]{1,0:T(8,128)(2,1)} %first_weight.3) | copy-start | bytes 98308
  6.8 3.9 %collective-permute-start.3 = (bf16[128,128]{1,0:T(8,128)(2,1)S(1)}, bf16[128,128]{1,0:T(8,128)(2,1)S(1)}, u32[]{:S(2)}, u32[]{:S(2)}) collective-permute-start(bf16[128,128]{1,0:T(8,128)(2,1)S(1)} %get-tuple-element.30), channel_id=1, source_target_pairs={{0,8},{1,9},{2,10},{3,11},{4,12},{5,13},{6,14},{7,15},{8,0},{9,1},... | collective-permute-start | bytes 98312 | tf_op jit(solution)/shard_map/ppermute | solution.py:18
  11.0 4.9 %copy-start.2 = (bf16[1152,128]{1,0:T(8,128)(2,1)S(1)}, bf16[1152,128]{1,0:T(8,128)(2,1)}, u32[]{:S(2)}) copy-start(bf16[1152,128]{1,0:T(8,128)(2,1)} %targets.1) | copy-start | bytes 884740
  11.0 4.9 %copy-start.4 = (bf16[128,128]{1,0:T(8,128)(2,1)S(1)}, bf16[128,128]{1,0:T(8,128)(2,1)}, u32[]{:S(2)}) copy-start(bf16[128,128]{1,0:T(8,128)(2,1)} %second_weight.1) | copy-start | bytes 98308
  11.0 4.8 %collective-permute-start.4 = (bf16[128,128]{1,0:T(8,128)(2,1)S(1)}, bf16[128,128]{1,0:T(8,128)(2,1)S(1)}, u32[]{:S(2)}, u32[]{:S(2)}) collective-permute-start(bf16[128,128]{1,0:T(8,128)(2,1)S(1)} %get-tuple-element.37), channel_id=1, source_target_pairs={{0,1},{1,0},{2,3},{3,2},{4,5},{5,4},{6,7},{7,6},{8,9},{9,8},{10,11... | collective-permute-start | bytes 98312 | tf_op jit(solution)/shard_map/ppermute | solution.py:18
  11.1 4.8 %collective-permute-start.5 = (bf16[128,128]{1,0:T(8,128)(2,1)S(1)}, bf16[128,128]{1,0:T(8,128)(2,1)S(1)}, u32[]{:S(2)}, u32[]{:S(2)}) collective-permute-start(bf16[128,128]{1,0:T(8,128)(2,1)S(1)} %get-tuple-element.38), channel_id=1, source_target_pairs={{0,2},{1,3},{2,0},{3,1},{4,6},{5,7},{6,4},{7,5},{8,10},{9,11},{10,... | collective-permute-start | bytes 98312 | tf_op jit(solution)/shard_map/ppermute | solution.py:18
  11.7 4.2 %collective-permute-start.6 = (bf16[128,128]{1,0:T(8,128)(2,1)S(1)}, bf16[128,128]{1,0:T(8,128)(2,1)S(1)}, u32[]{:S(2)}, u32[]{:S(2)}) collective-permute-start(bf16[128,128]{1,0:T(8,128)(2,1)S(1)} %get-tuple-element.39), channel_id=1, source_target_pairs={{0,4},{1,5},{2,6},{3,7},{4,0},{5,1},{6,2},{7,3},{8,12},{9,13},{10,... | collective-permute-start | bytes 98312 | tf_op jit(solution)/shard_map/ppermute | solution.py:18
  12.0 3.9 %collective-permute-start.7 = (bf16[128,128]{1,0:T(8,128)(2,1)S(1)}, bf16[128,128]{1,0:T(8,128)(2,1)S(1)}, u32[]{:S(2)}, u32[]{:S(2)}) collective-permute-start(bf16[128,128]{1,0:T(8,128)(2,1)S(1)} %get-tuple-element.40), channel_id=1, source_target_pairs={{0,8},{1,9},{2,10},{3,11},{4,12},{5,13},{6,14},{7,15},{8,0},{9,1},... | collective-permute-start | bytes 98312 | tf_op jit(solution)/shard_map/ppermute | solution.py:18
  17.8 1.4 %collective-permute-start.8 = (f32[256,128]{1,0:T(8,128)S(1)}, f32[256,128]{1,0:T(8,128)S(1)}, u32[]{:S(2)}, u32[]{:S(2)}) collective-permute-start(f32[256,128]{1,0:T(8,128)S(1)} %get-tuple-element.42), channel_id=1, source_target_pairs={{0,1},{1,0},{2,3},{3,2},{4,5},{5,4},{6,7},{7,6},{8,9},{9,8},{10,11... | collective-permute-start | bytes 393224 | tf_op jit(solution)/shard_map/ppermute | solution.py:18
  19.2 5.2 %collective-permute-start.11 = (bf16[256,128]{1,0:T(8,128)(2,1)S(1)}, bf16[256,128]{1,0:T(8,128)(2,1)S(1)}, u32[]{:S(2)}, u32[]{:S(2)}) collective-permute-start(bf16[256,128]{1,0:T(8,128)(2,1)S(1)} %add_convert_fusion.1), channel_id=1, source_target_pairs={{0,6},{1,7},{2,4},{3,5},{4,2},{5,3},{6,0},{7,1},{8,14},{9,15},{10,... | collective-permute-start | bytes 196616 | tf_op jit(solution)/shard_map/ppermute | solution.py:18
  21.9 4.3 %collective-permute-start.10 = (bf16[256,128]{1,0:T(8,128)(2,1)S(1)}, bf16[256,128]{1,0:T(8,128)(2,1)S(1)}, u32[]{:S(2)}, u32[]{:S(2)}) collective-permute-start(bf16[256,128]{1,0:T(8,128)(2,1)S(1)} %add_convert_fusion.1), channel_id=1, source_target_pairs={{0,4},{1,5},{2,6},{3,7},{4,0},{5,1},{6,2},{7,3},{8,12},{9,13},{10,... | collective-permute-start | bytes 196616 | tf_op jit(solution)/shard_map/ppermute | solution.py:18
  22.4 4.3 %collective-permute-start.9 = (bf16[256,128]{1,0:T(8,128)(2,1)S(1)}, bf16[256,128]{1,0:T(8,128)(2,1)S(1)}, u32[]{:S(2)}, u32[]{:S(2)}) collective-permute-start(bf16[256,128]{1,0:T(8,128)(2,1)S(1)} %add_convert_fusion.1), channel_id=1, source_target_pairs={{0,2},{1,3},{2,0},{3,1},{4,6},{5,7},{6,4},{7,5},{8,10},{9,11},{10,... | collective-permute-start | bytes 196616 | tf_op jit(solution)/shard_map/ppermute | solution.py:18
  26.7 6.1 %collective-permute-start.14 = (bf16[256,128]{1,0:T(8,128)(2,1)S(1)}, bf16[256,128]{1,0:T(8,128)(2,1)S(1)}, u32[]{:S(2)}, u32[]{:S(2)}) collective-permute-start(bf16[256,128]{1,0:T(8,128)(2,1)S(1)} %add_convert_fusion), channel_id=1, source_target_pairs={{0,24},{1,25},{2,26},{3,27},{4,28},{5,29},{6,30},{7,31},{8,16},{9,... | collective-permute-start | bytes 196616 | tf_op jit(solution)/shard_map/ppermute | solution.py:18
  30.4 5.2 %collective-permute-start.13 = (bf16[256,128]{1,0:T(8,128)(2,1)S(1)}, bf16[256,128]{1,0:T(8,128)(2,1)S(1)}, u32[]{:S(2)}, u32[]{:S(2)}) collective-permute-start(bf16[256,128]{1,0:T(8,128)(2,1)S(1)} %add_convert_fusion), channel_id=1, source_target_pairs={{0,16},{1,17},{2,18},{3,19},{4,20},{5,21},{6,22},{7,23},{8,24},{9,... | collective-permute-start | bytes 196616 | tf_op jit(solution)/shard_map/ppermute | solution.py:18
  30.4 5.2 %collective-permute-start.12 = (bf16[256,128]{1,0:T(8,128)(2,1)S(1)}, bf16[256,128]{1,0:T(8,128)(2,1)S(1)}, u32[]{:S(2)}, u32[]{:S(2)}) collective-permute-start(bf16[256,128]{1,0:T(8,128)(2,1)S(1)} %add_convert_fusion), channel_id=1, source_target_pairs={{0,8},{1,9},{2,10},{3,11},{4,12},{5,13},{6,14},{7,15},{8,0},{9,1},... | collective-permute-start | bytes 196616 | tf_op jit(solution)/shard_map/ppermute | solution.py:18

commit v6 on v5

--- a/solution.py
+++ b/solution.py
@@ -169,18 +169,46 @@
     grads[size:, :] = dot_rows(second_agg, error_b)
 
 
+def mixed(value, even_mask, odd_mask):
+    masks = (even_mask, odd_mask)
+    pairs = [(source, source ^ masks[source % 2]) for source in range(lax.axis_size("dom"))]
+    return lax.ppermute(value, "dom", pairs)
+
+
+def four_kernel(own, first, second, third, total):
+    even = lax.rem(lax.axis_index("dom"), 2) == 0
+    own, first, second, third = (
+        part[...].astype(jnp.float32) for part in (own, first, second, third)
+    )
+    total[...] = jnp.where(even, (own + first) + (second + third), (own + second) + (first + third))
+
+
+def half_kernel(own, near, far, half):
+    even = lax.rem(lax.axis_index("dom"), 2) == 0
+    mine = jnp.where(even, own[...].astype(jnp.float32), far[...].astype(jnp.float32))
+    half[...] = mine + near[...].astype(jnp.float32)
+
+
 def summed(total):
+    size = lax.axis_size("dom")
+    wide = [(total.shape, jnp.float32)]
     total = total + swapped(total, 1)
-    size = lax.axis_size("dom")
     mask = 2
     while mask < size:
         low = total.astype(jnp.bfloat16)
-        ways = (1, 2, 3) if 2 * mask < size else (1,)
-        terms = [low, *(swapped(low, mask * way) for way in ways)]
-        pairs = [term.astype(jnp.float32) for term in terms]
-        while len(pairs) > 1:
-            pairs = [left + right for left, right in zip(pairs[::2], pairs[1::2])]
-        total = pairs[0]
+        if 2 * mask >= size:
+            total = low.astype(jnp.float32) + swapped(low, mask).astype(jnp.float32)
+        elif mask == 2:
+            terms = [
+                mixed(low, mask, 2 * mask),
+                mixed(low, 2 * mask, mask),
+                mixed(low, 3 * mask, 3 * mask),
+            ]
+            (total,) = call(four_kernel, wide, low, *terms)
+        else:
+            near, far = mixed(low, mask, 2 * mask), mixed(low, mask, 3 * mask)
+            (half,) = call(half_kernel, wide, low, near, far)
+            total = half + swapped(half, 1)
         mask *= 4
     return total
 

time: 36.4 us -> 35.2 us (0.967)
  starting transfers between devices: 17 us -> 15.3 us
  waiting for transfers between devices: 9.18 us -> 9.6 us
    ppermute x0 -> x5, waiting for transfers between devices: none -> 7.74 us  [mixed(): return lax.ppermute(value, 'dom', pairs)]
    ppermute x15 -> x10, starting transfers between devices: 17 us -> 9.62 us  [swapped(): return lax.ppermute(value, 'dom', pairs)]
    ppermute x15 -> x10, waiting for transfers between devices: 9.18 us -> 1.87 us  [swapped(): return lax.ppermute(value, 'dom', pairs)]
    ppermute x0 -> x5, starting transfers between devices: none -> 5.64 us  [mixed(): return lax.ppermute(value, 'dom', pairs)]
    pallas_call x6 -> x8, Pallas kernels: 7.76 us -> 7.84 us  [call(): pl.pallas_call(body, out_shape=[pltpu.VMEM(shape, dtype) for shape, dtype...]
  transfers between devices with their start and end apart: 15 -> 15, of which waited for: 7 -> 8; matrix products, arithmetic and copies ran while one was open for 2% -> 2% of each run, Pallas kernels for 11% -> 12%
where the time goes in v6:
time: 35.2 us; the launch traced here: 35 us
  starting transfers between devices  15.3 us (43%)
  waiting for transfers between devices  9.6 us (27%)
  Pallas kernels  7.84 us (22%)
  local copies, waits for them, and re-layouts  1.41 us (4%)
  between operations  0.82 us (2%)
    ppermute x10, starting transfers between devices, swapped(): return lax.ppermute(value, 'dom', pairs)  9.62 us
    pallas_call x8, Pallas kernels, call(): pl.pallas_call(body, out_shape=[pltpu.VMEM(shape, dtype) for shape, dtype...  7.84 us
    ppermute x5, waiting for transfers between devices, mixed(): return lax.ppermute(value, 'dom', pairs)  7.74 us
    ppermute x5, starting transfers between devices, mixed(): return lax.ppermute(value, 'dom', pairs)  5.64 us
    ppermute x10, waiting for transfers between devices, swapped(): return lax.ppermute(value, 'dom', pairs)  1.87 us
    unnamed x15, local copies, waits for them, and re-layouts  0.75 us
  transfers between devices with their start and end apart: 15, of which 8 were waited for; matrix products, arithmetic and copies ran while one was open for 2% of the time, Pallas kernels for 12%

profile of v6, /device:TPU:0, one launch (start us, length us, event | category | flops | bytes accessed | tf_op | source)
XLA Modules:
  0.0 35.0 jit_solution(14578170703570856129)
XLA Ops:
  0.6 1.0 %shard_map.103 = (bf16[1152,128]{1,0:T(8,128)(2,1)S(1)}, bf16[512,1152]{1,0:T(8,128)(2,1)S(1)}) custom-call(bf16[1152,128]{1,0:T(8,128)(2,1)} %features.1, s32[4,128]{1,0:T(4,128)} %send_rows.3), custom_call_target="tpu_custom_call" | custom-call | tf_op jit(solution)/shard_map/pallas_call | solution.py:40
  1.7 0.0 copy-start
  1.7 0.0 copy-start.1
  1.7 0.0 copy-start.5
  1.7 0.0 copy-start.6
  1.7 0.5 %shard_map.105 = (bf16[128,128]{1,0:T(8,128)(2,1)S(1)}, bf16[128,128]{1,0:T(8,128)(2,1)S(1)}, bf16[128,128]{1,0:T(8,128)(2,1)S(1)}, bf16[128,128]{1,0:T(8,128)(2,1)S(1)}) custom-call(bf16[512,1152]{1,0:T(8,128)(2,1)S(1)} %get-tuple-element.24.picker, bf16[1152,128]{1,0:T(8,128)(2,1)S(1)} %get-tuple-element.23.features), custom_call_target="tpu_custom_call" | custom-call | flops 4000000000 | bytes 1048576 | tf_op jit(solution)/shard_map/pallas_call | solution.py:40
  2.2 0.5 %collective-permute-start = (bf16[128,128]{1,0:T(8,128)(2,1)S(1)}, bf16[128,128]{1,0:T(8,128)(2,1)S(1)}, u32[]{:S(2)}, u32[]{:S(2)}) collective-permute-start(bf16[128,128]{1,0:T(8,128)(2,1)S(1)} %get-tuple-element.27), channel_id=1, source_target_pairs={{0,1},{1,0},{2,3},{3,2},{4,5},{5,4},{6,7},{7,6},{8,9},{9,8},{10,11... | collective-permute-start | bytes 98312 | tf_op jit(solution)/shard_map/ppermute | solution.py:18
  2.7 2.6 %collective-permute-start.1 = (bf16[128,128]{1,0:T(8,128)(2,1)S(1)}, bf16[128,128]{1,0:T(8,128)(2,1)S(1)}, u32[]{:S(2)}, u32[]{:S(2)}) collective-permute-start(bf16[128,128]{1,0:T(8,128)(2,1)S(1)} %get-tuple-element.28), channel_id=1, source_target_pairs={{0,2},{1,3},{2,0},{3,1},{4,6},{5,7},{6,4},{7,5},{8,10},{9,11},{10,... | collective-permute-start | bytes 98312 | tf_op jit(solution)/shard_map/ppermute | solution.py:18
  5.3 1.5 %collective-permute-start.2 = (bf16[128,128]{1,0:T(8,128)(2,1)S(1)}, bf16[128,128]{1,0:T(8,128)(2,1)S(1)}, u32[]{:S(2)}, u32[]{:S(2)}) collective-permute-start(bf16[128,128]{1,0:T(8,128)(2,1)S(1)} %get-tuple-element.29), channel_id=1, source_target_pairs={{0,4},{1,5},{2,6},{3,7},{4,0},{5,1},{6,2},{7,3},{8,12},{9,13},{10,... | collective-permute-start | bytes 98312 | tf_op jit(solution)/shard_map/ppermute | solution.py:18
  6.8 0.0 copy-start.3
  6.8 1.6 %collective-permute-start.3 = (bf16[128,128]{1,0:T(8,128)(2,1)S(1)}, bf16[128,128]{1,0:T(8,128)(2,1)S(1)}, u32[]{:S(2)}, u32[]{:S(2)}) collective-permute-start(bf16[128,128]{1,0:T(8,128)(2,1)S(1)} %get-tuple-element.30), channel_id=1, source_target_pairs={{0,8},{1,9},{2,10},{3,11},{4,12},{5,13},{6,14},{7,15},{8,0},{9,1},... | collective-permute-start | bytes 98312 | tf_op jit(solution)/shard_map/ppermute | solution.py:18
  8.4 0.0 copy-done
  8.4 0.0 copy-done.1
  8.4 0.0 copy-done.5
  8.4 0.0 copy-done.6
  8.4 2.1 %shard_map.104 = (bf16[1152,1152]{1,0:T(8,128)(2,1)S(1)}, f32[1152,128]{1,0:T(8,128)S(1)}, f32[512,128]{1,0:T(8,128)S(1)}, bf16[512,512]{1,0:T(8,128)(2,1)S(1)}) custom-call(bf16[1152,1152]{1,0:T(8,128)(2,1)S(1)} %copy-done.1, s32[18,18]{1,0:T(8,128)S(1)} %copy-done.5, bf16[1152,128]{1,0:T(8,128)(2,1)S(1)} %get-tuple-element.23.features, ...), custom_call_target="tpu_custom_call" | custom-call | tf_op jit(solution)/shard_map/pallas_call | solution.py:40
  10.5 0.0 collective-permute-done.rest_0_
  10.5 0.0 collective-permute-done.1.rest_1_
  10.5 0.0 collective-permute-done.2.rest_2_
  10.5 0.2 collective-permute-done.3.rest_3_
  10.7 0.3 shard_map.107
  11.0 0.0 copy-start.2
  11.0 0.0 copy-start.4
  11.0 0.1 collective-permute-start.4
  11.1 0.6 %collective-permute-start.5 = (bf16[128,128]{1,0:T(8,128)(2,1)S(1)}, bf16[128,128]{1,0:T(8,128)(2,1)S(1)}, u32[]{:S(2)}, u32[]{:S(2)}) collective-permute-start(bf16[128,128]{1,0:T(8,128)(2,1)S(1)} %get-tuple-element.38), channel_id=1, source_target_pairs={{0,2},{1,3},{2,0},{3,1},{4,6},{5,7},{6,4},{7,5},{8,10},{9,11},{10,... | collective-permute-start | bytes 98312 | tf_op jit(solution)/shard_map/ppermute | solution.py:18
  11.7 0.3 collective-permute-start.6
  12.0 1.8 %collective-permute-start.7 = (bf16[128,128]{1,0:T(8,128)(2,1)S(1)}, bf16[128,128]{1,0:T(8,128)(2,1)S(1)}, u32[]{:S(2)}, u32[]{:S(2)}) collective-permute-start(bf16[128,128]{1,0:T(8,128)(2,1)S(1)} %get-tuple-element.40), channel_id=1, source_target_pairs={{0,8},{1,9},{2,10},{3,11},{4,12},{5,13},{6,14},{7,15},{8,0},{9,1},... | collective-permute-start | bytes 98312 | tf_op jit(solution)/shard_map/ppermute | solution.py:18
  13.8 0.0 copy-done.3
  13.8 2.1 %shard_map.106 = (bf16[1152,128]{1,0:T(8,128)(2,1)S(1)}, bf16[1152,128]{1,0:T(8,128)(2,1)S(1)}, f32[128,1152]{1,0:T(8,128)S(1)}, f32[1152,128]{1,0:T(8,128)S(1)}) custom-call(f32[1152,128]{1,0:T(8,128)S(1)} %get-tuple-element.25.inner_first, bf16[1152,512]{1,0:T(8,128)(2,1)S(1)} %copy-done, bf16[128,128]{1,0:T(8,128)(2,1)S(1)} %copy-done.3, ...), custom_call_target="tpu_custom_call" | custom-call | tf_op jit(solution)/shard_map/pallas_call | solution.py:40
  15.9 0.0 collective-permute-done.4.rest_4_
  15.9 0.0 collective-permute-done.5.rest_5_
  15.9 0.0 collective-permute-done.6.rest_6_
  15.9 0.0 collective-permute-done.7.rest_7_
  16.0 0.0 copy-done.2
  16.0 0.0 copy-done.4
  16.0 1.8 %shard_map.108 = (bf16[1152,128]{1,0:T(8,128)(2,1)S(1)}, f32[256,128]{1,0:T(8,128)S(1)}) custom-call(f32[1152,128]{1,0:T(8,128)S(1)} %get-tuple-element.31.inner, bf16[1152,128]{1,0:T(8,128)(2,1)S(1)} %get-tuple-element.32.hidden, f32[128,1152]{1,0:T(8,128)S(1)} %get-tuple-element.33.slope, bf16[1152,128]{1,0:T(8,128)(2,1)S(1)} %get-tuple-element.34.agg, ...), custom_call_target="tpu_custom_call" | custom-call | tf_op jit(solution)/shard_map/pallas_call | solution.py:40
  17.8 0.1 collective-permute-start.8
  17.9 1.3 %collective-permute-done.8 = f32[256,128]{1,0:T(8,128)S(1)} collective-permute-done((f32[256,128]{1,0:T(8,128)S(1)}, f32[256,128]{1,0:T(8,128)S(1)}, u32[]{:S(2)}, u32[]{:S(2)}) %collective-permute-start.8) | collective-permute-done | bytes 131104 | tf_op jit(solution)/shard_map/ppermute | solution.py:18
  19.2 2.7 %collective-permute-start.11 = (bf16[256,128]{1,0:T(8,128)(2,1)S(1)}, bf16[256,128]{1,0:T(8,128)(2,1)S(1)}, u32[]{:S(2)}, u32[]{:S(2)}) collective-permute-start(bf16[256,128]{1,0:T(8,128)(2,1)S(1)} %add_convert_fusion.own), channel_id=1, source_target_pairs={{0,6},{1,7},{2,4},{3,5},{4,2},{5,3},{6,0},{7,1},{8,14},{9,15},{10,... | collective-permute-start | bytes 196616 | tf_op jit(solution)/shard_map/ppermute | solution.py:175
  21.9 0.5 %collective-permute-start.10 = (bf16[256,128]{1,0:T(8,128)(2,1)S(1)}, bf16[256,128]{1,0:T(8,128)(2,1)S(1)}, u32[]{:S(2)}, u32[]{:S(2)}) collective-permute-start(bf16[256,128]{1,0:T(8,128)(2,1)S(1)} %add_convert_fusion.own), channel_id=1, source_target_pairs={{0,4},{1,3},{2,6},{3,1},{4,0},{5,7},{6,2},{7,5},{8,12},{9,11},{10,... | collective-permute-start | bytes 196616 | tf_op jit(solution)/shard_map/ppermute | solution.py:175
  22.4 0.3 collective-permute-start.9
  22.8 1.9 %collective-permute-done.11.third = bf16[256,128]{1,0:T(8,128)(2,1)S(1)} collective-permute-done((bf16[256,128]{1,0:T(8,128)(2,1)S(1)}, bf16[256,128]{1,0:T(8,128)(2,1)S(1)}, u32[]{:S(2)}, u32[]{:S(2)}) %collective-permute-start.11) | collective-permute-done | bytes 65568 | tf_op jit(solution)/shard_map/ppermute | solution.py:175
  24.6 1.6 %collective-permute-done.10.second = bf16[256,128]{1,0:T(8,128)(2,1)S(1)} collective-permute-done((bf16[256,128]{1,0:T(8,128)(2,1)S(1)}, bf16[256,128]{1,0:T(8,128)(2,1)S(1)}, u32[]{:S(2)}, u32[]{:S(2)}) %collective-permute-start.10) | collective-permute-done | bytes 65568 | tf_op jit(solution)/shard_map/ppermute | solution.py:175
  26.2 0.5 %collective-permute-done.9.first = bf16[256,128]{1,0:T(8,128)(2,1)S(1)} collective-permute-done((bf16[256,128]{1,0:T(8,128)(2,1)S(1)}, bf16[256,128]{1,0:T(8,128)(2,1)S(1)}, u32[]{:S(2)}, u32[]{:S(2)}) %collective-permute-start.9) | collective-permute-done | bytes 65568 | tf_op jit(solution)/shard_map/ppermute | solution.py:175
  26.7 0.1 shard_map.109
  26.8 1.6 %collective-permute-start.13 = (bf16[256,128]{1,0:T(8,128)(2,1)S(1)}, bf16[256,128]{1,0:T(8,128)(2,1)S(1)}, u32[]{:S(2)}, u32[]{:S(2)}) collective-permute-start(bf16[256,128]{1,0:T(8,128)(2,1)S(1)} %convert_element_type.7.own), channel_id=1, source_target_pairs={{0,8},{1,25},{2,10},{3,27},{4,12},{5,29},{6,14},{7,31},{8,0},{9,17... | collective-permute-start | bytes 196616 | tf_op jit(solution)/shard_map/ppermute | solution.py:175
  28.4 0.4 %collective-permute-start.12 = (bf16[256,128]{1,0:T(8,128)(2,1)S(1)}, bf16[256,128]{1,0:T(8,128)(2,1)S(1)}, u32[]{:S(2)}, u32[]{:S(2)}) collective-permute-start(bf16[256,128]{1,0:T(8,128)(2,1)S(1)} %convert_element_type.7.own), channel_id=1, source_target_pairs={{0,8},{1,17},{2,10},{3,19},{4,12},{5,21},{6,14},{7,23},{8,0},{9,25... | collective-permute-start | bytes 196616 | tf_op jit(solution)/shard_map/ppermute | solution.py:175
  28.9 2.9 %collective-permute-done.13.far = bf16[256,128]{1,0:T(8,128)(2,1)S(1)} collective-permute-done((bf16[256,128]{1,0:T(8,128)(2,1)S(1)}, bf16[256,128]{1,0:T(8,128)(2,1)S(1)}, u32[]{:S(2)}, u32[]{:S(2)}) %collective-permute-start.13) | collective-permute-done | bytes 65568 | tf_op jit(solution)/shard_map/ppermute | solution.py:175
  31.7 0.9 %collective-permute-done.12.near = bf16[256,128]{1,0:T(8,128)(2,1)S(1)} collective-permute-done((bf16[256,128]{1,0:T(8,128)(2,1)S(1)}, bf16[256,128]{1,0:T(8,128)(2,1)S(1)}, u32[]{:S(2)}, u32[]{:S(2)}) %collective-permute-start.12) | collective-permute-done | bytes 65568 | tf_op jit(solution)/shard_map/ppermute | solution.py:175
  32.7 0.6 %collective-permute-start.14 = (f32[256,128]{1,0:T(8,128)S(1)}, f32[256,128]{1,0:T(8,128)S(1)}, u32[]{:S(2)}, u32[]{:S(2)}) collective-permute-start(f32[256,128]{1,0:T(8,128)S(1)} %shard_map.110), channel_id=1, source_target_pairs={{0,1},{1,0},{2,3},{3,2},{4,5},{5,4},{6,7},{7,6},{8,9},{9,8},{10,11... | collective-permute-start | bytes 393224 | tf_op jit(solution)/shard_map/ppermute | solution.py:18
  33.3 0.7 %copy.11 = bf16[1152,128]{1,0:T(8,128)(2,1)} copy(bf16[1152,128]{1,0:T(8,128)(2,1)S(1)} %get-tuple-element.45) | data formatting | bytes 589824
  34.0 0.3 collective-permute-done.14
  34.3 0.7 %fusion = (f32[128,128]{1,0:T(8,128)}, f32[128,128]{1,0:T(8,128)}) fusion(f32[256,128]{1,0:T(8,128)S(1)} %add.7), kind=kLoop, calls=%fused_computation.1 | loop fusion | bytes 262144 | tf_op jit(solution)/shard_map/slice | solution.py:286
  (4 shorter events, 0.1 us)
Async XLA Ops:
  1.7 6.7 %copy-start = (bf16[1152,512]{1,0:T(8,128)(2,1)S(1)}, bf16[1152,512]{1,0:T(8,128)(2,1)}, u32[]{:S(2)}) copy-start(bf16[1152,512]{1,0:T(8,128)(2,1)} %halo_bonds.5) | copy-start | bytes 3538948
  1.7 6.7 %copy-start.1 = (bf16[1152,1152]{1,0:T(8,128)(2,1)S(1)}, bf16[1152,1152]{1,0:T(8,128)(2,1)}, u32[]{:S(2)}) copy-start(bf16[1152,1152]{1,0:T(8,128)(2,1)} %local_bonds.1) | copy-start | bytes 7962628
  1.7 6.7 %copy-start.5 = (s32[18,18]{1,0:T(8,128)S(1)}, s32[18,18]{1,0:T(8,128)}, u32[]{:S(2)}) copy-start(s32[18,18]{1,0:T(8,128)} %tile_mask.1) | copy-start | bytes 3892
  1.7 6.7 %copy-start.6 = (s32[4,128]{1,0:T(4,128)S(1)}, s32[4,128]{1,0:T(4,128)}, u32[]{:S(2)}) copy-start(s32[4,128]{1,0:T(4,128)} %send_rows.3) | copy-start | bytes 6148
  2.2 8.3 %collective-permute-start = (bf16[128,128]{1,0:T(8,128)(2,1)S(1)}, bf16[128,128]{1,0:T(8,128)(2,1)S(1)}, u32[]{:S(2)}, u32[]{:S(2)}) collective-permute-start(bf16[128,128]{1,0:T(8,128)(2,1)S(1)} %get-tuple-element.27), channel_id=1, source_target_pairs={{0,1},{1,0},{2,3},{3,2},{4,5},{5,4},{6,7},{7,6},{8,9},{9,8},{10,11... | collective-permute-start | bytes 98312 | tf_op jit(solution)/shard_map/ppermute | solution.py:18
  2.7 7.8 %collective-permute-start.1 = (bf16[128,128]{1,0:T(8,128)(2,1)S(1)}, bf16[128,128]{1,0:T(8,128)(2,1)S(1)}, u32[]{:S(2)}, u32[]{:S(2)}) collective-permute-start(bf16[128,128]{1,0:T(8,128)(2,1)S(1)} %get-tuple-element.28), channel_id=1, source_target_pairs={{0,2},{1,3},{2,0},{3,1},{4,6},{5,7},{6,4},{7,5},{8,10},{9,11},{10,... | collective-permute-start | bytes 98312 | tf_op jit(solution)/shard_map/ppermute | solution.py:18
  5.3 5.2 %collective-permute-start.2 = (bf16[128,128]{1,0:T(8,128)(2,1)S(1)}, bf16[128,128]{1,0:T(8,128)(2,1)S(1)}, u32[]{:S(2)}, u32[]{:S(2)}) collective-permute-start(bf16[128,128]{1,0:T(8,128)(2,1)S(1)} %get-tuple-element.29), channel_id=1, source_target_pairs={{0,4},{1,5},{2,6},{3,7},{4,0},{5,1},{6,2},{7,3},{8,12},{9,13},{10,... | collective-permute-start | bytes 98312 | tf_op jit(solution)/shard_map/ppermute | solution.py:18
  6.8 7.0 %copy-start.3 = (bf16[128,128]{1,0:T(8,128)(2,1)S(1)}, bf16[128,128]{1,0:T(8,128)(2,1)}, u32[]{:S(2)}) copy-start(bf16[128,128]{1,0:T(8,128)(2,1)} %first_weight.3) | copy-start | bytes 98308
  6.8 3.9 %collective-permute-start.3 = (bf16[128,128]{1,0:T(8,128)(2,1)S(1)}, bf16[128,128]{1,0:T(8,128)(2,1)S(1)}, u32[]{:S(2)}, u32[]{:S(2)}) collective-permute-start(bf16[128,128]{1,0:T(8,128)(2,1)S(1)} %get-tuple-element.30), channel_id=1, source_target_pairs={{0,8},{1,9},{2,10},{3,11},{4,12},{5,13},{6,14},{7,15},{8,0},{9,1},... | collective-permute-start | bytes 98312 | tf_op jit(solution)/shard_map/ppermute | solution.py:18
  11.0 4.9 %copy-start.2 = (bf16[1152,128]{1,0:T(8,128)(2,1)S(1)}, bf16[1152,128]{1,0:T(8,128)(2,1)}, u32[]{:S(2)}) copy-start(bf16[1152,128]{1,0:T(8,128)(2,1)} %targets.1) | copy-start | bytes 884740
  11.0 4.9 %copy-start.4 = (bf16[128,128]{1,0:T(8,128)(2,1)S(1)}, bf16[128,128]{1,0:T(8,128)(2,1)}, u32[]{:S(2)}) copy-start(bf16[128,128]{1,0:T(8,128)(2,1)} %second_weight.1) | copy-start | bytes 98308
  11.0 4.8 %collective-permute-start.4 = (bf16[128,128]{1,0:T(8,128)(2,1)S(1)}, bf16[128,128]{1,0:T(8,128)(2,1)S(1)}, u32[]{:S(2)}, u32[]{:S(2)}) collective-permute-start(bf16[128,128]{1,0:T(8,128)(2,1)S(1)} %get-tuple-element.37), channel_id=1, source_target_pairs={{0,1},{1,0},{2,3},{3,2},{4,5},{5,4},{6,7},{7,6},{8,9},{9,8},{10,11... | collective-permute-start | bytes 98312 | tf_op jit(solution)/shard_map/ppermute | solution.py:18
  11.1 4.8 %collective-permute-start.5 = (bf16[128,128]{1,0:T(8,128)(2,1)S(1)}, bf16[128,128]{1,0:T(8,128)(2,1)S(1)}, u32[]{:S(2)}, u32[]{:S(2)}) collective-permute-start(bf16[128,128]{1,0:T(8,128)(2,1)S(1)} %get-tuple-element.38), channel_id=1, source_target_pairs={{0,2},{1,3},{2,0},{3,1},{4,6},{5,7},{6,4},{7,5},{8,10},{9,11},{10,... | collective-permute-start | bytes 98312 | tf_op jit(solution)/shard_map/ppermute | solution.py:18
  11.7 4.2 %collective-permute-start.6 = (bf16[128,128]{1,0:T(8,128)(2,1)S(1)}, bf16[128,128]{1,0:T(8,128)(2,1)S(1)}, u32[]{:S(2)}, u32[]{:S(2)}) collective-permute-start(bf16[128,128]{1,0:T(8,128)(2,1)S(1)} %get-tuple-element.39), channel_id=1, source_target_pairs={{0,4},{1,5},{2,6},{3,7},{4,0},{5,1},{6,2},{7,3},{8,12},{9,13},{10,... | collective-permute-start | bytes 98312 | tf_op jit(solution)/shard_map/ppermute | solution.py:18
  12.0 3.9 %collective-permute-start.7 = (bf16[128,128]{1,0:T(8,128)(2,1)S(1)}, bf16[128,128]{1,0:T(8,128)(2,1)S(1)}, u32[]{:S(2)}, u32[]{:S(2)}) collective-permute-start(bf16[128,128]{1,0:T(8,128)(2,1)S(1)} %get-tuple-element.40), channel_id=1, source_target_pairs={{0,8},{1,9},{2,10},{3,11},{4,12},{5,13},{6,14},{7,15},{8,0},{9,1},... | collective-permute-start | bytes 98312 | tf_op jit(solution)/shard_map/ppermute | solution.py:18
  17.8 1.4 %collective-permute-start.8 = (f32[256,128]{1,0:T(8,128)S(1)}, f32[256,128]{1,0:T(8,128)S(1)}, u32[]{:S(2)}, u32[]{:S(2)}) collective-permute-start(f32[256,128]{1,0:T(8,128)S(1)} %get-tuple-element.42), channel_id=1, source_target_pairs={{0,1},{1,0},{2,3},{3,2},{4,5},{5,4},{6,7},{7,6},{8,9},{9,8},{10,11... | collective-permute-start | bytes 393224 | tf_op jit(solution)/shard_map/ppermute | solution.py:18
  19.2 5.4 %collective-permute-start.11 = (bf16[256,128]{1,0:T(8,128)(2,1)S(1)}, bf16[256,128]{1,0:T(8,128)(2,1)S(1)}, u32[]{:S(2)}, u32[]{:S(2)}) collective-permute-start(bf16[256,128]{1,0:T(8,128)(2,1)S(1)} %add_convert_fusion.own), channel_id=1, source_target_pairs={{0,6},{1,7},{2,4},{3,5},{4,2},{5,3},{6,0},{7,1},{8,14},{9,15},{10,... | collective-permute-start | bytes 196616 | tf_op jit(solution)/shard_map/ppermute | solution.py:175
  21.9 4.3 %collective-permute-start.10 = (bf16[256,128]{1,0:T(8,128)(2,1)S(1)}, bf16[256,128]{1,0:T(8,128)(2,1)S(1)}, u32[]{:S(2)}, u32[]{:S(2)}) collective-permute-start(bf16[256,128]{1,0:T(8,128)(2,1)S(1)} %add_convert_fusion.own), channel_id=1, source_target_pairs={{0,4},{1,3},{2,6},{3,1},{4,0},{5,7},{6,2},{7,5},{8,12},{9,11},{10,... | collective-permute-start | bytes 196616 | tf_op jit(solution)/shard_map/ppermute | solution.py:175
  22.4 4.3 %collective-permute-start.9 = (bf16[256,128]{1,0:T(8,128)(2,1)S(1)}, bf16[256,128]{1,0:T(8,128)(2,1)S(1)}, u32[]{:S(2)}, u32[]{:S(2)}) collective-permute-start(bf16[256,128]{1,0:T(8,128)(2,1)S(1)} %add_convert_fusion.own), channel_id=1, source_target_pairs={{0,2},{1,5},{2,0},{3,7},{4,6},{5,1},{6,4},{7,3},{8,10},{9,13},{10,... | collective-permute-start | bytes 196616 | tf_op jit(solution)/shard_map/ppermute | solution.py:175
  26.8 5.0 %collective-permute-start.13 = (bf16[256,128]{1,0:T(8,128)(2,1)S(1)}, bf16[256,128]{1,0:T(8,128)(2,1)S(1)}, u32[]{:S(2)}, u32[]{:S(2)}) collective-permute-start(bf16[256,128]{1,0:T(8,128)(2,1)S(1)} %convert_element_type.7.own), channel_id=1, source_target_pairs={{0,8},{1,25},{2,10},{3,27},{4,12},{5,29},{6,14},{7,31},{8,0},{9,17... | collective-permute-start | bytes 196616 | tf_op jit(solution)/shard_map/ppermute | solution.py:175
  28.4 4.3 %collective-permute-start.12 = (bf16[256,128]{1,0:T(8,128)(2,1)S(1)}, bf16[256,128]{1,0:T(8,128)(2,1)S(1)}, u32[]{:S(2)}, u32[]{:S(2)}) collective-permute-start(bf16[256,128]{1,0:T(8,128)(2,1)S(1)} %convert_element_type.7.own), channel_id=1, source_target_pairs={{0,8},{1,17},{2,10},{3,19},{4,12},{5,21},{6,14},{7,23},{8,0},{9,25... | collective-permute-start | bytes 196616 | tf_op jit(solution)/shard_map/ppermute | solution.py:175
  32.7 1.6 %collective-permute-start.14 = (f32[256,128]{1,0:T(8,128)S(1)}, f32[256,128]{1,0:T(8,128)S(1)}, u32[]{:S(2)}, u32[]{:S(2)}) collective-permute-start(f32[256,128]{1,0:T(8,128)S(1)} %shard_map.110), channel_id=1, source_target_pairs={{0,1},{1,0},{2,3},{3,2},{4,5},{5,4},{6,7},{7,6},{8,9},{9,8},{10,11... | collective-permute-start | bytes 393224 | tf_op jit(solution)/shard_map/ppermute | solution.py:18

commit v7 on v6

--- a/solution.py
+++ b/solution.py
@@ -180,7 +180,8 @@
     own, first, second, third = (
         part[...].astype(jnp.float32) for part in (own, first, second, third)
     )
-    total[...] = jnp.where(even, (own + first) + (second + third), (own + second) + (first + third))
+    summed_up = jnp.where(even, (own + first) + (second + third), (own + second) + (first + third))
+    total[...] = summed_up.astype(total.dtype)
 
 
 def half_kernel(own, near, far, half):
@@ -204,7 +205,8 @@
                 mixed(low, 2 * mask, mask),
                 mixed(low, 3 * mask, 3 * mask),
             ]
-            (total,) = call(four_kernel, wide, low, *terms)
+            kind = low.dtype if 4 * mask < size else jnp.float32
+            (total,) = call(four_kernel, [(low.shape, kind)], low, *terms)
         else:
             near, far = mixed(low, mask, 2 * mask), mixed(low, mask, 3 * mask)
             (half,) = call(half_kernel, wide, low, near, far)

time: 35.2 us -> 35.1 us (level)
  no operation moved by 1% of the time
where the time goes in v7:
time: 35.1 us; the launch traced here: 35 us
  starting transfers between devices  15.3 us (44%)
  waiting for transfers between devices  9.6 us (27%)
  Pallas kernels  7.84 us (22%)
  local copies, waits for them, and re-layouts  1.41 us (4%)
  between operations  0.81 us (2%)
    ppermute x10, starting transfers between devices, swapped(): return lax.ppermute(value, 'dom', pairs)  9.62 us
    pallas_call x8, Pallas kernels, call(): pl.pallas_call(body, out_shape=[pltpu.VMEM(shape, dtype) for shape, dtype...  7.84 us
    ppermute x5, waiting for transfers between devices, mixed(): return lax.ppermute(value, 'dom', pairs)  7.74 us
    ppermute x5, starting transfers between devices, mixed(): return lax.ppermute(value, 'dom', pairs)  5.64 us
    ppermute x10, waiting for transfers between devices, swapped(): return lax.ppermute(value, 'dom', pairs)  1.87 us
    unnamed x15, local copies, waits for them, and re-layouts  0.75 us
  transfers between devices with their start and end apart: 15, of which 8 were waited for; matrix products, arithmetic and copies ran while one was open for 2% of the time, Pallas kernels for 12%

profile of v7, /device:TPU:0, one launch (start us, length us, event | category | flops | bytes accessed | tf_op | source)
XLA Modules:
  0.0 35.0 jit_solution(16889051822501817284)
XLA Ops:
  0.6 1.0 %shard_map.103 = (bf16[1152,128]{1,0:T(8,128)(2,1)S(1)}, bf16[512,1152]{1,0:T(8,128)(2,1)S(1)}) custom-call(bf16[1152,128]{1,0:T(8,128)(2,1)} %features.1, s32[4,128]{1,0:T(4,128)} %send_rows.3), custom_call_target="tpu_custom_call" | custom-call | tf_op jit(solution)/shard_map/pallas_call | solution.py:40
  1.7 0.0 copy-start
  1.7 0.0 copy-start.1
  1.7 0.0 copy-start.5
  1.7 0.0 copy-start.6
  1.7 0.5 %shard_map.105 = (bf16[128,128]{1,0:T(8,128)(2,1)S(1)}, bf16[128,128]{1,0:T(8,128)(2,1)S(1)}, bf16[128,128]{1,0:T(8,128)(2,1)S(1)}, bf16[128,128]{1,0:T(8,128)(2,1)S(1)}) custom-call(bf16[512,1152]{1,0:T(8,128)(2,1)S(1)} %get-tuple-element.24.picker, bf16[1152,128]{1,0:T(8,128)(2,1)S(1)} %get-tuple-element.23.features), custom_call_target="tpu_custom_call" | custom-call | flops 4000000000 | bytes 1048576 | tf_op jit(solution)/shard_map/pallas_call | solution.py:40
  2.2 0.5 %collective-permute-start = (bf16[128,128]{1,0:T(8,128)(2,1)S(1)}, bf16[128,128]{1,0:T(8,128)(2,1)S(1)}, u32[]{:S(2)}, u32[]{:S(2)}) collective-permute-start(bf16[128,128]{1,0:T(8,128)(2,1)S(1)} %get-tuple-element.27), channel_id=1, source_target_pairs={{0,1},{1,0},{2,3},{3,2},{4,5},{5,4},{6,7},{7,6},{8,9},{9,8},{10,11... | collective-permute-start | bytes 98312 | tf_op jit(solution)/shard_map/ppermute | solution.py:18
  2.7 2.6 %collective-permute-start.1 = (bf16[128,128]{1,0:T(8,128)(2,1)S(1)}, bf16[128,128]{1,0:T(8,128)(2,1)S(1)}, u32[]{:S(2)}, u32[]{:S(2)}) collective-permute-start(bf16[128,128]{1,0:T(8,128)(2,1)S(1)} %get-tuple-element.28), channel_id=1, source_target_pairs={{0,2},{1,3},{2,0},{3,1},{4,6},{5,7},{6,4},{7,5},{8,10},{9,11},{10,... | collective-permute-start | bytes 98312 | tf_op jit(solution)/shard_map/ppermute | solution.py:18
  5.3 1.5 %collective-permute-start.2 = (bf16[128,128]{1,0:T(8,128)(2,1)S(1)}, bf16[128,128]{1,0:T(8,128)(2,1)S(1)}, u32[]{:S(2)}, u32[]{:S(2)}) collective-permute-start(bf16[128,128]{1,0:T(8,128)(2,1)S(1)} %get-tuple-element.29), channel_id=1, source_target_pairs={{0,4},{1,5},{2,6},{3,7},{4,0},{5,1},{6,2},{7,3},{8,12},{9,13},{10,... | collective-permute-start | bytes 98312 | tf_op jit(solution)/shard_map/ppermute | solution.py:18
  6.8 0.0 copy-start.3
  6.8 1.6 %collective-permute-start.3 = (bf16[128,128]{1,0:T(8,128)(2,1)S(1)}, bf16[128,128]{1,0:T(8,128)(2,1)S(1)}, u32[]{:S(2)}, u32[]{:S(2)}) collective-permute-start(bf16[128,128]{1,0:T(8,128)(2,1)S(1)} %get-tuple-element.30), channel_id=1, source_target_pairs={{0,8},{1,9},{2,10},{3,11},{4,12},{5,13},{6,14},{7,15},{8,0},{9,1},... | collective-permute-start | bytes 98312 | tf_op jit(solution)/shard_map/ppermute | solution.py:18
  8.4 0.0 copy-done
  8.4 0.0 copy-done.1
  8.4 0.0 copy-done.5
  8.4 0.0 copy-done.6
  8.4 2.1 %shard_map.104 = (bf16[1152,1152]{1,0:T(8,128)(2,1)S(1)}, f32[1152,128]{1,0:T(8,128)S(1)}, f32[512,128]{1,0:T(8,128)S(1)}, bf16[512,512]{1,0:T(8,128)(2,1)S(1)}) custom-call(bf16[1152,1152]{1,0:T(8,128)(2,1)S(1)} %copy-done.1, s32[18,18]{1,0:T(8,128)S(1)} %copy-done.5, bf16[1152,128]{1,0:T(8,128)(2,1)S(1)} %get-tuple-element.23.features, ...), custom_call_target="tpu_custom_call" | custom-call | tf_op jit(solution)/shard_map/pallas_call | solution.py:40
  10.5 0.0 collective-permute-done.rest_0_
  10.5 0.0 collective-permute-done.1.rest_1_
  10.5 0.0 collective-permute-done.2.rest_2_
  10.5 0.2 collective-permute-done.3.rest_3_
  10.7 0.3 shard_map.107
  11.0 0.0 copy-start.2
  11.0 0.0 copy-start.4
  11.0 0.1 collective-permute-start.4
  11.1 0.6 %collective-permute-start.5 = (bf16[128,128]{1,0:T(8,128)(2,1)S(1)}, bf16[128,128]{1,0:T(8,128)(2,1)S(1)}, u32[]{:S(2)}, u32[]{:S(2)}) collective-permute-start(bf16[128,128]{1,0:T(8,128)(2,1)S(1)} %get-tuple-element.38), channel_id=1, source_target_pairs={{0,2},{1,3},{2,0},{3,1},{4,6},{5,7},{6,4},{7,5},{8,10},{9,11},{10,... | collective-permute-start | bytes 98312 | tf_op jit(solution)/shard_map/ppermute | solution.py:18
  11.7 0.3 collective-permute-start.6
  12.0 1.8 %collective-permute-start.7 = (bf16[128,128]{1,0:T(8,128)(2,1)S(1)}, bf16[128,128]{1,0:T(8,128)(2,1)S(1)}, u32[]{:S(2)}, u32[]{:S(2)}) collective-permute-start(bf16[128,128]{1,0:T(8,128)(2,1)S(1)} %get-tuple-element.40), channel_id=1, source_target_pairs={{0,8},{1,9},{2,10},{3,11},{4,12},{5,13},{6,14},{7,15},{8,0},{9,1},... | collective-permute-start | bytes 98312 | tf_op jit(solution)/shard_map/ppermute | solution.py:18
  13.8 0.0 copy-done.3
  13.8 2.1 %shard_map.106 = (bf16[1152,128]{1,0:T(8,128)(2,1)S(1)}, bf16[1152,128]{1,0:T(8,128)(2,1)S(1)}, f32[128,1152]{1,0:T(8,128)S(1)}, f32[1152,128]{1,0:T(8,128)S(1)}) custom-call(f32[1152,128]{1,0:T(8,128)S(1)} %get-tuple-element.25.inner_first, bf16[1152,512]{1,0:T(8,128)(2,1)S(1)} %copy-done, bf16[128,128]{1,0:T(8,128)(2,1)S(1)} %copy-done.3, ...), custom_call_target="tpu_custom_call" | custom-call | tf_op jit(solution)/shard_map/pallas_call | solution.py:40
  15.9 0.0 collective-permute-done.4.rest_4_
  15.9 0.0 collective-permute-done.5.rest_5_
  15.9 0.0 collective-permute-done.6.rest_6_
  15.9 0.0 collective-permute-done.7.rest_7_
  16.0 0.0 copy-done.2
  16.0 0.0 copy-done.4
  16.0 1.8 %shard_map.108 = (bf16[1152,128]{1,0:T(8,128)(2,1)S(1)}, f32[256,128]{1,0:T(8,128)S(1)}) custom-call(f32[1152,128]{1,0:T(8,128)S(1)} %get-tuple-element.31.inner, bf16[1152,128]{1,0:T(8,128)(2,1)S(1)} %get-tuple-element.32.hidden, f32[128,1152]{1,0:T(8,128)S(1)} %get-tuple-element.33.slope, bf16[1152,128]{1,0:T(8,128)(2,1)S(1)} %get-tuple-element.34.agg, ...), custom_call_target="tpu_custom_call" | custom-call | tf_op jit(solution)/shard_map/pallas_call | solution.py:40
  17.8 0.1 collective-permute-start.8
  17.9 1.3 %collective-permute-done.8 = f32[256,128]{1,0:T(8,128)S(1)} collective-permute-done((f32[256,128]{1,0:T(8,128)S(1)}, f32[256,128]{1,0:T(8,128)S(1)}, u32[]{:S(2)}, u32[]{:S(2)}) %collective-permute-start.8) | collective-permute-done | bytes 131104 | tf_op jit(solution)/shard_map/ppermute | solution.py:18
  19.2 2.7 %collective-permute-start.11 = (bf16[256,128]{1,0:T(8,128)(2,1)S(1)}, bf16[256,128]{1,0:T(8,128)(2,1)S(1)}, u32[]{:S(2)}, u32[]{:S(2)}) collective-permute-start(bf16[256,128]{1,0:T(8,128)(2,1)S(1)} %add_convert_fusion.own), channel_id=1, source_target_pairs={{0,6},{1,7},{2,4},{3,5},{4,2},{5,3},{6,0},{7,1},{8,14},{9,15},{10,... | collective-permute-start | bytes 196616 | tf_op jit(solution)/shard_map/ppermute | solution.py:175
  21.9 0.5 %collective-permute-start.10 = (bf16[256,128]{1,0:T(8,128)(2,1)S(1)}, bf16[256,128]{1,0:T(8,128)(2,1)S(1)}, u32[]{:S(2)}, u32[]{:S(2)}) collective-permute-start(bf16[256,128]{1,0:T(8,128)(2,1)S(1)} %add_convert_fusion.own), channel_id=1, source_target_pairs={{0,4},{1,3},{2,6},{3,1},{4,0},{5,7},{6,2},{7,5},{8,12},{9,11},{10,... | collective-permute-start | bytes 196616 | tf_op jit(solution)/shard_map/ppermute | solution.py:175
  22.4 0.3 collective-permute-start.9
  22.8 1.9 %collective-permute-done.11.third = bf16[256,128]{1,0:T(8,128)(2,1)S(1)} collective-permute-done((bf16[256,128]{1,0:T(8,128)(2,1)S(1)}, bf16[256,128]{1,0:T(8,128)(2,1)S(1)}, u32[]{:S(2)}, u32[]{:S(2)}) %collective-permute-start.11) | collective-permute-done | bytes 65568 | tf_op jit(solution)/shard_map/ppermute | solution.py:175
  24.6 1.6 %collective-permute-done.10.second = bf16[256,128]{1,0:T(8,128)(2,1)S(1)} collective-permute-done((bf16[256,128]{1,0:T(8,128)(2,1)S(1)}, bf16[256,128]{1,0:T(8,128)(2,1)S(1)}, u32[]{:S(2)}, u32[]{:S(2)}) %collective-permute-start.10) | collective-permute-done | bytes 65568 | tf_op jit(solution)/shard_map/ppermute | solution.py:175
  26.2 0.5 %collective-permute-done.9.first = bf16[256,128]{1,0:T(8,128)(2,1)S(1)} collective-permute-done((bf16[256,128]{1,0:T(8,128)(2,1)S(1)}, bf16[256,128]{1,0:T(8,128)(2,1)S(1)}, u32[]{:S(2)}, u32[]{:S(2)}) %collective-permute-start.9) | collective-permute-done | bytes 65568 | tf_op jit(solution)/shard_map/ppermute | solution.py:175
  26.7 0.1 shard_map.109.own
  26.7 1.6 %collective-permute-start.13 = (bf16[256,128]{1,0:T(8,128)(2,1)S(1)}, bf16[256,128]{1,0:T(8,128)(2,1)S(1)}, u32[]{:S(2)}, u32[]{:S(2)}) collective-permute-start(bf16[256,128]{1,0:T(8,128)(2,1)S(1)} %shard_map.109.own), channel_id=1, source_target_pairs={{0,8},{1,25},{2,10},{3,27},{4,12},{5,29},{6,14},{7,31},{8,0},{9,17... | collective-permute-start | bytes 196616 | tf_op jit(solution)/shard_map/ppermute | solution.py:175
  28.4 0.4 %collective-permute-start.12 = (bf16[256,128]{1,0:T(8,128)(2,1)S(1)}, bf16[256,128]{1,0:T(8,128)(2,1)S(1)}, u32[]{:S(2)}, u32[]{:S(2)}) collective-permute-start(bf16[256,128]{1,0:T(8,128)(2,1)S(1)} %shard_map.109.own), channel_id=1, source_target_pairs={{0,8},{1,17},{2,10},{3,19},{4,12},{5,21},{6,14},{7,23},{8,0},{9,25... | collective-permute-start | bytes 196616 | tf_op jit(solution)/shard_map/ppermute | solution.py:175
  28.8 2.9 %collective-permute-done.13.far = bf16[256,128]{1,0:T(8,128)(2,1)S(1)} collective-permute-done((bf16[256,128]{1,0:T(8,128)(2,1)S(1)}, bf16[256,128]{1,0:T(8,128)(2,1)S(1)}, u32[]{:S(2)}, u32[]{:S(2)}) %collective-permute-start.13) | collective-permute-done | bytes 65568 | tf_op jit(solution)/shard_map/ppermute | solution.py:175
  31.7 0.9 %collective-permute-done.12.near = bf16[256,128]{1,0:T(8,128)(2,1)S(1)} collective-permute-done((bf16[256,128]{1,0:T(8,128)(2,1)S(1)}, bf16[256,128]{1,0:T(8,128)(2,1)S(1)}, u32[]{:S(2)}, u32[]{:S(2)}) %collective-permute-start.12) | collective-permute-done | bytes 65568 | tf_op jit(solution)/shard_map/ppermute | solution.py:175
  32.7 0.6 %collective-permute-start.14 = (f32[256,128]{1,0:T(8,128)S(1)}, f32[256,128]{1,0:T(8,128)S(1)}, u32[]{:S(2)}, u32[]{:S(2)}) collective-permute-start(f32[256,128]{1,0:T(8,128)S(1)} %shard_map.110), channel_id=1, source_target_pairs={{0,1},{1,0},{2,3},{3,2},{4,5},{5,4},{6,7},{7,6},{8,9},{9,8},{10,11... | collective-permute-start | bytes 393224 | tf_op jit(solution)/shard_map/ppermute | solution.py:18
  33.3 0.7 %copy.11 = bf16[1152,128]{1,0:T(8,128)(2,1)} copy(bf16[1152,128]{1,0:T(8,128)(2,1)S(1)} %get-tuple-element.45) | data formatting | bytes 589824
  34.0 0.3 collective-permute-done.14
  34.3 0.7 %fusion = (f32[128,128]{1,0:T(8,128)}, f32[128,128]{1,0:T(8,128)}) fusion(f32[256,128]{1,0:T(8,128)S(1)} %add.7), kind=kLoop, calls=%fused_computation.1 | loop fusion | bytes 262144 | tf_op jit(solution)/shard_map/slice | solution.py:288
  (3 shorter events, 0.1 us)
Async XLA Ops:
  1.7 6.7 %copy-start = (bf16[1152,512]{1,0:T(8,128)(2,1)S(1)}, bf16[1152,512]{1,0:T(8,128)(2,1)}, u32[]{:S(2)}) copy-start(bf16[1152,512]{1,0:T(8,128)(2,1)} %halo_bonds.5) | copy-start | bytes 3538948
  1.7 6.7 %copy-start.1 = (bf16[1152,1152]{1,0:T(8,128)(2,1)S(1)}, bf16[1152,1152]{1,0:T(8,128)(2,1)}, u32[]{:S(2)}) copy-start(bf16[1152,1152]{1,0:T(8,128)(2,1)} %local_bonds.1) | copy-start | bytes 7962628
  1.7 6.7 %copy-start.5 = (s32[18,18]{1,0:T(8,128)S(1)}, s32[18,18]{1,0:T(8,128)}, u32[]{:S(2)}) copy-start(s32[18,18]{1,0:T(8,128)} %tile_mask.1) | copy-start | bytes 3892
  1.7 6.7 %copy-start.6 = (s32[4,128]{1,0:T(4,128)S(1)}, s32[4,128]{1,0:T(4,128)}, u32[]{:S(2)}) copy-start(s32[4,128]{1,0:T(4,128)} %send_rows.3) | copy-start | bytes 6148
  2.2 8.3 %collective-permute-start = (bf16[128,128]{1,0:T(8,128)(2,1)S(1)}, bf16[128,128]{1,0:T(8,128)(2,1)S(1)}, u32[]{:S(2)}, u32[]{:S(2)}) collective-permute-start(bf16[128,128]{1,0:T(8,128)(2,1)S(1)} %get-tuple-element.27), channel_id=1, source_target_pairs={{0,1},{1,0},{2,3},{3,2},{4,5},{5,4},{6,7},{7,6},{8,9},{9,8},{10,11... | collective-permute-start | bytes 98312 | tf_op jit(solution)/shard_map/ppermute | solution.py:18
  2.7 7.8 %collective-permute-start.1 = (bf16[128,128]{1,0:T(8,128)(2,1)S(1)}, bf16[128,128]{1,0:T(8,128)(2,1)S(1)}, u32[]{:S(2)}, u32[]{:S(2)}) collective-permute-start(bf16[128,128]{1,0:T(8,128)(2,1)S(1)} %get-tuple-element.28), channel_id=1, source_target_pairs={{0,2},{1,3},{2,0},{3,1},{4,6},{5,7},{6,4},{7,5},{8,10},{9,11},{10,... | collective-permute-start | bytes 98312 | tf_op jit(solution)/shard_map/ppermute | solution.py:18
  5.3 5.2 %collective-permute-start.2 = (bf16[128,128]{1,0:T(8,128)(2,1)S(1)}, bf16[128,128]{1,0:T(8,128)(2,1)S(1)}, u32[]{:S(2)}, u32[]{:S(2)}) collective-permute-start(bf16[128,128]{1,0:T(8,128)(2,1)S(1)} %get-tuple-element.29), channel_id=1, source_target_pairs={{0,4},{1,5},{2,6},{3,7},{4,0},{5,1},{6,2},{7,3},{8,12},{9,13},{10,... | collective-permute-start | bytes 98312 | tf_op jit(solution)/shard_map/ppermute | solution.py:18
  6.8 7.0 %copy-start.3 = (bf16[128,128]{1,0:T(8,128)(2,1)S(1)}, bf16[128,128]{1,0:T(8,128)(2,1)}, u32[]{:S(2)}) copy-start(bf16[128,128]{1,0:T(8,128)(2,1)} %first_weight.3) | copy-start | bytes 98308
  6.8 3.9 %collective-permute-start.3 = (bf16[128,128]{1,0:T(8,128)(2,1)S(1)}, bf16[128,128]{1,0:T(8,128)(2,1)S(1)}, u32[]{:S(2)}, u32[]{:S(2)}) collective-permute-start(bf16[128,128]{1,0:T(8,128)(2,1)S(1)} %get-tuple-element.30), channel_id=1, source_target_pairs={{0,8},{1,9},{2,10},{3,11},{4,12},{5,13},{6,14},{7,15},{8,0},{9,1},... | collective-permute-start | bytes 98312 | tf_op jit(solution)/shard_map/ppermute | solution.py:18
  11.0 4.9 %copy-start.2 = (bf16[1152,128]{1,0:T(8,128)(2,1)S(1)}, bf16[1152,128]{1,0:T(8,128)(2,1)}, u32[]{:S(2)}) copy-start(bf16[1152,128]{1,0:T(8,128)(2,1)} %targets.1) | copy-start | bytes 884740
  11.0 4.9 %copy-start.4 = (bf16[128,128]{1,0:T(8,128)(2,1)S(1)}, bf16[128,128]{1,0:T(8,128)(2,1)}, u32[]{:S(2)}) copy-start(bf16[128,128]{1,0:T(8,128)(2,1)} %second_weight.1) | copy-start | bytes 98308
  11.0 4.8 %collective-permute-start.4 = (bf16[128,128]{1,0:T(8,128)(2,1)S(1)}, bf16[128,128]{1,0:T(8,128)(2,1)S(1)}, u32[]{:S(2)}, u32[]{:S(2)}) collective-permute-start(bf16[128,128]{1,0:T(8,128)(2,1)S(1)} %get-tuple-element.37), channel_id=1, source_target_pairs={{0,1},{1,0},{2,3},{3,2},{4,5},{5,4},{6,7},{7,6},{8,9},{9,8},{10,11... | collective-permute-start | bytes 98312 | tf_op jit(solution)/shard_map/ppermute | solution.py:18
  11.1 4.8 %collective-permute-start.5 = (bf16[128,128]{1,0:T(8,128)(2,1)S(1)}, bf16[128,128]{1,0:T(8,128)(2,1)S(1)}, u32[]{:S(2)}, u32[]{:S(2)}) collective-permute-start(bf16[128,128]{1,0:T(8,128)(2,1)S(1)} %get-tuple-element.38), channel_id=1, source_target_pairs={{0,2},{1,3},{2,0},{3,1},{4,6},{5,7},{6,4},{7,5},{8,10},{9,11},{10,... | collective-permute-start | bytes 98312 | tf_op jit(solution)/shard_map/ppermute | solution.py:18
  11.7 4.2 %collective-permute-start.6 = (bf16[128,128]{1,0:T(8,128)(2,1)S(1)}, bf16[128,128]{1,0:T(8,128)(2,1)S(1)}, u32[]{:S(2)}, u32[]{:S(2)}) collective-permute-start(bf16[128,128]{1,0:T(8,128)(2,1)S(1)} %get-tuple-element.39), channel_id=1, source_target_pairs={{0,4},{1,5},{2,6},{3,7},{4,0},{5,1},{6,2},{7,3},{8,12},{9,13},{10,... | collective-permute-start | bytes 98312 | tf_op jit(solution)/shard_map/ppermute | solution.py:18
  12.0 3.9 %collective-permute-start.7 = (bf16[128,128]{1,0:T(8,128)(2,1)S(1)}, bf16[128,128]{1,0:T(8,128)(2,1)S(1)}, u32[]{:S(2)}, u32[]{:S(2)}) collective-permute-start(bf16[128,128]{1,0:T(8,128)(2,1)S(1)} %get-tuple-element.40), channel_id=1, source_target_pairs={{0,8},{1,9},{2,10},{3,11},{4,12},{5,13},{6,14},{7,15},{8,0},{9,1},... | collective-permute-start | bytes 98312 | tf_op jit(solution)/shard_map/ppermute | solution.py:18
  17.8 1.4 %collective-permute-start.8 = (f32[256,128]{1,0:T(8,128)S(1)}, f32[256,128]{1,0:T(8,128)S(1)}, u32[]{:S(2)}, u32[]{:S(2)}) collective-permute-start(f32[256,128]{1,0:T(8,128)S(1)} %get-tuple-element.42), channel_id=1, source_target_pairs={{0,1},{1,0},{2,3},{3,2},{4,5},{5,4},{6,7},{7,6},{8,9},{9,8},{10,11... | collective-permute-start | bytes 393224 | tf_op jit(solution)/shard_map/ppermute | solution.py:18
  19.2 5.4 %collective-permute-start.11 = (bf16[256,128]{1,0:T(8,128)(2,1)S(1)}, bf16[256,128]{1,0:T(8,128)(2,1)S(1)}, u32[]{:S(2)}, u32[]{:S(2)}) collective-permute-start(bf16[256,128]{1,0:T(8,128)(2,1)S(1)} %add_convert_fusion.own), channel_id=1, source_target_pairs={{0,6},{1,7},{2,4},{3,5},{4,2},{5,3},{6,0},{7,1},{8,14},{9,15},{10,... | collective-permute-start | bytes 196616 | tf_op jit(solution)/shard_map/ppermute | solution.py:175
  21.9 4.3 %collective-permute-start.10 = (bf16[256,128]{1,0:T(8,128)(2,1)S(1)}, bf16[256,128]{1,0:T(8,128)(2,1)S(1)}, u32[]{:S(2)}, u32[]{:S(2)}) collective-permute-start(bf16[256,128]{1,0:T(8,128)(2,1)S(1)} %add_convert_fusion.own), channel_id=1, source_target_pairs={{0,4},{1,3},{2,6},{3,1},{4,0},{5,7},{6,2},{7,5},{8,12},{9,11},{10,... | collective-permute-start | bytes 196616 | tf_op jit(solution)/shard_map/ppermute | solution.py:175
  22.4 4.3 %collective-permute-start.9 = (bf16[256,128]{1,0:T(8,128)(2,1)S(1)}, bf16[256,128]{1,0:T(8,128)(2,1)S(1)}, u32[]{:S(2)}, u32[]{:S(2)}) collective-permute-start(bf16[256,128]{1,0:T(8,128)(2,1)S(1)} %add_convert_fusion.own), channel_id=1, source_target_pairs={{0,2},{1,5},{2,0},{3,7},{4,6},{5,1},{6,4},{7,3},{8,10},{9,13},{10,... | collective-permute-start | bytes 196616 | tf_op jit(solution)/shard_map/ppermute | solution.py:175
  26.7 5.0 %collective-permute-start.13 = (bf16[256,128]{1,0:T(8,128)(2,1)S(1)}, bf16[256,128]{1,0:T(8,128)(2,1)S(1)}, u32[]{:S(2)}, u32[]{:S(2)}) collective-permute-start(bf16[256,128]{1,0:T(8,128)(2,1)S(1)} %shard_map.109.own), channel_id=1, source_target_pairs={{0,8},{1,25},{2,10},{3,27},{4,12},{5,29},{6,14},{7,31},{8,0},{9,17... | collective-permute-start | bytes 196616 | tf_op jit(solution)/shard_map/ppermute | solution.py:175
  28.4 4.3 %collective-permute-start.12 = (bf16[256,128]{1,0:T(8,128)(2,1)S(1)}, bf16[256,128]{1,0:T(8,128)(2,1)S(1)}, u32[]{:S(2)}, u32[]{:S(2)}) collective-permute-start(bf16[256,128]{1,0:T(8,128)(2,1)S(1)} %shard_map.109.own), channel_id=1, source_target_pairs={{0,8},{1,17},{2,10},{3,19},{4,12},{5,21},{6,14},{7,23},{8,0},{9,25... | collective-permute-start | bytes 196616 | tf_op jit(solution)/shard_map/ppermute | solution.py:175
  32.7 1.6 %collective-permute-start.14 = (f32[256,128]{1,0:T(8,128)S(1)}, f32[256,128]{1,0:T(8,128)S(1)}, u32[]{:S(2)}, u32[]{:S(2)}) collective-permute-start(f32[256,128]{1,0:T(8,128)S(1)} %shard_map.110), channel_id=1, source_target_pairs={{0,1},{1,0},{2,3},{3,2},{4,5},{5,4},{6,7},{7,6},{8,9},{9,8},{10,11... | collective-permute-start | bytes 393224 | tf_op jit(solution)/shard_map/ppermute | solution.py:18

commit v8 on v7

--- a/solution.py
+++ b/solution.py
@@ -193,6 +193,8 @@
 def summed(total):
     size = lax.axis_size("dom")
     wide = [(total.shape, jnp.float32)]
+    middle = total.shape[0] // 2
+    parts = slice(None, middle), slice(middle, None)
     total = total + swapped(total, 1)
     mask = 2
     while mask < size:
@@ -210,9 +212,12 @@
         else:
             near, far = mixed(low, mask, 2 * mask), mixed(low, mask, 3 * mask)
             (half,) = call(half_kernel, wide, low, near, far)
-            total = half + swapped(half, 1)
+            other = swapped(half, 1)
+            if 4 * mask >= size:
+                return [half[part] + other[part] for part in parts]
+            total = half + other
         mask *= 4
-    return total
+    return [total[part] for part in parts]
 
 
 def local(
@@ -284,8 +289,7 @@
         *halo_agg,
         scratch=[stacked, stacked],
     )
-    grads = summed(grads)
-    return prediction, grads[:wide], grads[wide:]
+    return (prediction, *summed(grads))
 
 
 def solution(mesh):

time: 35.1 us -> 35.1 us (level)
  local copies, waits for them, and re-layouts: 1.41 us -> 0.75 us
  other arithmetic: 0.04 us -> 0.69 us
    slice x1 -> x0, local copies, waits for them, and re-layouts: 0.66 us -> none  [local(): return (prediction, grads[:wide], grads[wide:])]
    add x1, other arithmetic: 0.02 us -> 0.67 us  [summed(): return [half[part] + other[part] for part in parts]]
where the time goes in v8:
time: 35.1 us; the launch traced here: 35 us
  starting transfers between devices  15.3 us (44%)
  waiting for transfers between devices  9.6 us (27%)
  Pallas kernels  7.84 us (22%)
  between operations  0.81 us (2%)
  local copies, waits for them, and re-layouts  0.75 us (2%)
  other arithmetic  0.69 us (2%)
    ppermute x10, starting transfers between devices, swapped(): return lax.ppermute(value, 'dom', pairs)  9.62 us
    pallas_call x8, Pallas kernels, call(): pl.pallas_call(body, out_shape=[pltpu.VMEM(shape, dtype) for shape, dtype...  7.84 us
    ppermute x5, waiting for transfers between devices, mixed(): return lax.ppermute(value, 'dom', pairs)  7.74 us
    ppermute x5, starting transfers between devices, mixed(): return lax.ppermute(value, 'dom', pairs)  5.64 us
    ppermute x10, waiting for transfers between devices, swapped(): return lax.ppermute(value, 'dom', pairs)  1.87 us
    unnamed x15, local copies, waits for them, and re-layouts  0.75 us
  transfers between devices with their start and end apart: 15, of which 8 were waited for; matrix products, arithmetic and copies ran while one was open for 2% of the time, Pallas kernels for 12%

profile of v8, /device:TPU:0, one launch (start us, length us, event | category | flops | bytes accessed | tf_op | source)
XLA Modules:
  0.0 35.0 jit_solution(18284210178355282990)
XLA Ops:
  0.6 1.0 %shard_map.103 = (bf16[1152,128]{1,0:T(8,128)(2,1)S(1)}, bf16[512,1152]{1,0:T(8,128)(2,1)S(1)}) custom-call(bf16[1152,128]{1,0:T(8,128)(2,1)} %features.1, s32[4,128]{1,0:T(4,128)} %send_rows.3), custom_call_target="tpu_custom_call" | custom-call | tf_op jit(solution)/shard_map/pallas_call | solution.py:40
  1.7 0.0 copy-start
  1.7 0.0 copy-start.1
  1.7 0.0 copy-start.5
  1.7 0.0 copy-start.6
  1.7 0.5 %shard_map.105 = (bf16[128,128]{1,0:T(8,128)(2,1)S(1)}, bf16[128,128]{1,0:T(8,128)(2,1)S(1)}, bf16[128,128]{1,0:T(8,128)(2,1)S(1)}, bf16[128,128]{1,0:T(8,128)(2,1)S(1)}) custom-call(bf16[512,1152]{1,0:T(8,128)(2,1)S(1)} %get-tuple-element.24.picker, bf16[1152,128]{1,0:T(8,128)(2,1)S(1)} %get-tuple-element.23.features), custom_call_target="tpu_custom_call" | custom-call | flops 4000000000 | bytes 1048576 | tf_op jit(solution)/shard_map/pallas_call | solution.py:40
  2.2 0.5 %collective-permute-start = (bf16[128,128]{1,0:T(8,128)(2,1)S(1)}, bf16[128,128]{1,0:T(8,128)(2,1)S(1)}, u32[]{:S(2)}, u32[]{:S(2)}) collective-permute-start(bf16[128,128]{1,0:T(8,128)(2,1)S(1)} %get-tuple-element.27), channel_id=1, source_target_pairs={{0,1},{1,0},{2,3},{3,2},{4,5},{5,4},{6,7},{7,6},{8,9},{9,8},{10,11... | collective-permute-start | bytes 98312 | tf_op jit(solution)/shard_map/ppermute | solution.py:18
  2.7 2.6 %collective-permute-start.1 = (bf16[128,128]{1,0:T(8,128)(2,1)S(1)}, bf16[128,128]{1,0:T(8,128)(2,1)S(1)}, u32[]{:S(2)}, u32[]{:S(2)}) collective-permute-start(bf16[128,128]{1,0:T(8,128)(2,1)S(1)} %get-tuple-element.28), channel_id=1, source_target_pairs={{0,2},{1,3},{2,0},{3,1},{4,6},{5,7},{6,4},{7,5},{8,10},{9,11},{10,... | collective-permute-start | bytes 98312 | tf_op jit(solution)/shard_map/ppermute | solution.py:18
  5.3 1.5 %collective-permute-start.2 = (bf16[128,128]{1,0:T(8,128)(2,1)S(1)}, bf16[128,128]{1,0:T(8,128)(2,1)S(1)}, u32[]{:S(2)}, u32[]{:S(2)}) collective-permute-start(bf16[128,128]{1,0:T(8,128)(2,1)S(1)} %get-tuple-element.29), channel_id=1, source_target_pairs={{0,4},{1,5},{2,6},{3,7},{4,0},{5,1},{6,2},{7,3},{8,12},{9,13},{10,... | collective-permute-start | bytes 98312 | tf_op jit(solution)/shard_map/ppermute | solution.py:18
  6.8 0.0 copy-start.3
  6.8 1.6 %collective-permute-start.3 = (bf16[128,128]{1,0:T(8,128)(2,1)S(1)}, bf16[128,128]{1,0:T(8,128)(2,1)S(1)}, u32[]{:S(2)}, u32[]{:S(2)}) collective-permute-start(bf16[128,128]{1,0:T(8,128)(2,1)S(1)} %get-tuple-element.30), channel_id=1, source_target_pairs={{0,8},{1,9},{2,10},{3,11},{4,12},{5,13},{6,14},{7,15},{8,0},{9,1},... | collective-permute-start | bytes 98312 | tf_op jit(solution)/shard_map/ppermute | solution.py:18
  8.4 0.0 copy-done
  8.4 0.0 copy-done.1
  8.4 0.0 copy-done.5
  8.4 0.0 copy-done.6
  8.4 2.1 %shard_map.104 = (bf16[1152,1152]{1,0:T(8,128)(2,1)S(1)}, f32[1152,128]{1,0:T(8,128)S(1)}, f32[512,128]{1,0:T(8,128)S(1)}, bf16[512,512]{1,0:T(8,128)(2,1)S(1)}) custom-call(bf16[1152,1152]{1,0:T(8,128)(2,1)S(1)} %copy-done.1, s32[18,18]{1,0:T(8,128)S(1)} %copy-done.5, bf16[1152,128]{1,0:T(8,128)(2,1)S(1)} %get-tuple-element.23.features, ...), custom_call_target="tpu_custom_call" | custom-call | tf_op jit(solution)/shard_map/pallas_call | solution.py:40
  10.5 0.0 collective-permute-done.rest_0_
  10.5 0.0 collective-permute-done.1.rest_1_
  10.5 0.0 collective-permute-done.2.rest_2_
  10.5 0.2 collective-permute-done.3.rest_3_
  10.7 0.3 shard_map.107
  11.0 0.0 copy-start.2
  11.0 0.0 copy-start.4
  11.0 0.1 collective-permute-start.4
  11.1 0.6 %collective-permute-start.5 = (bf16[128,128]{1,0:T(8,128)(2,1)S(1)}, bf16[128,128]{1,0:T(8,128)(2,1)S(1)}, u32[]{:S(2)}, u32[]{:S(2)}) collective-permute-start(bf16[128,128]{1,0:T(8,128)(2,1)S(1)} %get-tuple-element.38), channel_id=1, source_target_pairs={{0,2},{1,3},{2,0},{3,1},{4,6},{5,7},{6,4},{7,5},{8,10},{9,11},{10,... | collective-permute-start | bytes 98312 | tf_op jit(solution)/shard_map/ppermute | solution.py:18
  11.7 0.3 collective-permute-start.6
  12.0 1.8 %collective-permute-start.7 = (bf16[128,128]{1,0:T(8,128)(2,1)S(1)}, bf16[128,128]{1,0:T(8,128)(2,1)S(1)}, u32[]{:S(2)}, u32[]{:S(2)}) collective-permute-start(bf16[128,128]{1,0:T(8,128)(2,1)S(1)} %get-tuple-element.40), channel_id=1, source_target_pairs={{0,8},{1,9},{2,10},{3,11},{4,12},{5,13},{6,14},{7,15},{8,0},{9,1},... | collective-permute-start | bytes 98312 | tf_op jit(solution)/shard_map/ppermute | solution.py:18
  13.8 0.0 copy-done.3
  13.8 2.1 %shard_map.106 = (bf16[1152,128]{1,0:T(8,128)(2,1)S(1)}, bf16[1152,128]{1,0:T(8,128)(2,1)S(1)}, f32[128,1152]{1,0:T(8,128)S(1)}, f32[1152,128]{1,0:T(8,128)S(1)}) custom-call(f32[1152,128]{1,0:T(8,128)S(1)} %get-tuple-element.25.inner_first, bf16[1152,512]{1,0:T(8,128)(2,1)S(1)} %copy-done, bf16[128,128]{1,0:T(8,128)(2,1)S(1)} %copy-done.3, ...), custom_call_target="tpu_custom_call" | custom-call | tf_op jit(solution)/shard_map/pallas_call | solution.py:40
  15.9 0.0 collective-permute-done.4.rest_4_
  15.9 0.0 collective-permute-done.5.rest_5_
  15.9 0.0 collective-permute-done.6.rest_6_
  15.9 0.0 collective-permute-done.7.rest_7_
  16.0 0.0 copy-done.2
  16.0 0.0 copy-done.4
  16.0 1.8 %shard_map.108 = (bf16[1152,128]{1,0:T(8,128)(2,1)S(1)}, f32[256,128]{1,0:T(8,128)S(1)}) custom-call(f32[1152,128]{1,0:T(8,128)S(1)} %get-tuple-element.31.inner, bf16[1152,128]{1,0:T(8,128)(2,1)S(1)} %get-tuple-element.32.hidden, f32[128,1152]{1,0:T(8,128)S(1)} %get-tuple-element.33.slope, bf16[1152,128]{1,0:T(8,128)(2,1)S(1)} %get-tuple-element.34.agg, ...), custom_call_target="tpu_custom_call" | custom-call | tf_op jit(solution)/shard_map/pallas_call | solution.py:40
  17.8 0.1 collective-permute-start.8
  17.9 1.3 %collective-permute-done.8 = f32[256,128]{1,0:T(8,128)S(1)} collective-permute-done((f32[256,128]{1,0:T(8,128)S(1)}, f32[256,128]{1,0:T(8,128)S(1)}, u32[]{:S(2)}, u32[]{:S(2)}) %collective-permute-start.8) | collective-permute-done | bytes 131104 | tf_op jit(solution)/shard_map/ppermute | solution.py:18
  19.2 2.7 %collective-permute-start.11 = (bf16[256,128]{1,0:T(8,128)(2,1)S(1)}, bf16[256,128]{1,0:T(8,128)(2,1)S(1)}, u32[]{:S(2)}, u32[]{:S(2)}) collective-permute-start(bf16[256,128]{1,0:T(8,128)(2,1)S(1)} %add_convert_fusion.own), channel_id=1, source_target_pairs={{0,6},{1,7},{2,4},{3,5},{4,2},{5,3},{6,0},{7,1},{8,14},{9,15},{10,... | collective-permute-start | bytes 196616 | tf_op jit(solution)/shard_map/ppermute | solution.py:175
  21.9 0.5 %collective-permute-start.10 = (bf16[256,128]{1,0:T(8,128)(2,1)S(1)}, bf16[256,128]{1,0:T(8,128)(2,1)S(1)}, u32[]{:S(2)}, u32[]{:S(2)}) collective-permute-start(bf16[256,128]{1,0:T(8,128)(2,1)S(1)} %add_convert_fusion.own), channel_id=1, source_target_pairs={{0,4},{1,3},{2,6},{3,1},{4,0},{5,7},{6,2},{7,5},{8,12},{9,11},{10,... | collective-permute-start | bytes 196616 | tf_op jit(solution)/shard_map/ppermute | solution.py:175
  22.4 0.3 collective-permute-start.9
  22.8 1.9 %collective-permute-done.11.third = bf16[256,128]{1,0:T(8,128)(2,1)S(1)} collective-permute-done((bf16[256,128]{1,0:T(8,128)(2,1)S(1)}, bf16[256,128]{1,0:T(8,128)(2,1)S(1)}, u32[]{:S(2)}, u32[]{:S(2)}) %collective-permute-start.11) | collective-permute-done | bytes 65568 | tf_op jit(solution)/shard_map/ppermute | solution.py:175
  24.6 1.6 %collective-permute-done.10.second = bf16[256,128]{1,0:T(8,128)(2,1)S(1)} collective-permute-done((bf16[256,128]{1,0:T(8,128)(2,1)S(1)}, bf16[256,128]{1,0:T(8,128)(2,1)S(1)}, u32[]{:S(2)}, u32[]{:S(2)}) %collective-permute-start.10) | collective-permute-done | bytes 65568 | tf_op jit(solution)/shard_map/ppermute | solution.py:175
  26.2 0.5 %collective-permute-done.9.first = bf16[256,128]{1,0:T(8,128)(2,1)S(1)} collective-permute-done((bf16[256,128]{1,0:T(8,128)(2,1)S(1)}, bf16[256,128]{1,0:T(8,128)(2,1)S(1)}, u32[]{:S(2)}, u32[]{:S(2)}) %collective-permute-start.9) | collective-permute-done | bytes 65568 | tf_op jit(solution)/shard_map/ppermute | solution.py:175
  26.7 0.1 shard_map.109.own
  26.7 1.6 %collective-permute-start.13 = (bf16[256,128]{1,0:T(8,128)(2,1)S(1)}, bf16[256,128]{1,0:T(8,128)(2,1)S(1)}, u32[]{:S(2)}, u32[]{:S(2)}) collective-permute-start(bf16[256,128]{1,0:T(8,128)(2,1)S(1)} %shard_map.109.own), channel_id=1, source_target_pairs={{0,8},{1,25},{2,10},{3,27},{4,12},{5,29},{6,14},{7,31},{8,0},{9,17... | collective-permute-start | bytes 196616 | tf_op jit(solution)/shard_map/ppermute | solution.py:175
  28.4 0.4 %collective-permute-start.12 = (bf16[256,128]{1,0:T(8,128)(2,1)S(1)}, bf16[256,128]{1,0:T(8,128)(2,1)S(1)}, u32[]{:S(2)}, u32[]{:S(2)}) collective-permute-start(bf16[256,128]{1,0:T(8,128)(2,1)S(1)} %shard_map.109.own), channel_id=1, source_target_pairs={{0,8},{1,17},{2,10},{3,19},{4,12},{5,21},{6,14},{7,23},{8,0},{9,25... | collective-permute-start | bytes 196616 | tf_op jit(solution)/shard_map/ppermute | solution.py:175
  28.8 2.9 %collective-permute-done.13.far = bf16[256,128]{1,0:T(8,128)(2,1)S(1)} collective-permute-done((bf16[256,128]{1,0:T(8,128)(2,1)S(1)}, bf16[256,128]{1,0:T(8,128)(2,1)S(1)}, u32[]{:S(2)}, u32[]{:S(2)}) %collective-permute-start.13) | collective-permute-done | bytes 65568 | tf_op jit(solution)/shard_map/ppermute | solution.py:175
  31.7 0.9 %collective-permute-done.12.near = bf16[256,128]{1,0:T(8,128)(2,1)S(1)} collective-permute-done((bf16[256,128]{1,0:T(8,128)(2,1)S(1)}, bf16[256,128]{1,0:T(8,128)(2,1)S(1)}, u32[]{:S(2)}, u32[]{:S(2)}) %collective-permute-start.12) | collective-permute-done | bytes 65568 | tf_op jit(solution)/shard_map/ppermute | solution.py:175
  32.7 0.6 %collective-permute-start.14 = (f32[256,128]{1,0:T(8,128)S(1)}, f32[256,128]{1,0:T(8,128)S(1)}, u32[]{:S(2)}, u32[]{:S(2)}) collective-permute-start(f32[256,128]{1,0:T(8,128)S(1)} %shard_map.110), channel_id=1, source_target_pairs={{0,1},{1,0},{2,3},{3,2},{4,5},{5,4},{6,7},{7,6},{8,9},{9,8},{10,11... | collective-permute-start | bytes 393224 | tf_op jit(solution)/shard_map/ppermute | solution.py:18
  33.3 0.7 %copy.11 = bf16[1152,128]{1,0:T(8,128)(2,1)} copy(bf16[1152,128]{1,0:T(8,128)(2,1)S(1)} %get-tuple-element.45) | data formatting | bytes 589824
  34.0 0.3 collective-permute-done.14
  34.3 0.7 %slice_add_fusion = (f32[128,128]{1,0:T(8,128)}, f32[128,128]{1,0:T(8,128)}) fusion(f32[256,128]{1,0:T(8,128)S(1)} %collective-permute-done.14, f32[256,128]{1,0:T(8,128)S(1)} %shard_map.110), kind=kLoop, calls=%fused_computation.1 | loop fusion | flops 32768 | bytes 393216 | tf_op jit(solution)/shard_map/add | solution.py:217
  (2 shorter events, 0.0 us)
Async XLA Ops:
  1.7 6.7 %copy-start = (bf16[1152,512]{1,0:T(8,128)(2,1)S(1)}, bf16[1152,512]{1,0:T(8,128)(2,1)}, u32[]{:S(2)}) copy-start(bf16[1152,512]{1,0:T(8,128)(2,1)} %halo_bonds.5) | copy-start | bytes 3538948
  1.7 6.7 %copy-start.1 = (bf16[1152,1152]{1,0:T(8,128)(2,1)S(1)}, bf16[1152,1152]{1,0:T(8,128)(2,1)}, u32[]{:S(2)}) copy-start(bf16[1152,1152]{1,0:T(8,128)(2,1)} %local_bonds.1) | copy-start | bytes 7962628
  1.7 6.7 %copy-start.5 = (s32[18,18]{1,0:T(8,128)S(1)}, s32[18,18]{1,0:T(8,128)}, u32[]{:S(2)}) copy-start(s32[18,18]{1,0:T(8,128)} %tile_mask.1) | copy-start | bytes 3892
  1.7 6.7 %copy-start.6 = (s32[4,128]{1,0:T(4,128)S(1)}, s32[4,128]{1,0:T(4,128)}, u32[]{:S(2)}) copy-start(s32[4,128]{1,0:T(4,128)} %send_rows.3) | copy-start | bytes 6148
  2.2 8.3 %collective-permute-start = (bf16[128,128]{1,0:T(8,128)(2,1)S(1)}, bf16[128,128]{1,0:T(8,128)(2,1)S(1)}, u32[]{:S(2)}, u32[]{:S(2)}) collective-permute-start(bf16[128,128]{1,0:T(8,128)(2,1)S(1)} %get-tuple-element.27), channel_id=1, source_target_pairs={{0,1},{1,0},{2,3},{3,2},{4,5},{5,4},{6,7},{7,6},{8,9},{9,8},{10,11... | collective-permute-start | bytes 98312 | tf_op jit(solution)/shard_map/ppermute | solution.py:18
  2.7 7.8 %collective-permute-start.1 = (bf16[128,128]{1,0:T(8,128)(2,1)S(1)}, bf16[128,128]{1,0:T(8,128)(2,1)S(1)}, u32[]{:S(2)}, u32[]{:S(2)}) collective-permute-start(bf16[128,128]{1,0:T(8,128)(2,1)S(1)} %get-tuple-element.28), channel_id=1, source_target_pairs={{0,2},{1,3},{2,0},{3,1},{4,6},{5,7},{6,4},{7,5},{8,10},{9,11},{10,... | collective-permute-start | bytes 98312 | tf_op jit(solution)/shard_map/ppermute | solution.py:18
  5.3 5.2 %collective-permute-start.2 = (bf16[128,128]{1,0:T(8,128)(2,1)S(1)}, bf16[128,128]{1,0:T(8,128)(2,1)S(1)}, u32[]{:S(2)}, u32[]{:S(2)}) collective-permute-start(bf16[128,128]{1,0:T(8,128)(2,1)S(1)} %get-tuple-element.29), channel_id=1, source_target_pairs={{0,4},{1,5},{2,6},{3,7},{4,0},{5,1},{6,2},{7,3},{8,12},{9,13},{10,... | collective-permute-start | bytes 98312 | tf_op jit(solution)/shard_map/ppermute | solution.py:18
  6.8 7.0 %copy-start.3 = (bf16[128,128]{1,0:T(8,128)(2,1)S(1)}, bf16[128,128]{1,0:T(8,128)(2,1)}, u32[]{:S(2)}) copy-start(bf16[128,128]{1,0:T(8,128)(2,1)} %first_weight.3) | copy-start | bytes 98308
  6.8 3.9 %collective-permute-start.3 = (bf16[128,128]{1,0:T(8,128)(2,1)S(1)}, bf16[128,128]{1,0:T(8,128)(2,1)S(1)}, u32[]{:S(2)}, u32[]{:S(2)}) collective-permute-start(bf16[128,128]{1,0:T(8,128)(2,1)S(1)} %get-tuple-element.30), channel_id=1, source_target_pairs={{0,8},{1,9},{2,10},{3,11},{4,12},{5,13},{6,14},{7,15},{8,0},{9,1},... | collective-permute-start | bytes 98312 | tf_op jit(solution)/shard_map/ppermute | solution.py:18
  11.0 4.9 %copy-start.2 = (bf16[1152,128]{1,0:T(8,128)(2,1)S(1)}, bf16[1152,128]{1,0:T(8,128)(2,1)}, u32[]{:S(2)}) copy-start(bf16[1152,128]{1,0:T(8,128)(2,1)} %targets.1) | copy-start | bytes 884740
  11.0 4.9 %copy-start.4 = (bf16[128,128]{1,0:T(8,128)(2,1)S(1)}, bf16[128,128]{1,0:T(8,128)(2,1)}, u32[]{:S(2)}) copy-start(bf16[128,128]{1,0:T(8,128)(2,1)} %second_weight.1) | copy-start | bytes 98308
  11.0 4.8 %collective-permute-start.4 = (bf16[128,128]{1,0:T(8,128)(2,1)S(1)}, bf16[128,128]{1,0:T(8,128)(2,1)S(1)}, u32[]{:S(2)}, u32[]{:S(2)}) collective-permute-start(bf16[128,128]{1,0:T(8,128)(2,1)S(1)} %get-tuple-element.37), channel_id=1, source_target_pairs={{0,1},{1,0},{2,3},{3,2},{4,5},{5,4},{6,7},{7,6},{8,9},{9,8},{10,11... | collective-permute-start | bytes 98312 | tf_op jit(solution)/shard_map/ppermute | solution.py:18
  11.1 4.8 %collective-permute-start.5 = (bf16[128,128]{1,0:T(8,128)(2,1)S(1)}, bf16[128,128]{1,0:T(8,128)(2,1)S(1)}, u32[]{:S(2)}, u32[]{:S(2)}) collective-permute-start(bf16[128,128]{1,0:T(8,128)(2,1)S(1)} %get-tuple-element.38), channel_id=1, source_target_pairs={{0,2},{1,3},{2,0},{3,1},{4,6},{5,7},{6,4},{7,5},{8,10},{9,11},{10,... | collective-permute-start | bytes 98312 | tf_op jit(solution)/shard_map/ppermute | solution.py:18
  11.7 4.2 %collective-permute-start.6 = (bf16[128,128]{1,0:T(8,128)(2,1)S(1)}, bf16[128,128]{1,0:T(8,128)(2,1)S(1)}, u32[]{:S(2)}, u32[]{:S(2)}) collective-permute-start(bf16[128,128]{1,0:T(8,128)(2,1)S(1)} %get-tuple-element.39), channel_id=1, source_target_pairs={{0,4},{1,5},{2,6},{3,7},{4,0},{5,1},{6,2},{7,3},{8,12},{9,13},{10,... | collective-permute-start | bytes 98312 | tf_op jit(solution)/shard_map/ppermute | solution.py:18
  12.0 3.9 %collective-permute-start.7 = (bf16[128,128]{1,0:T(8,128)(2,1)S(1)}, bf16[128,128]{1,0:T(8,128)(2,1)S(1)}, u32[]{:S(2)}, u32[]{:S(2)}) collective-permute-start(bf16[128,128]{1,0:T(8,128)(2,1)S(1)} %get-tuple-element.40), channel_id=1, source_target_pairs={{0,8},{1,9},{2,10},{3,11},{4,12},{5,13},{6,14},{7,15},{8,0},{9,1},... | collective-permute-start | bytes 98312 | tf_op jit(solution)/shard_map/ppermute | solution.py:18
  17.8 1.4 %collective-permute-start.8 = (f32[256,128]{1,0:T(8,128)S(1)}, f32[256,128]{1,0:T(8,128)S(1)}, u32[]{:S(2)}, u32[]{:S(2)}) collective-permute-start(f32[256,128]{1,0:T(8,128)S(1)} %get-tuple-element.42), channel_id=1, source_target_pairs={{0,1},{1,0},{2,3},{3,2},{4,5},{5,4},{6,7},{7,6},{8,9},{9,8},{10,11... | collective-permute-start | bytes 393224 | tf_op jit(solution)/shard_map/ppermute | solution.py:18
  19.2 5.4 %collective-permute-start.11 = (bf16[256,128]{1,0:T(8,128)(2,1)S(1)}, bf16[256,128]{1,0:T(8,128)(2,1)S(1)}, u32[]{:S(2)}, u32[]{:S(2)}) collective-permute-start(bf16[256,128]{1,0:T(8,128)(2,1)S(1)} %add_convert_fusion.own), channel_id=1, source_target_pairs={{0,6},{1,7},{2,4},{3,5},{4,2},{5,3},{6,0},{7,1},{8,14},{9,15},{10,... | collective-permute-start | bytes 196616 | tf_op jit(solution)/shard_map/ppermute | solution.py:175
  21.9 4.3 %collective-permute-start.10 = (bf16[256,128]{1,0:T(8,128)(2,1)S(1)}, bf16[256,128]{1,0:T(8,128)(2,1)S(1)}, u32[]{:S(2)}, u32[]{:S(2)}) collective-permute-start(bf16[256,128]{1,0:T(8,128)(2,1)S(1)} %add_convert_fusion.own), channel_id=1, source_target_pairs={{0,4},{1,3},{2,6},{3,1},{4,0},{5,7},{6,2},{7,5},{8,12},{9,11},{10,... | collective-permute-start | bytes 196616 | tf_op jit(solution)/shard_map/ppermute | solution.py:175
  22.4 4.3 %collective-permute-start.9 = (bf16[256,128]{1,0:T(8,128)(2,1)S(1)}, bf16[256,128]{1,0:T(8,128)(2,1)S(1)}, u32[]{:S(2)}, u32[]{:S(2)}) collective-permute-start(bf16[256,128]{1,0:T(8,128)(2,1)S(1)} %add_convert_fusion.own), channel_id=1, source_target_pairs={{0,2},{1,5},{2,0},{3,7},{4,6},{5,1},{6,4},{7,3},{8,10},{9,13},{10,... | collective-permute-start | bytes 196616 | tf_op jit(solution)/shard_map/ppermute | solution.py:175
  26.7 5.0 %collective-permute-start.13 = (bf16[256,128]{1,0:T(8,128)(2,1)S(1)}, bf16[256,128]{1,0:T(8,128)(2,1)S(1)}, u32[]{:S(2)}, u32[]{:S(2)}) collective-permute-start(bf16[256,128]{1,0:T(8,128)(2,1)S(1)} %shard_map.109.own), channel_id=1, source_target_pairs={{0,8},{1,25},{2,10},{3,27},{4,12},{5,29},{6,14},{7,31},{8,0},{9,17... | collective-permute-start | bytes 196616 | tf_op jit(solution)/shard_map/ppermute | solution.py:175
  28.4 4.3 %collective-permute-start.12 = (bf16[256,128]{1,0:T(8,128)(2,1)S(1)}, bf16[256,128]{1,0:T(8,128)(2,1)S(1)}, u32[]{:S(2)}, u32[]{:S(2)}) collective-permute-start(bf16[256,128]{1,0:T(8,128)(2,1)S(1)} %shard_map.109.own), channel_id=1, source_target_pairs={{0,8},{1,17},{2,10},{3,19},{4,12},{5,21},{6,14},{7,23},{8,0},{9,25... | collective-permute-start | bytes 196616 | tf_op jit(solution)/shard_map/ppermute | solution.py:175
  32.7 1.6 %collective-permute-start.14 = (f32[256,128]{1,0:T(8,128)S(1)}, f32[256,128]{1,0:T(8,128)S(1)}, u32[]{:S(2)}, u32[]{:S(2)}) collective-permute-start(f32[256,128]{1,0:T(8,128)S(1)} %shard_map.110), channel_id=1, source_target_pairs={{0,1},{1,0},{2,3},{3,2},{4,5},{5,4},{6,7},{7,6},{8,9},{9,8},{10,11... | collective-permute-start | bytes 393224 | tf_op jit(solution)/shard_map/ppermute | solution.py:18
